TPU v7x, 32 devices: a whole 2x2x4 slice. The times are simulated.
32 devices in a mesh: member: 2 (over y), lon: 4 (over z), lat: 4 (over x, core).
Axes of the slice: x: 2, y: 2, z: 4, core: 2. Of those that a mesh axis runs over, the one named last changes fastest.
Arguments:
- tracer: float32 [20, 16, 64, 512], P('member', None, 'lat', 'lon'), parts along dimension 0, may hold values from -6 to 6
- ocean_mask: int32 [64, 512], P('lat', 'lon'), may hold values 0 or 1
- diffusivity: float32 [64, 512], P('lat', 'lon'), may hold values from 0.12 to 0.24
- remap_cell: int32 [2048, 128], P(('lon', 'lat')), may hold values from 0 to 2047
- remap_column: int32 [2048, 128], P(('lon', 'lat')), may hold values from 0 to 255
- remap_weight: float32 [2048, 128], P(('lon', 'lat')), may hold values from 0.05 to 0.2
- remap_owner: int32 [2048, 1], P(('lon', 'lat')), may hold values from 0 to 15; in each aligned block of 128 rows (0 to 127, 128 to 255, ...) at most 21 rows name the same one
Outputs:
- updated: float32 [20, 16, 64, 512], P('member', None, 'lat', 'lon'), parts along dimension 0
- atmosphere: float32 [20, 4096], P('member', ('lon', 'lat')), parts along dimension 0
There are 2 independent parts, one for each index of `member`. A program takes and returns all parts, laid end to end along the dimension named above; an argument that names none is the same for every part. Nothing has to cross between parts.
Inputs may be any that keep to these rules, and one draw needn't show every extreme that they name: `remap_owner`: among the 128 blocks of one device at most 21 have the same owner.
All inputs are finite; a program needn't handle non-finite values. No bound on the sum of `ocean_mask` on one device may be relied on, other than what follows from the above.
Results may differ from a plain program's by a relative error of at most 0.000082.
Values sent between devices are 32-bit elements; how exact they have to be, the bound alone decides.
No kernel may reach another device: no remote copies, remote signals or barrier semaphores. Data moves between devices by JAX's collectives and lax.ppermute only.
A program may use at most 64 MiB of HBM per device.

v0:
```python
import jax
import jax.numpy as jnp
from jax import lax
from jax.sharding import PartitionSpec as P

ACOL = 256
SUBSTEPS = 3


neighbour_offsets = ((1, 0), (-1, 0), (0, 1), (0, -1))


def extended_2(value, sides, width, wrap):
    for axis, dim in sides:
        size, length = (lax.axis_size(axis), value.shape[dim])
        up = [(i, (i + 1) % size) for i in range(size if wrap else size - 1)]
        down = [(j, i) for i, j in up]
        last = lax.slice_in_dim(value, length - width, length, axis=dim)
        initial = lax.slice_in_dim(value, 0, width, axis=dim)
        before = lax.ppermute(last, axis, up)
        after = lax.ppermute(initial, axis, down)
        value = jnp.concatenate([before, value, after], axis=dim)
    return value


def partner(block, axis, distance):
    count = lax.axis_size(axis)
    route = []
    for low in range(count):
        high = low | 1 << distance
        if high != low and high < count:
            route += [(low, high), (high, low)]
    return lax.ppermute(block, axis, route)


def neighbour(array, shift_row, shift_col):
    height = array.shape[-2] - 2
    breadth = array.shape[-1] - 2
    return array[
        ..., 1 + shift_row : 1 + shift_row + height, 1 + shift_col : 1 + shift_col + breadth
    ]


def relax(extended):
    wetness = extended[-2]
    spread = extended[-1]
    fields = extended[:-2]
    centre_wet = wetness[1:-1, 1:-1]
    centre_diff = spread[1:-1, 1:-1]
    centre = fields[:, 1:-1, 1:-1]
    change = jnp.zeros_like(centre)
    for shift_row, shift_col in neighbour_offsets:
        beside_wet = neighbour(wetness, shift_row, shift_col)
        beside_diff = neighbour(spread, shift_row, shift_col)
        beside = neighbour(fields, shift_row, shift_col)
        coupling = 0.5 * (centre_diff + beside_diff) * centre_wet * beside_wet
        change = change + coupling * (beside - centre)
    return jnp.concatenate([centre + change, centre_wet[None], centre_diff[None]], axis=0)


def extend(fields_stack, halo_depth):
    with_rows = extended_2(fields_stack, (("lat", 1),), halo_depth, False)
    mirrored = jnp.flip(fields_stack[:, -halo_depth:, :], axis=(1, 2))
    lon_count = lax.axis_size("lon")
    for bit_index in range(lon_count.bit_length() - 1):
        mirrored = partner(mirrored, "lon", bit_index)
    on_top = lax.axis_index("lat") == lax.axis_size("lat") - 1
    northern = jnp.where(on_top, mirrored, with_rows[:, -halo_depth:, :])
    with_rows = jnp.concatenate([with_rows[:, :-halo_depth, :], northern], axis=1)
    return extended_2(with_rows, (("lon", 2),), halo_depth, True)


def remap_surface(tracer, remap_cell, remap_column, remap_weight, remap_owner):
    tracers, levels, height, breadth = tracer.shape
    blocks, entries = remap_cell.shape
    surface = tracer[:, 0].reshape(tracers, height * breadth)
    picked = (
        jnp.take(surface, remap_cell.reshape(-1), axis=1).reshape(tracers, blocks, entries)
        * remap_weight[None]
    )
    payload = jnp.concatenate(
        [jnp.transpose(picked, (1, 0, 2)), remap_column.astype(jnp.float32)[:, None, :]], axis=1
    )
    lon_count = lax.axis_size("lon")
    lat_count = lax.axis_size("lat")
    owners = lon_count * lat_count
    capacity = max(2, 8 * blocks // (3 * owners))
    owner_ids = remap_owner[:, 0]
    owner_hits = (owner_ids[:, None] == jnp.arange(owners, dtype=jnp.int32)[None, :]).astype(
        jnp.int32
    )
    slot_rank = jnp.sum(jnp.cumsum(owner_hits, axis=0) * owner_hits, axis=1) - 1
    slot_index = owner_ids * capacity + slot_rank
    outgoing = (
        jnp.zeros((owners * capacity, tracers + 1, entries), jnp.float32)
        .at[slot_index]
        .set(payload)
    )
    incoming = lax.all_to_all(
        outgoing.reshape(owners, capacity, tracers + 1, entries),
        ("lon", "lat"),
        split_axis=0,
        concat_axis=0,
        tiled=True,
    )
    groups = incoming.reshape(16, owners * capacity // 16, tracers + 1, entries)
    column_iota = jnp.arange(ACOL, dtype=jnp.float32)

    def add_group(accumulated, slot_group):
        values = jnp.transpose(slot_group[:, :tracers, :], (1, 0, 2)).reshape(tracers, -1)
        targets = slot_group[:, tracers, :].reshape(-1)
        selector = (targets[:, None] == column_iota[None, :]).astype(jnp.float32)
        product = jnp.dot(
            values, selector, precision=lax.Precision.HIGHEST, preferred_element_type=jnp.float32
        )
        return (accumulated + product, None)

    accumulated, unused = lax.scan(add_group, jnp.zeros((tracers, ACOL), jnp.float32), groups)
    return accumulated


def on_device(tracer, ocean_mask, diffusivity, remap_cell, remap_column, remap_weight, remap_owner):
    tracers, levels, height, breadth = tracer.shape
    atmosphere = remap_surface(tracer, remap_cell, remap_column, remap_weight, remap_owner)
    wetness = ocean_mask.astype(jnp.float32)
    fields_stack = jnp.concatenate(
        [tracer.reshape(tracers * levels, height, breadth), wetness[None], diffusivity[None]],
        axis=0,
    )
    for substep in range(SUBSTEPS):
        fields_stack = relax(extend(fields_stack, 1))
    updated = fields_stack[:-2].reshape(tracers, levels, height, breadth)
    return (updated, atmosphere)


def solution(mesh):
    in_specs = (
        P("member", None, "lat", "lon"),
        P("lat", "lon"),
        P("lat", "lon"),
        P(("lon", "lat"), None),
        P(("lon", "lat"), None),
        P(("lon", "lat"), None),
        P(("lon", "lat"), None),
    )
    out_specs = (P("member", None, "lat", "lon"), P("member", ("lon", "lat")))
    return jax.shard_map(
        on_device, mesh=mesh, in_specs=in_specs, out_specs=out_specs, check_vma=False
    )
```

profile of v0, /device:TPU:0, one launch (start us, length us, event | category | flops | bytes accessed | tf_op | source)
XLA Modules:
  0.0 262.4 jit_solution(15394109574302296122)
XLA Ops:
  1.4 1.5 pad_maximum_fusion.58
  2.9 2.4 collective-permute-start
  5.3 1.3 rev.10
  6.6 2.5 collective-permute-start.1
  9.1 1.3 collective-permute-start.3
  10.9 54.8 %gather_fusion = f32[16384,10]{1,0:T(8,128)} fusion(f32[10,2048]{0,1:T(8,128)S(1)} %bitcast.66, s32[16384]{0:T(1024)S(1)} %broadcast_clamp_fusion), kind=kCustom, calls=%fused_computation | custom fusion | bytes 1376256 | tf_op jit(solution)/shard_map/jit(_take)/gather | solution.py:78
  65.7 5.3 %copy.51 = f32[10,128,128]{2,0,1:T(8,128)S(1)} copy(f32[10,128,128]{0,2,1:T(8,128)} %bitcast.73) | data formatting | bytes 1310720 | tf_op jit(solution)/shard_map/jit(_take)/gather | solution.py:78
  71.0 1.2 multiply_bitcast_fusion
  72.2 2.6 collective-permute-start.2
  75.0 4.0 %collective-permute-done.2 = f32[162,1,128]{2,1,0:T(1,128)S(1)} collective-permute-done((f32[162,1,128]{2,1,0:T(1,128)S(1)}, f32[162,1,128]{2,1,0:T(1,128)S(1)}, u32[]{:S(2)}, u32[]{:S(2)}) %collective-permute-start.2) | collective-permute-done | bytes 82976 | tf_op jit(solution)/shard_map/ppermute | solution.py:33
  79.5 2.0 fusion.72
  81.4 2.9 %copy.32 = f32[162,18,1]{0,2,1:T(1,128)} copy(f32[162,18,1]{2,1,0:T(8,128)} %get-tuple-element.58) | data formatting | bytes 23328 | tf_op jit(solution)/shard_map/slice | solution.py:18
  84.3 1.3 copy.33
  85.6 3.8 %collective-permute-start.5 = (f32[162,18,1]{0,2,1:T(1,128)}, f32[162,18,1]{0,2,1:T(1,128)}, u32[]{:S(2)}, u32[]{:S(2)}) collective-permute-start(f32[162,18,1]{0,2,1:T(1,128)} %copy.33), channel_id=1, source_target_pairs={{4,0},{8,4},{12,8},{0,12},{5,1},{9,5},{13,9},{1,13},{6,2},{10,6},{... | collective-permute-start | bytes 35000 | tf_op jit(solution)/shard_map/ppermute | solution.py:21
  89.4 1.3 select_reduce_fusion
  90.8 1.7 copy.34
  92.6 3.0 %copy.35 = f32[162,18,1]{2,1,0:T(8,128)} copy(f32[162,18,1]{0,2,1:T(1,128)} %collective-permute-done.5) | data formatting | bytes 23328 | tf_op jit(solution)/shard_map/ppermute | solution.py:21
  97.2 5.6 %fusion.32 = f32[160,16,128]{2,1,0:T(8,128)S(1)} fusion(f32[160,16,128]{2,1,0:T(8,128)S(1)} %bitcast.70, f32[162,18,1]{2,1,0:T(8,128)} %copy-done.2, f32[162,1,128]{2,1,0:T(1,128)S(1)} %broadcast_select_fusion.2, f32[162,1,128]{2,1,0:T(1,128)S(1)} %collective-permute-done, f32[1,16,128]{2,1,0:T(8,128)S(1)} %bitcast.82, ...), kind=kLoop, calls=%fused_computation.73 | loop fusion | flops 9175040 | bytes 2859808 | tf_op jit(solution)/shard_map/add | solution.py:58
  102.9 1.3 rev.11
  104.4 1.3 collective-permute-start.9
  105.7 3.1 %collective-permute-done.7 = f32[162,1,128]{2,1,0:T(1,128)S(1)} collective-permute-done((f32[162,1,128]{2,1,0:T(1,128)S(1)}, f32[162,1,128]{2,1,0:T(1,128)S(1)}, u32[]{:S(2)}, u32[]{:S(2)}) %collective-permute-start.7) | collective-permute-done | bytes 82976 | tf_op jit(solution)/shard_map/ppermute | solution.py:33
  108.8 1.3 collective-permute-start.8
  111.2 1.7 broadcast_in_dim.60
  112.9 13.7 %scatter_fusion = f32[336,11,128]{2,1,0:T(8,128)} fusion(f32[336,11,128]{2,1,0:T(8,128)} %broadcast_in_dim.60, s32[128]{0:T(128)S(1)} %fusion.69, f32[128,11,128]{2,1,0:T(8,128)S(1)} %copy-done.7), kind=kCustom, calls=%fused_computation.1 | custom fusion | bytes 2163200 | tf_op jit(solution)/shard_map/scatter | solution.py:97
  126.6 3.8 %copy.53 = f32[16,21,11,128]{3,1,2,0:T(8,128)} copy(f32[16,21,11,128]{3,2,1,0:T(8,128)} %bitcast.72) | data formatting | bytes 3784704 | tf_op jit(solution)/shard_map/reshape | solution.py:100
  130.4 5.9 %all-to-all-start = ((f32[16,21,11,128]{3,1,2,0:T(8,128)}), f32[16,21,11,128]{3,1,2,0:T(8,128)}, u32[]{:S(2)}, u32[]{:S(2)}) async-start(f32[16,21,11,128]{3,1,2,0:T(8,128)} %copy.53), calls=%async_computation | async-start | bytes 4325376 | tf_op jit(solution)/shard_map/all_to_all | solution.py:99
  136.3 2.4 collective-permute-start.6
  139.7 2.6 fusion.71
  142.3 2.3 copy.38
  144.6 1.7 collective-permute-start.10
  146.3 2.3 copy.39
  148.5 2.2 collective-permute-start.11
  150.7 26.1 %collective-permute-done.10 = f32[162,18,1]{0,2,1:T(1,128)S(1)} collective-permute-done((f32[162,18,1]{0,2,1:T(1,128)S(1)}, f32[162,18,1]{0,2,1:T(1,128)S(1)}, u32[]{:S(2)}, u32[]{:S(2)}) %collective-permute-start.10) | collective-permute-done | bytes 11696 | tf_op jit(solution)/shard_map/ppermute | solution.py:20
  176.8 2.3 copy.40
  179.1 2.3 copy.41
  183.6 4.4 %fusion.20 = f32[160,16,128]{2,1,0:T(8,128)S(1)} fusion(f32[160,16,128]{2,1,0:T(8,128)S(1)} %fusion.32, f32[162,18,1]{2,1,0:T(8,128)S(1)} %copy-done.1, f32[162,1,128]{2,1,0:T(1,128)S(1)} %broadcast_select_fusion.1, f32[162,1,128]{2,1,0:T(1,128)S(1)} %collective-permute-done.6, f32[1,16,128]{2,1,0:T(8,128)S(1)} %get-tuple-element.80, ...), kind=kLoop, calls=%fused_computation.45 | loop fusion | flops 9175040 | bytes 2859808 | tf_op jit(solution)/shard_map/add | solution.py:58
  188.2 1.3 rev.12
  189.6 9.4 %collective-permute-start.13 = (f32[162,1,128]{2,1,0:T(1,128)S(1)}, f32[162,1,128]{2,1,0:T(1,128)S(1)}, u32[]{:S(2)}, u32[]{:S(2)}) collective-permute-start(f32[162,1,128]{2,1,0:T(1,128)S(1)} %rev.12), channel_id=1, source_target_pairs={{0,4},{4,0},{8,12},{12,8},{1,5},{5,1},{9,13},{13,9},{2,6},{6,2},{1... | collective-permute-start | bytes 248840 | tf_op jit(solution)/shard_map/ppermute | solution.py:33
  199.0 1.3 collective-permute-start.15
  201.4 3.9 %collective-permute-start.14 = (f32[162,1,128]{2,1,0:T(1,128)S(1)}, f32[162,1,128]{2,1,0:T(1,128)S(1)}, u32[]{:S(2)}, u32[]{:S(2)}) collective-permute-start(f32[162,1,128]{2,1,0:T(1,128)S(1)} %collective-permute-done.13), channel_id=1, source_target_pairs={{0,8},{8,0},{4,12},{12,4},{1,9},{9,1},{5,13},{13,5},{2,10},{10,2},... | collective-permute-start | bytes 248840 | tf_op jit(solution)/shard_map/ppermute | solution.py:33
  205.4 1.3 collective-permute-start.12
  206.7 2.0 collective-permute-done.14
  209.1 2.0 fusion.70
  211.1 2.3 copy.44
  214.6 3.6 %collective-permute-start.17 = (f32[162,18,1]{0,2,1:T(1,128)S(1)}, f32[162,18,1]{0,2,1:T(1,128)}, u32[]{:S(2)}, u32[]{:S(2)}) collective-permute-start(f32[162,18,1]{0,2,1:T(1,128)S(1)} %copy.45), channel_id=1, source_target_pairs={{4,0},{8,4},{12,8},{0,12},{5,1},{9,5},{13,9},{1,13},{6,2},{10,6},{... | collective-permute-start | bytes 35000 | tf_op jit(solution)/shard_map/ppermute | solution.py:21
  220.1 3.0 %copy.47 = f32[162,18,1]{2,1,0:T(8,128)} copy(f32[162,18,1]{0,2,1:T(1,128)} %collective-permute-done.17) | data formatting | bytes 23328 | tf_op jit(solution)/shard_map/ppermute | solution.py:21
  224.7 5.2 %fusion.8 = f32[160,16,128]{2,1,0:T(8,128)} fusion(f32[160,16,128]{2,1,0:T(8,128)S(1)} %fusion.20, f32[162,18,1]{2,1,0:T(8,128)S(1)} %copy.46, f32[162,1,128]{2,1,0:T(1,128)S(1)} %broadcast_select_fusion, f32[162,1,128]{2,1,0:T(1,128)S(1)} %collective-permute-done.12, f32[1,16,128]{2,1,0:T(8,128)S(1)} %get-tuple-element.78, ...), kind=kLoop, calls=%fused_computation.17 | loop fusion | flops 9175040 | bytes 2859808 | tf_op jit(solution)/shard_map/add | solution.py:58
  229.9 31.9 %while.11 = (s32[]{:T(128)}, f32[10,256]{1,0:T(8,128)S(1)}, f32[16,21,11,128]{3,1,2,0:T(8,128)}, s32[]{:T(128)}, f32[]{:T(128)}, /*index=5*/s32[]{:T(128)}) while((s32[]{:T(128)}, f32[10,256]{1,0:T(8,128)S(1)}, f32[16,21,11,128]{3,1,2,0:T(8,128)}, s32[]{:T(128)}, f32[]{:T(128)}, /*index=5*/s32[]{:T(128)}) %tuple.52), condition=%wide.region_4.5_spmd.clone, body=%wide.region_3.4_spmd.clone.sunk | while | flops 83268608 | bytes 1235543 | solution.py:118
  (176 shorter events, 46.3 us)
Async XLA Ops:
  0.6 9.8 %copy-start = (f32[10,16,16,128]{3,2,1,0:T(8,128)S(1)}, f32[10,16,16,128]{3,2,1,0:T(8,128)}, u32[]{:S(2)}) copy-start(f32[10,16,16,128]{3,2,1,0:T(8,128)} %param.9) | copy-start | bytes 3932164
  1.4 9.3 %copy-start.8 = (s32[128,128]{1,0:T(8,128)S(1)}, s32[128,128]{1,0:T(8,128)}, u32[]{:S(2)}) copy-start(s32[128,128]{1,0:T(8,128)} %param.12) | copy-start | bytes 196612
  2.9 76.2 %collective-permute-start = (f32[162,1,128]{2,1,0:T(1,128)S(1)}, f32[162,1,128]{2,1,0:T(1,128)S(1)}, u32[]{:S(2)}, u32[]{:S(2)}) collective-permute-start(f32[162,1,128]{2,1,0:T(1,128)S(1)} %get-tuple-element.64), channel_id=1, source_target_pairs={{0,1},{1,2},{2,3},{4,5},{5,6},{6,7},{8,9},{9,10},{10,11},{12,13},{... | collective-permute-start | bytes 248840 | tf_op jit(solution)/shard_map/ppermute | solution.py:20
  6.6 65.5 %collective-permute-start.1 = (f32[162,1,128]{2,1,0:T(1,128)S(1)}, f32[162,1,128]{2,1,0:T(1,128)S(1)}, u32[]{:S(2)}, u32[]{:S(2)}) collective-permute-start(f32[162,1,128]{2,1,0:T(1,128)S(1)} %rev.10), channel_id=1, source_target_pairs={{0,4},{4,0},{8,12},{12,8},{1,5},{5,1},{9,13},{13,9},{2,6},{6,2},{1... | collective-permute-start | bytes 248840 | tf_op jit(solution)/shard_map/ppermute | solution.py:33
  9.1 65.9 %collective-permute-start.3 = (f32[162,1,128]{2,1,0:T(1,128)S(1)}, f32[162,1,128]{2,1,0:T(1,128)S(1)}, u32[]{:S(2)}, u32[]{:S(2)}) collective-permute-start(f32[162,1,128]{2,1,0:T(1,128)S(1)} %get-tuple-element.63), channel_id=1, source_target_pairs={{1,0},{2,1},{3,2},{5,4},{6,5},{7,6},{9,8},{10,9},{11,10},{13,12},{... | collective-permute-start | bytes 248840 | tf_op jit(solution)/shard_map/ppermute | solution.py:21
  65.7 5.3 %copy-start.10 = (f32[128,128]{1,0:T(8,128)S(1)}, f32[128,128]{1,0:T(8,128)}, u32[]{:S(2)}) copy-start(f32[128,128]{1,0:T(8,128)} %param.14) | copy-start | bytes 196612
  70.9 3.8 %copy-start.12 = (s32[128,1]{0,1:T(1,128)S(1)}, s32[128,1]{0,1:T(1,128)}, u32[]{:S(2)}) copy-start(s32[128,1]{0,1:T(1,128)} %param.15) | copy-start | bytes 1540
  71.0 8.2 %copy-start.9 = (f32[16,128]{1,0:T(8,128)S(1)}, f32[16,128]{1,0:T(8,128)}, u32[]{:S(2)}) copy-start(f32[16,128]{1,0:T(8,128)} %param.11) | copy-start | bytes 24580
  72.2 6.9 %collective-permute-start.2 = (f32[162,1,128]{2,1,0:T(1,128)S(1)}, f32[162,1,128]{2,1,0:T(1,128)S(1)}, u32[]{:S(2)}, u32[]{:S(2)}) collective-permute-start(f32[162,1,128]{2,1,0:T(1,128)S(1)} %collective-permute-done.1), channel_id=1, source_target_pairs={{0,8},{8,0},{4,12},{12,4},{1,9},{9,1},{5,13},{13,5},{2,10},{10,2},... | collective-permute-start | bytes 248840 | tf_op jit(solution)/shard_map/ppermute | solution.py:33
  84.3 6.5 %collective-permute-start.4 = (f32[162,18,1]{0,2,1:T(1,128)}, f32[162,18,1]{0,2,1:T(1,128)}, u32[]{:S(2)}, u32[]{:S(2)}) collective-permute-start(f32[162,18,1]{0,2,1:T(1,128)} %copy.32), channel_id=1, source_target_pairs={{0,4},{4,8},{8,12},{12,0},{1,5},{5,9},{9,13},{13,1},{2,6},{6,10},{... | collective-permute-start | bytes 35000 | tf_op jit(solution)/shard_map/ppermute | solution.py:20
  85.6 6.9 %collective-permute-start.5 = (f32[162,18,1]{0,2,1:T(1,128)}, f32[162,18,1]{0,2,1:T(1,128)}, u32[]{:S(2)}, u32[]{:S(2)}) collective-permute-start(f32[162,18,1]{0,2,1:T(1,128)} %copy.33), channel_id=1, source_target_pairs={{4,0},{8,4},{12,8},{0,12},{5,1},{9,5},{13,9},{1,13},{6,2},{10,6},{... | collective-permute-start | bytes 35000 | tf_op jit(solution)/shard_map/ppermute | solution.py:21
  92.5 4.0 %copy-start.2 = (f32[162,18,1]{2,1,0:T(8,128)}, f32[162,18,1]{2,1,0:T(8,128)S(1)}, u32[]{:S(2)}) copy-start(f32[162,18,1]{2,1,0:T(8,128)S(1)} %copy.34) | copy-start | bytes 34996
  95.6 1.6 copy-start.5
  102.8 1.6 copy-start.13
  102.8 1.6 copy-start.14
  102.8 1.6 copy-start.11
  102.8 7.3 %copy-start.6 = (f32[128,10,128]{2,1,0:T(8,128)S(1)}, f32[128,10,128]{2,1,0:T(8,128)}, u32[]{:S(2)}) copy-start(f32[128,10,128]{2,1,0:T(8,128)} %multiply_bitcast_fusion) | copy-start | bytes 1966084
  104.3 4.5 %collective-permute-start.7 = (f32[162,1,128]{2,1,0:T(1,128)S(1)}, f32[162,1,128]{2,1,0:T(1,128)S(1)}, u32[]{:S(2)}, u32[]{:S(2)}) collective-permute-start(f32[162,1,128]{2,1,0:T(1,128)S(1)} %rev.11), channel_id=1, source_target_pairs={{0,4},{4,0},{8,12},{12,8},{1,5},{5,1},{9,13},{13,9},{2,6},{6,2},{1... | collective-permute-start | bytes 248840 | tf_op jit(solution)/shard_map/ppermute | solution.py:33
  104.4 34.3 %collective-permute-start.9 = (f32[162,1,128]{2,1,0:T(1,128)S(1)}, f32[162,1,128]{2,1,0:T(1,128)S(1)}, u32[]{:S(2)}, u32[]{:S(2)}) collective-permute-start(f32[162,1,128]{2,1,0:T(1,128)S(1)} %get-tuple-element.61), channel_id=1, source_target_pairs={{1,0},{2,1},{3,2},{5,4},{6,5},{7,6},{9,8},{10,9},{11,10},{13,12},{... | collective-permute-start | bytes 248840 | tf_op jit(solution)/shard_map/ppermute | solution.py:21
  108.8 29.9 %collective-permute-start.8 = (f32[162,1,128]{2,1,0:T(1,128)S(1)}, f32[162,1,128]{2,1,0:T(1,128)S(1)}, u32[]{:S(2)}, u32[]{:S(2)}) collective-permute-start(f32[162,1,128]{2,1,0:T(1,128)S(1)} %collective-permute-done.7), channel_id=1, source_target_pairs={{0,8},{8,0},{4,12},{12,4},{1,9},{9,1},{5,13},{13,5},{2,10},{10,2},... | collective-permute-start | bytes 248840 | tf_op jit(solution)/shard_map/ppermute | solution.py:33
  111.2 1.7 copy-start.7
  130.4 99.6 %all-to-all-start = ((f32[16,21,11,128]{3,1,2,0:T(8,128)}), f32[16,21,11,128]{3,1,2,0:T(8,128)}, u32[]{:S(2)}, u32[]{:S(2)}) async-start(f32[16,21,11,128]{3,1,2,0:T(8,128)} %copy.53), calls=%async_computation | async-start | bytes 4325376 | tf_op jit(solution)/shard_map/all_to_all | solution.py:99
  136.3 3.2 %collective-permute-start.6 = (f32[162,1,128]{2,1,0:T(1,128)S(1)}, f32[162,1,128]{2,1,0:T(1,128)S(1)}, u32[]{:S(2)}, u32[]{:S(2)}) collective-permute-start(f32[162,1,128]{2,1,0:T(1,128)S(1)} %get-tuple-element.62), channel_id=1, source_target_pairs={{0,1},{1,2},{2,3},{4,5},{5,6},{6,7},{8,9},{9,10},{10,11},{12,13},{... | collective-permute-start | bytes 248840 | tf_op jit(solution)/shard_map/ppermute | solution.py:20
  144.6 32.2 %collective-permute-start.10 = (f32[162,18,1]{0,2,1:T(1,128)S(1)}, f32[162,18,1]{0,2,1:T(1,128)S(1)}, u32[]{:S(2)}, u32[]{:S(2)}) collective-permute-start(f32[162,18,1]{0,2,1:T(1,128)S(1)} %copy.38), channel_id=1, source_target_pairs={{0,4},{4,8},{8,12},{12,0},{1,5},{5,9},{9,13},{13,1},{2,6},{6,10},{... | collective-permute-start | bytes 35000 | tf_op jit(solution)/shard_map/ppermute | solution.py:20
  148.5 30.6 %collective-permute-start.11 = (f32[162,18,1]{0,2,1:T(1,128)S(1)}, f32[162,18,1]{0,2,1:T(1,128)S(1)}, u32[]{:S(2)}, u32[]{:S(2)}) collective-permute-start(f32[162,18,1]{0,2,1:T(1,128)S(1)} %copy.39), channel_id=1, source_target_pairs={{4,0},{8,4},{12,8},{0,12},{5,1},{9,5},{13,9},{1,13},{6,2},{10,6},{... | collective-permute-start | bytes 35000 | tf_op jit(solution)/shard_map/ppermute | solution.py:21
  181.4 1.6 copy-start.1
  181.4 2.2 copy-start.3
  189.6 11.9 %collective-permute-start.13 = (f32[162,1,128]{2,1,0:T(1,128)S(1)}, f32[162,1,128]{2,1,0:T(1,128)S(1)}, u32[]{:S(2)}, u32[]{:S(2)}) collective-permute-start(f32[162,1,128]{2,1,0:T(1,128)S(1)} %rev.12), channel_id=1, source_target_pairs={{0,4},{4,0},{8,12},{12,8},{1,5},{5,1},{9,13},{13,9},{2,6},{6,2},{1... | collective-permute-start | bytes 248840 | tf_op jit(solution)/shard_map/ppermute | solution.py:33
  199.0 7.7 %collective-permute-start.15 = (f32[162,1,128]{2,1,0:T(1,128)S(1)}, f32[162,1,128]{2,1,0:T(1,128)S(1)}, u32[]{:S(2)}, u32[]{:S(2)}) collective-permute-start(f32[162,1,128]{2,1,0:T(1,128)S(1)} %get-tuple-element.59), channel_id=1, source_target_pairs={{1,0},{2,1},{3,2},{5,4},{6,5},{7,6},{9,8},{10,9},{11,10},{13,12},{... | collective-permute-start | bytes 248840 | tf_op jit(solution)/shard_map/ppermute | solution.py:21
  201.4 7.3 %collective-permute-start.14 = (f32[162,1,128]{2,1,0:T(1,128)S(1)}, f32[162,1,128]{2,1,0:T(1,128)S(1)}, u32[]{:S(2)}, u32[]{:S(2)}) collective-permute-start(f32[162,1,128]{2,1,0:T(1,128)S(1)} %collective-permute-done.13), channel_id=1, source_target_pairs={{0,8},{8,0},{4,12},{12,4},{1,9},{9,1},{5,13},{13,5},{2,10},{10,2},... | collective-permute-start | bytes 248840 | tf_op jit(solution)/shard_map/ppermute | solution.py:33
  205.4 3.4 %collective-permute-start.12 = (f32[162,1,128]{2,1,0:T(1,128)S(1)}, f32[162,1,128]{2,1,0:T(1,128)S(1)}, u32[]{:S(2)}, u32[]{:S(2)}) collective-permute-start(f32[162,1,128]{2,1,0:T(1,128)S(1)} %get-tuple-element.60), channel_id=1, source_target_pairs={{0,1},{1,2},{2,3},{4,5},{5,6},{6,7},{8,9},{9,10},{10,11},{12,13},{... | collective-permute-start | bytes 248840 | tf_op jit(solution)/shard_map/ppermute | solution.py:20
  213.4 5.7 %collective-permute-start.16 = (f32[162,18,1]{0,2,1:T(1,128)S(1)}, f32[162,18,1]{0,2,1:T(1,128)S(1)}, u32[]{:S(2)}, u32[]{:S(2)}) collective-permute-start(f32[162,18,1]{0,2,1:T(1,128)S(1)} %copy.44), channel_id=1, source_target_pairs={{0,4},{4,8},{8,12},{12,0},{1,5},{5,9},{9,13},{13,1},{2,6},{6,10},{... | collective-permute-start | bytes 35000 | tf_op jit(solution)/shard_map/ppermute | solution.py:20
  214.6 5.5 %collective-permute-start.17 = (f32[162,18,1]{0,2,1:T(1,128)S(1)}, f32[162,18,1]{0,2,1:T(1,128)}, u32[]{:S(2)}, u32[]{:S(2)}) collective-permute-start(f32[162,18,1]{0,2,1:T(1,128)S(1)} %copy.45), channel_id=1, source_target_pairs={{4,0},{8,4},{12,8},{0,12},{5,1},{9,5},{13,9},{1,13},{6,2},{10,6},{... | collective-permute-start | bytes 35000 | tf_op jit(solution)/shard_map/ppermute | solution.py:21
  223.1 1.6 copy-start.4
  224.7 5.2 %copy-start.15 = (f32[10,256]{1,0:T(8,128)S(1)}, f32[10,256]{1,0:T(8,128)}, u32[]{:S(2)}) copy-start(f32[10,256]{1,0:T(8,128)} %custom-call) | copy-start | bytes 30724
  261.8 0.6 copy-start.16
where the time goes:
time: 265 us; the launch traced here: 262 us
  local copies, waits for them, and re-layouts  134 us (51%)
  starting transfers between devices  47.4 us (18%)
  waiting for transfers between devices  37.8 us (14%)
  other arithmetic  26.2 us (10%)
  matrix products  15.5 us (6%)
    gather x2, local copies, waits for them, and re-layouts, remap_surface(): jnp.take(surface, remap_cell.reshape(-1), axis=1)  60 us
    ppermute x6, waiting for transfers between devices, extended_2(): before = lax.ppermute(last, axis, up)  27.5 us
    ppermute x6, starting transfers between devices, partner(): return lax.ppermute(block, axis, route)  19.8 us
    dot_general x16, matrix products, add_group(): jnp.dot(values, selector, precision=lax.Precision.HIGHEST, preferred_elem...  15.5 us
    add x3, other arithmetic, relax(): centre + change  15.3 us
    squeeze x16, local copies, waits for them, and re-layouts, remap_surface(): lax.scan(add_group, jnp.zeros((tracers, ACOL), jnp.float32), groups)  14.7 us
    scatter x1, local copies, waits for them, and re-layouts, remap_surface(): outgoing = jnp.zeros((owners * capacity, tracers + 1, entries), jnp.float...  13.7 us
    ppermute x6, starting transfers between devices, extended_2(): after = lax.ppermute(initial, axis, down)  13.5 us
  transfers between devices with their start and end apart: 19, of which 7 were waited for; matrix products, arithmetic and copies ran while one was open for 47% of the time, Pallas kernels for 0%

commit v1 on v0

v1 whole, which is shorter than its diff:
```python
import functools

import jax
import jax.numpy as jnp
from jax import lax
from jax.experimental import pallas as pl
from jax.experimental.pallas import tpu as pltpu
from jax.sharding import PartitionSpec as P

ACOL = 256
SUBSTEPS = 3
LANES = 128
GROUP = 8
EDGE = 6
F32 = jnp.float32


def lane_iota(rows=GROUP):
    return lax.broadcasted_iota(jnp.int32, (rows, LANES), 1)


def edge_lane(row):
    return EDGE * (row + 2) + 2


def edge_pattern():
    place = lane_iota() % EDGE
    return jnp.where(place < 3, 2 - place, LANES + 2 - place)


def in_row(row):
    lane = lane_iota()
    return (lane >= EDGE * (row + 2)) & (lane < EDGE * (row + 3))


def take_lanes(value, index):
    return jnp.take_along_axis(value, index, axis=1)


def pack_kernel(height, chunks, info_ref, tracer_ref, mask_ref, diff_ref, a_ref, b_ref, m_ref):
    odd = info_ref[0]
    top = info_ref[1]
    lane = lane_iota()
    flip = jnp.where(jnp.full(lane.shape, top) == 1, LANES - 1 - lane, lane)
    pattern = edge_pattern()

    def near(d):
        return jnp.where(odd == 1, height - 1 - d, d)

    def one(c, unused):
        base = c * (GROUP * height)
        edges = jnp.zeros((GROUP, LANES), F32)
        for row in range(height):
            value = tracer_ref[pl.ds(base + row, GROUP, stride=height), :]
            edges = jnp.where(in_row(row), take_lanes(value, pattern), edges)
        m_ref[pl.ds(c * GROUP, GROUP), :] = edges
        for d in range(SUBSTEPS):
            first = tracer_ref[pl.ds(base + near(d), GROUP, stride=height), :]
            a_ref[d, pl.ds(c * GROUP, GROUP), :] = take_lanes(first, flip)
            b_ref[d, pl.ds(c * GROUP, GROUP), :] = tracer_ref[
                pl.ds(base + height - 1 - near(d), GROUP, stride=height), :
            ]
        return unused

    lax.fori_loop(0, chunks, one, 0)

    sub = lax.broadcasted_iota(jnp.int32, (GROUP, LANES), 0)

    def fixed(row):
        wet = jnp.broadcast_to(mask_ref[pl.ds(row, 1), :].astype(F32), (GROUP, LANES))
        spread = jnp.broadcast_to(diff_ref[pl.ds(row, 1), :], (GROUP, LANES))
        return jnp.where(sub == 0, wet, jnp.where(sub == 1, spread, 0.0))

    last = pl.ds(chunks * GROUP, GROUP)
    edges = jnp.zeros((GROUP, LANES), F32)
    for row in range(height):
        edges = jnp.where(in_row(row), take_lanes(fixed(row), pattern), edges)
    m_ref[last, :] = edges
    m_ref[pl.ds((chunks + 1) * GROUP, GROUP), :] = jnp.zeros((GROUP, LANES), F32)
    for d in range(SUBSTEPS):
        a_ref[d, last, :] = take_lanes(fixed(near(d)), flip)
        b_ref[d, last, :] = fixed(height - 1 - near(d))


def pick_rows(odd, a_ref, b_ref, d, rows):
    first = a_ref[d, rows, :]
    second = b_ref[d, rows, :]
    swap = jnp.full(first.shape, odd) == 1
    return jnp.where(swap, first, second), jnp.where(swap, second, first)


def columns_kernel(height, chunks, info_ref, a_ref, b_ref, m_ref, east_ref, west_ref):
    odd = info_ref[0]
    pattern = edge_pattern()
    to_west = lane_iota() % EDGE < 3

    def extended(c):
        rows = pl.ds(c * GROUP, GROUP)
        edges = m_ref[rows, :]
        for d in range(SUBSTEPS - 1):
            north, south = pick_rows(odd, a_ref, b_ref, d, rows)
            edges = jnp.where(in_row(height + d), take_lanes(north, pattern), edges)
            edges = jnp.where(in_row(-1 - d), take_lanes(south, pattern), edges)
        return edges

    def put(i, first, second):
        rows = pl.ds(i * GROUP, GROUP)
        west_ref[rows, :] = jnp.where(to_west, first, pltpu.roll(second, 3, 1))
        east_ref[rows, :] = jnp.where(to_west, pltpu.roll(second, LANES - 3, 1), first)

    def one(i, unused):
        put(i, extended(2 * i), extended(2 * i + 1))
        return unused

    lax.fori_loop(0, chunks // 2, one, 0)
    put(chunks // 2, extended(chunks), m_ref[pl.ds((chunks + 1) * GROUP, GROUP), :])


def stencil_kernel(
    height,
    info_ref,
    tracer_ref,
    mask_ref,
    diff_ref,
    a_ref,
    b_ref,
    fe_ref,
    fw_ref,
    out_ref,
    coef,
    edge_coef,
):
    odd = info_ref[0]
    step = pl.program_id(0)
    chunks_all = pl.num_programs(0) * 2
    lane = lane_iota()
    to_east = lane % EDGE < 3
    is_e0 = lane % EDGE == 2
    is_w2 = lane % EDGE == 3
    low, high = -2, height + 2

    def pull(edges, row):
        return pltpu.roll(edges, (LANES - (edge_lane(row) + 1)) % LANES, 1)

    def sides(value, edges, row):
        beyond = pull(edges, row)
        east = jnp.where(lane == LANES - 1, beyond, pltpu.roll(value, LANES - 1, 1))
        west = jnp.where(lane == 0, beyond, pltpu.roll(value, 1, 1))
        return east, west

    def inner(values, rows):
        found = jnp.zeros((GROUP, LANES), F32)
        for row in rows:
            found = jnp.where(in_row(row), pltpu.roll(values[row], edge_lane(row) + 1, 1), found)
        return found

    def edge_neighbours(edges, found):
        right = jnp.where(is_e0, found, pltpu.roll(edges, LANES - 1, 1))
        left = jnp.where(is_w2, found, pltpu.roll(edges, 1, 1))
        return (
            right,
            left,
            pltpu.roll(edges, LANES - EDGE, 1),
            pltpu.roll(edges, EDGE, 1),
        )

    @pl.when(step == 0)
    def prepare():
        rows = pl.ds(chunks_all * GROUP, GROUP)
        wet, spread = {}, {}

        def spread_out(value):
            return (
                jnp.broadcast_to(value[0:1, :], (GROUP, LANES)),
                jnp.broadcast_to(value[1:2, :], (GROUP, LANES)),
            )

        for row in range(height):
            wet[row] = jnp.broadcast_to(mask_ref[row : row + 1, :].astype(F32), (GROUP, LANES))
            spread[row] = jnp.broadcast_to(diff_ref[row : row + 1, :], (GROUP, LANES))
        for d in range(SUBSTEPS):
            north, south = pick_rows(odd, a_ref, b_ref, d, rows)
            wet[height + d], spread[height + d] = spread_out(north)
            wet[-1 - d], spread[-1 - d] = spread_out(south)
        half = pl.ds((chunks_all // 2) * GROUP, GROUP)
        edge_wet, edge_spread = spread_out(jnp.where(to_east, fe_ref[half, :], fw_ref[half, :]))

        def coupling(m, s, m_n, s_n):
            return 0.5 * (s + s_n) * m * m_n

        for row in range(low, high):
            m, s = wet[row], spread[row]
            m_e, m_w = sides(m, edge_wet, row)
            s_e, s_w = sides(s, edge_spread, row)
            north = coupling(m, s, wet[row + 1], spread[row + 1])
            south = coupling(m, s, wet[row - 1], spread[row - 1])
            east = coupling(m, s, m_e, s_e)
            west = coupling(m, s, m_w, s_w)
            at = row - low
            coef[at, 0] = 1.0 - (north + south + east + west)
            coef[at, 1] = north
            coef[at, 2] = south
            coef[at, 3] = east
            coef[at, 4] = west
        span = range(-1, height + 1)
        m_n = edge_neighbours(edge_wet, inner(wet, span))
        s_n = edge_neighbours(edge_spread, inner(spread, span))
        total = jnp.zeros((GROUP, LANES), F32)
        for i in range(4):
            c = coupling(edge_wet, edge_spread, m_n[i], s_n[i])
            edge_coef[1 + i] = c
            total = total + c
        edge_coef[0] = 1.0 - total

    from_east = fe_ref[pl.ds(step * GROUP, GROUP), :]
    from_west = fw_ref[pl.ds(step * GROUP, GROUP), :]
    for part in range(2):
        rows = pl.ds((2 * step + part) * GROUP, GROUP)
        base = part * GROUP * height
        value = {
            row: tracer_ref[pl.ds(base + row, GROUP, stride=height), :] for row in range(height)
        }
        for d in range(SUBSTEPS):
            value[height + d], value[-1 - d] = pick_rows(odd, a_ref, b_ref, d, rows)
        if part == 0:
            edges = jnp.where(to_east, from_east, from_west)
        else:
            edges = jnp.where(
                to_east, pltpu.roll(from_east, LANES - 3, 1), pltpu.roll(from_west, 3, 1)
            )
        for s in range(SUBSTEPS):
            reach = SUBSTEPS - 1 - s
            fresh = {}
            for row in range(-reach, height + reach):
                at = row - low
                east, west = sides(value[row], edges, row)
                fresh[row] = (
                    coef[at, 0] * value[row]
                    + (coef[at, 1] * value[row + 1] + coef[at, 2] * value[row - 1])
                    + (coef[at, 3] * east + coef[at, 4] * west)
                )
            if reach:
                n = edge_neighbours(edges, inner(value, range(1 - reach, height + reach - 1)))
                edges = (
                    edge_coef[0] * edges
                    + (edge_coef[1] * n[0] + edge_coef[2] * n[1])
                    + (edge_coef[3] * n[2] + edge_coef[4] * n[3])
                )
            value = fresh
        for row in range(height):
            out_ref[pl.ds(base + row, GROUP, stride=height), :] = value[row]


def remap_kernel(tracers, height, owners, owner_ref, surface_ref, cell_ref, column_ref, weight_ref, out_ref, picked_ref, total_ref):
    pad = 2 * GROUP
    total_ref[...] = jnp.zeros_like(total_ref)
    column = lax.broadcasted_iota(jnp.int32, (ACOL, LANES), 0)

    def one(g, unused):
        rows = pl.ds(g * GROUP, GROUP)
        cell = cell_ref[rows, :]
        at_lane = cell % LANES
        at_row = cell // LANES
        found = [jnp.zeros((GROUP, LANES), F32)] * tracers
        for row in range(height):
            here = at_row == row
            for k in range(tracers):
                source = jnp.broadcast_to(surface_ref[k, row : row + 1, :], (GROUP, LANES))
                found[k] = jnp.where(here, take_lanes(source, at_lane), found[k])
        weight = weight_ref[rows, :]
        for k in range(tracers):
            picked_ref[pl.ds(g * (GROUP * pad) + k, GROUP, stride=pad), :] = found[k] * weight
        for j in range(GROUP):
            block = g * GROUP + j
            value = picked_ref[pl.ds(block * pad, pad), :]
            coarse = value.astype(jnp.bfloat16)
            fine = (value - coarse.astype(F32)).astype(jnp.bfloat16)
            chosen = (column == column_ref[pl.ds(block, 1), :]).astype(F32).astype(jnp.bfloat16)
            product = lax.dot_general(
                jnp.concatenate([coarse, fine], axis=0),
                chosen,
                (((1,), (1,)), ((), ())),
                preferred_element_type=F32,
            )
            owner = owner_ref[block]
            total_ref[owner] = total_ref[owner] + (product[:pad] + product[pad:])
        return unused

    lax.fori_loop(0, cell_ref.shape[0] // GROUP, one, 0)

    def write(o, unused):
        for half in range(ACOL // LANES):
            out_ref[o, pl.ds(half * tracers, tracers), :] = total_ref[
                o, pl.ds(0, tracers), pl.ds(half * LANES, LANES)
            ]
        return unused

    lax.fori_loop(0, owners, write, 0)


def sum_kernel(tracers, parts_ref, out_ref):
    total = jnp.sum(parts_ref[...], axis=0)
    for half in range(ACOL // LANES):
        out_ref[:, half * LANES : (half + 1) * LANES] = total[half * tracers : (half + 1) * tracers]


def routes(lon, lat):
    def device(i, j):
        return i * lat + j

    def swaps(first, stop):
        found = []
        for i in range(lon):
            for j in range(first, stop, 2):
                found += [(device(i, j), device(i, j + 1)), (device(i, j + 1), device(i, j))]
        return found

    fold = [(device(i, lat - 1), device(lon - 1 - i, lat - 1)) for i in range(lon)]
    east = [(device(i, j), device((i + 1) % lon, j)) for i in range(lon) for j in range(lat)]
    west = [(b, a) for a, b in east]
    return swaps(1, lat - 1) + fold, swaps(0, lat), east, west


def whole():
    return pl.BlockSpec(memory_space=pltpu.VMEM)


def scalars():
    return pl.BlockSpec(memory_space=pltpu.SMEM)


def on_device(lon, lat, tracer, ocean_mask, diffusivity, remap_cell, remap_column, remap_weight, remap_owner):
    tracers, levels, height, breadth = tracer.shape
    layers = tracers * levels
    chunks = layers // GROUP
    owners = lon * lat
    both = ("lon", "lat")
    route_a, route_b, route_east, route_west = routes(lon, lat)
    lat_index = lax.axis_index("lat")
    info = jnp.stack([lat_index % 2, (lat_index == lat - 1).astype(jnp.int32)]).astype(jnp.int32)
    flat = tracer.reshape(layers * height, breadth)
    shape = jax.ShapeDtypeStruct
    rows = layers + 2 * GROUP

    with jax.named_scope("pack"):
        send_a, send_b, edges = pl.pallas_call(
            functools.partial(pack_kernel, height, chunks),
            out_shape=(
                shape((SUBSTEPS, rows - GROUP, LANES), F32),
                shape((SUBSTEPS, rows - GROUP, LANES), F32),
                shape((rows, LANES), F32),
            ),
            in_specs=[scalars(), whole(), whole(), whole()],
            out_specs=(whole(), whole(), whole()),
        )(info, flat, ocean_mask, diffusivity)
    got_a = lax.ppermute(send_a, both, route_a)
    got_b = lax.ppermute(send_b, both, route_b)

    with jax.named_scope("remap"):
        partial = pl.pallas_call(
            functools.partial(remap_kernel, tracers, height, owners),
            out_shape=shape((owners, tracers * ACOL // LANES, LANES), F32),
            grid=(1,),
            in_specs=[
                scalars(),
                pl.BlockSpec((tracers, height, LANES), lambda i: (0, 0, 0)),
                whole(),
                whole(),
                whole(),
            ],
            out_specs=whole(),
            scratch_shapes=[
                pltpu.VMEM((remap_cell.shape[0] * 2 * GROUP, LANES), F32),
                pltpu.VMEM((owners, 2 * GROUP, ACOL), F32),
            ],
        )(
            remap_owner.reshape(-1),
            tracer.reshape(tracers, levels * height, breadth),
            remap_cell,
            remap_column,
            remap_weight,
        )
    parts = lax.all_to_all(partial, both, 0, 0, tiled=True)

    with jax.named_scope("columns"):
        send_east, send_west = pl.pallas_call(
            functools.partial(columns_kernel, height, chunks),
            out_shape=(shape((rows // 2, LANES), F32), shape((rows // 2, LANES), F32)),
            in_specs=[scalars(), whole(), whole(), whole()],
            out_specs=(whole(), whole()),
        )(info, got_a, got_b, edges)
    from_west = lax.ppermute(send_east, both, route_east)
    from_east = lax.ppermute(send_west, both, route_west)

    block = pl.BlockSpec((levels * height, LANES), lambda i: (i, 0))
    with jax.named_scope("stencil"):
        updated = pl.pallas_call(
            functools.partial(stencil_kernel, height),
            out_shape=shape(flat.shape, F32),
            grid=(tracers,),
            in_specs=[scalars(), block, whole(), whole(), whole(), whole(), whole(), whole()],
            out_specs=block,
            scratch_shapes=[
                pltpu.VMEM((height + 4, 5, GROUP, LANES), F32),
                pltpu.VMEM((5, GROUP, LANES), F32),
            ],
        )(info, flat, ocean_mask, diffusivity, got_a, got_b, from_east, from_west)

    with jax.named_scope("sum"):
        atmosphere = pl.pallas_call(
            functools.partial(sum_kernel, tracers),
            out_shape=shape((tracers, ACOL), F32),
            in_specs=[whole()],
            out_specs=whole(),
        )(parts)
    return updated.reshape(tracer.shape), atmosphere


def solution(mesh):
    in_specs = (
        P("member", None, "lat", "lon"),
        P("lat", "lon"),
        P("lat", "lon"),
        P(("lon", "lat"), None),
        P(("lon", "lat"), None),
        P(("lon", "lat"), None),
        P(("lon", "lat"), None),
    )
    out_specs = (P("member", None, "lat", "lon"), P("member", ("lon", "lat")))
    return jax.shard_map(
        functools.partial(on_device, mesh.shape["lon"], mesh.shape["lat"]),
        mesh=mesh,
        in_specs=in_specs,
        out_specs=out_specs,
        check_vma=False,
    )
```

time: 265 us -> 57.9 us (0.22)
  the two profiles are of different devices: /device:TPU:0 before, /device:TPU:7 now
where the time goes in v1:
time: 57.9 us; the launch traced here: 57.4 us
  Pallas kernels  29.9 us (52%)
  starting transfers between devices  14.6 us (25%)
  waiting for transfers between devices  9.42 us (16%)
  local copies, waits for them, and re-layouts  2.1 us (4%)
  between operations  0.66 us (1%)
  other arithmetic  0.61 us (1%)
    pallas_call x1, Pallas kernels, on_device(): pl.pallas_call(functools.partial(stencil_kernel, height), out_shape=shape...  11.2 us
    pallas_call x1, Pallas kernels, on_device(): pl.pallas_call(functools.partial(remap_kernel, tracers, height, owners),...  9.86 us
    all_to_all x1, starting transfers between devices, on_device(): parts = lax.all_to_all(partial, both, 0, 0, tiled=True)  6.67 us
    ppermute x1, starting transfers between devices, on_device(): got_a = lax.ppermute(send_a, both, route_a)  4.88 us
    ppermute x1, waiting for transfers between devices, on_device(): got_a = lax.ppermute(send_a, both, route_a)  4.21 us
    pallas_call x1, Pallas kernels, on_device(): pl.pallas_call(functools.partial(pack_kernel, height, chunks), out_shape=...  4.1 us
    ppermute x1, waiting for transfers between devices, on_device(): from_west = lax.ppermute(send_east, both, route_east)  3.5 us
    pallas_call x1, Pallas kernels, on_device(): pl.pallas_call(functools.partial(columns_kernel, height, chunks), out_sha...  3.22 us
  transfers between devices with their start and end apart: 5, of which 3 were waited for; matrix products, arithmetic and copies ran while one was open for 1% of the time, Pallas kernels for 32%

profile of v1, /device:TPU:7, one launch (start us, length us, event | category | flops | bytes accessed | tf_op | source)
XLA Modules:
  0.0 57.4 jit_solution(13821217049397822123)
XLA Ops:
  0.6 9.9 %remap.1 = f32[16,20,128]{2,1,0:T(8,128)} custom-call(s32[128]{0:T(128)} %bitcast.10, f32[10,256,128]{2,1,0:T(8,128)} %bitcast.6, s32[128,128]{1,0:T(8,128)} %cell_ref.1, s32[128,128]{1,0:T(8,128)} %column_ref.1, f32[128,128]{1,0:T(8,128)} %weight_ref.1), custom_call_target="tpu_custom_call" | custom-call | tf_op jit(solution)/shard_map/remap/pallas_call | solution.py:360
  10.5 6.7 %all-to-all-start = ((f32[16,20,128]{2,1,0:T(8,128)}), f32[16,20,128]{2,1,0:T(8,128)S(1)}, u32[]{:S(2)}, u32[]{:S(2)}) async-start(f32[16,20,128]{2,1,0:T(8,128)} %remap.1), calls=%async_computation | async-start | bytes 393216 | tf_op jit(solution)/shard_map/all_to_all | solution.py:383
  17.2 0.6 %pad_add_fusion.info_ref = s32[2]{0:T(128)} fusion(s32[1]{0:T(128)} %bitcast.1, s32[1]{0:T(128)} %bitcast), kind=kLoop, calls=%fused_computation | loop fusion | flops 2 | bytes 16 | tf_op jit(solution)/shard_map/stack | solution.py:340
  17.8 4.1 %pack.1 = (f32[3,168,128]{2,1,0:T(8,128)}, f32[3,168,128]{2,1,0:T(8,128)}, f32[176,128]{1,0:T(8,128)}) custom-call(s32[2]{0:T(128)} %pad_add_fusion.info_ref, f32[2560,128]{1,0:T(8,128)} %bitcast.7, s32[16,128]{1,0:T(8,128)} %mask_ref.3, f32[16,128]{1,0:T(8,128)} %diff_ref.3), custom_call_target="tpu_custom_call" | custom-call | tf_op jit(solution)/shard_map/pack/pallas_call | solution.py:346
  21.9 4.9 %collective-permute-start = (f32[3,168,128]{2,1,0:T(8,128)}, f32[3,168,128]{2,1,0:T(8,128)S(1)}, u32[]{:S(2)}, u32[]{:S(2)}) collective-permute-start(f32[3,168,128]{2,1,0:T(8,128)} %get-tuple-element.7), channel_id=1, source_target_pairs={{1,2},{2,1},{5,6},{6,5},{9,10},{10,9},{13,14},{14,13},{3,15},{7,11... | collective-permute-start | bytes 774152 | tf_op jit(solution)/shard_map/ppermute | solution.py:356
  26.8 0.1 collective-permute-start.1
  26.8 4.2 %collective-permute-done.a_ref = f32[3,168,128]{2,1,0:T(8,128)S(1)} collective-permute-done((f32[3,168,128]{2,1,0:T(8,128)}, f32[3,168,128]{2,1,0:T(8,128)S(1)}, u32[]{:S(2)}, u32[]{:S(2)}) %collective-permute-start) | collective-permute-done | bytes 258080 | tf_op jit(solution)/shard_map/ppermute | solution.py:356
  31.1 0.0 copy-start
  31.1 0.0 collective-permute-done.1.b_ref
  31.1 0.0 copy-start.1
  31.1 0.7 %copy-done = f32[3,168,128]{2,1,0:T(8,128)} copy-done((f32[3,168,128]{2,1,0:T(8,128)}, f32[3,168,128]{2,1,0:T(8,128)S(1)}, u32[]{:S(2)}) %copy-start) | copy-done | bytes 258072
  31.8 0.1 copy-done.1
  31.9 3.2 %columns.1 = (f32[88,128]{1,0:T(8,128)}, f32[88,128]{1,0:T(8,128)}) custom-call(s32[2]{0:T(128)} %pad_add_fusion.info_ref, f32[3,168,128]{2,1,0:T(8,128)} %copy-done, f32[3,168,128]{2,1,0:T(8,128)} %copy-done.1, f32[176,128]{1,0:T(8,128)} %get-tuple-element.9.m_ref), custom_call_target="tpu_custom_call" | custom-call | tf_op jit(solution)/shard_map/columns/pallas_call | solution.py:386
  35.1 3.0 %collective-permute-start.2 = (f32[88,128]{1,0:T(8,128)}, f32[88,128]{1,0:T(8,128)S(1)}, u32[]{:S(2)}, u32[]{:S(2)}) collective-permute-start(f32[88,128]{1,0:T(8,128)} %get-tuple-element.10), channel_id=1, source_target_pairs={{4,0},{5,1},{6,2},{7,3},{8,4},{9,5},{10,6},{11,7},{12,8},{13,9},{1... | collective-permute-start | bytes 135176 | tf_op jit(solution)/shard_map/ppermute | solution.py:393
  38.1 0.0 collective-permute-start.3
  38.1 1.7 %collective-permute-done.2.fe_ref = f32[88,128]{1,0:T(8,128)S(1)} collective-permute-done((f32[88,128]{1,0:T(8,128)}, f32[88,128]{1,0:T(8,128)S(1)}, u32[]{:S(2)}, u32[]{:S(2)}) %collective-permute-start.2) | collective-permute-done | bytes 45088 | tf_op jit(solution)/shard_map/ppermute | solution.py:393
  39.8 0.0 copy-start.3
  39.8 3.5 %collective-permute-done.3.fw_ref = f32[88,128]{1,0:T(8,128)S(1)} collective-permute-done((f32[88,128]{1,0:T(8,128)}, f32[88,128]{1,0:T(8,128)S(1)}, u32[]{:S(2)}, u32[]{:S(2)}) %collective-permute-start.3) | collective-permute-done | bytes 45088 | tf_op jit(solution)/shard_map/ppermute | solution.py:392
  43.3 0.0 copy-done.3
  43.3 0.0 copy-start.4
  43.3 0.6 %copy-done.4 = f32[88,128]{1,0:T(8,128)} copy-done((f32[88,128]{1,0:T(8,128)}, f32[88,128]{1,0:T(8,128)S(1)}, u32[]{:S(2)}) %copy-start.4) | copy-done | bytes 45080
  43.9 11.2 %stencil.1 = f32[2560,128]{1,0:T(8,128)} custom-call(s32[2]{0:T(128)} %pad_add_fusion.info_ref, f32[2560,128]{1,0:T(8,128)} %bitcast.8, s32[16,128]{1,0:T(8,128)} %mask_ref.3, f32[16,128]{1,0:T(8,128)} %diff_ref.3, f32[3,168,128]{2,1,0:T(8,128)} %copy-done, f32[3,168,128]{2,1,0:T(8,128)} %copy-done.1, f32[88,128]{1,0:T(8,128)} %copy-done.3, f32[88,128]{1,0:T(8,128)} %copy-done.4), custom_call_target="tpu_custom_call" | custom-call | tf_op jit(solution)/shard_map/stencil/pallas_call | solution.py:397
  55.1 0.0 all-to-all-done.parts_ref
  55.1 0.0 copy-start.2
  55.1 0.7 %copy-done.2 = f32[16,20,128]{2,1,0:T(8,128)} copy-done((f32[16,20,128]{2,1,0:T(8,128)}, f32[16,20,128]{2,1,0:T(8,128)S(1)}, u32[]{:S(2)}) %copy-start.2) | copy-done | bytes 163864
  55.8 1.6 %sum.1 = f32[10,256]{1,0:T(8,128)} custom-call(f32[16,20,128]{2,1,0:T(8,128)} %copy-done.2), custom_call_target="tpu_custom_call" | custom-call | tf_op jit(solution)/shard_map/sum/pallas_call | solution.py:410
Async XLA Ops:
  10.5 44.6 %all-to-all-start = ((f32[16,20,128]{2,1,0:T(8,128)}), f32[16,20,128]{2,1,0:T(8,128)S(1)}, u32[]{:S(2)}, u32[]{:S(2)}) async-start(f32[16,20,128]{2,1,0:T(8,128)} %remap.1), calls=%async_computation | async-start | bytes 393216 | tf_op jit(solution)/shard_map/all_to_all | solution.py:383
  21.9 9.2 %collective-permute-start = (f32[3,168,128]{2,1,0:T(8,128)}, f32[3,168,128]{2,1,0:T(8,128)S(1)}, u32[]{:S(2)}, u32[]{:S(2)}) collective-permute-start(f32[3,168,128]{2,1,0:T(8,128)} %get-tuple-element.7), channel_id=1, source_target_pairs={{1,2},{2,1},{5,6},{6,5},{9,10},{10,9},{13,14},{14,13},{3,15},{7,11... | collective-permute-start | bytes 774152 | tf_op jit(solution)/shard_map/ppermute | solution.py:356
  26.8 4.3 %collective-permute-start.1 = (f32[3,168,128]{2,1,0:T(8,128)}, f32[3,168,128]{2,1,0:T(8,128)S(1)}, u32[]{:S(2)}, u32[]{:S(2)}) collective-permute-start(f32[3,168,128]{2,1,0:T(8,128)} %get-tuple-element.8), channel_id=1, source_target_pairs={{0,1},{1,0},{2,3},{3,2},{4,5},{5,4},{6,7},{7,6},{8,9},{9,8},{10,11... | collective-permute-start | bytes 774152 | tf_op jit(solution)/shard_map/ppermute | solution.py:357
  31.1 0.7 %copy-start = (f32[3,168,128]{2,1,0:T(8,128)}, f32[3,168,128]{2,1,0:T(8,128)S(1)}, u32[]{:S(2)}) copy-start(f32[3,168,128]{2,1,0:T(8,128)S(1)} %collective-permute-done.a_ref) | copy-start | bytes 774148
  31.1 0.8 %copy-start.1 = (f32[3,168,128]{2,1,0:T(8,128)}, f32[3,168,128]{2,1,0:T(8,128)S(1)}, u32[]{:S(2)}) copy-start(f32[3,168,128]{2,1,0:T(8,128)S(1)} %collective-permute-done.1.b_ref) | copy-start | bytes 774148
  35.1 4.7 %collective-permute-start.2 = (f32[88,128]{1,0:T(8,128)}, f32[88,128]{1,0:T(8,128)S(1)}, u32[]{:S(2)}, u32[]{:S(2)}) collective-permute-start(f32[88,128]{1,0:T(8,128)} %get-tuple-element.10), channel_id=1, source_target_pairs={{4,0},{5,1},{6,2},{7,3},{8,4},{9,5},{10,6},{11,7},{12,8},{13,9},{1... | collective-permute-start | bytes 135176 | tf_op jit(solution)/shard_map/ppermute | solution.py:393
  38.1 5.2 %collective-permute-start.3 = (f32[88,128]{1,0:T(8,128)}, f32[88,128]{1,0:T(8,128)S(1)}, u32[]{:S(2)}, u32[]{:S(2)}) collective-permute-start(f32[88,128]{1,0:T(8,128)} %get-tuple-element.11), channel_id=1, source_target_pairs={{0,4},{1,5},{2,6},{3,7},{4,8},{5,9},{6,10},{7,11},{8,12},{9,13},{1... | collective-permute-start | bytes 135176 | tf_op jit(solution)/shard_map/ppermute | solution.py:392
  39.8 3.5 %copy-start.3 = (f32[88,128]{1,0:T(8,128)}, f32[88,128]{1,0:T(8,128)S(1)}, u32[]{:S(2)}) copy-start(f32[88,128]{1,0:T(8,128)S(1)} %collective-permute-done.2.fe_ref) | copy-start | bytes 135172
  43.3 0.6 %copy-start.4 = (f32[88,128]{1,0:T(8,128)}, f32[88,128]{1,0:T(8,128)S(1)}, u32[]{:S(2)}) copy-start(f32[88,128]{1,0:T(8,128)S(1)} %collective-permute-done.3.fw_ref) | copy-start | bytes 135172
  55.1 0.7 %copy-start.2 = (f32[16,20,128]{2,1,0:T(8,128)}, f32[16,20,128]{2,1,0:T(8,128)S(1)}, u32[]{:S(2)}) copy-start(f32[16,20,128]{2,1,0:T(8,128)S(1)} %all-to-all-done.parts_ref) | copy-start | bytes 491524

commit v2 on v0

v2 whole, which is shorter than its diff:
```python
import functools

import jax
import jax.numpy as jnp
from jax import lax
from jax.experimental import pallas as pl
from jax.experimental.pallas import tpu as pltpu
from jax.sharding import PartitionSpec as P

ACOL = 256
SUBSTEPS = 3
LANES = 128
GROUP = 8
F32 = jnp.float32

STRIP = 18
PER = 7
SETS = 3
HALF = 6


def lane_iota():
    return lax.broadcasted_iota(jnp.int32, (GROUP, LANES), 1)


def shift(value, amount):
    amount = amount % LANES
    return pltpu.roll(value, amount, 1) if amount else value


def take_lanes(value, index):
    return jnp.take_along_axis(value, index, axis=1)


def is_odd():
    return lax.axis_index("lat") % 2


def base_of(chunk):
    return chunk // PER, STRIP * (chunk % PER)


def message_rows(layers):
    return SUBSTEPS * (layers + GROUP), SUBSTEPS * (layers + GROUP) + SUBSTEPS * SETS * GROUP


def pack_kernel(
    height,
    chunks,
    parts,
    tracer_ref,
    mask_ref,
    diff_ref,
    a_ref,
    b_ref,
    p_ref,
    x_ref,
    tile,
    wet_tile,
    spread_tile,
    sems,
):
    odd = jnp.full((GROUP, LANES), is_odd()) == 1
    top = (lax.axis_index("lat") == lax.axis_size("lat") - 1).astype(jnp.int32)
    each = chunks // parts
    size = each * GROUP * height
    copies = [
        pltpu.make_async_copy(
            tracer_ref.at[pl.ds(p * size, size)], tile.at[pl.ds(p * size, size)], sems.at[p]
        )
        for p in range(parts)
    ]
    copies.append(pltpu.make_async_copy(mask_ref, wet_tile, sems.at[parts]))
    copies.append(pltpu.make_async_copy(diff_ref, spread_tile, sems.at[parts + 1]))
    for copy in copies:
        copy.start()

    lane = lane_iota()
    place = lane % STRIP
    is_top = jnp.full((GROUP, LANES), top) == 1
    flip = jnp.where(is_top, LANES - 1 - lane, lane)
    flip_strip = jnp.where(is_top & (place < 2 * HALF), lane - place + 2 * HALF - 1 - place, lane)
    stride = (chunks + 1) * GROUP
    strips_at = SUBSTEPS * stride

    def send(c, value):
        for d in range(SUBSTEPS):
            rows = pl.ds(d * stride + c * GROUP, GROUP)
            near, far = value[d], value[height - 1 - d]
            a_ref[rows, :] = take_lanes(jnp.where(odd, far, near), flip)
            b_ref[rows, :] = jnp.where(odd, near, far)

    strips = {}

    def edge(c, value):
        which, base = base_of(c)
        here = (lane >= base) & (lane < base + 2 * HALF)
        for row in range(height):
            before = strips.get((row, which), jnp.zeros((GROUP, LANES), F32))
            strips[row, which] = jnp.where(here, shift(value[row], base + HALF), before)

    for p in range(parts):
        copies[p].wait()
        for c in range(p * each, (p + 1) * each):
            value = {}
            for row in range(height):
                value[row] = tile[pl.ds(c * GROUP * height + row, GROUP, stride=height), :]
                x_ref[row, pl.ds(c * GROUP, GROUP), :] = value[row]
            send(c, value)
            edge(c, value)

    copies[parts].wait()
    copies[parts + 1].wait()
    sub = lax.broadcasted_iota(jnp.int32, (GROUP, LANES), 0)
    value = {}
    for row in range(height):
        wet = jnp.broadcast_to(wet_tile[row : row + 1, :].astype(F32), (GROUP, LANES))
        spread = jnp.broadcast_to(spread_tile[row : row + 1, :], (GROUP, LANES))
        value[row] = jnp.where(sub == 0, wet, jnp.where(sub == 1, spread, 0.0))
    send(chunks, value)
    edge(chunks, value)

    zero = jnp.zeros((GROUP, LANES), F32)
    for row in range(height):
        for g in range(SETS):
            p_ref[row, g] = strips.get((row, g), zero)
    for d in range(SUBSTEPS):
        for g in range(SETS):
            near, far = strips.get((d, g), zero), strips.get((height - 1 - d, g), zero)
            rows = pl.ds(strips_at + (d * SETS + g) * GROUP, GROUP)
            a_ref[rows, :] = take_lanes(jnp.where(odd, far, near), flip_strip)
            b_ref[rows, :] = jnp.where(odd, near, far)


def pick_rows(odd, a_ref, b_ref, rows):
    first = a_ref[rows, :]
    second = b_ref[rows, :]
    return jnp.where(odd, first, second), jnp.where(odd, second, first)


def own_strips(height, chunks, a_ref, b_ref, p_ref, depth):
    odd = jnp.full((GROUP, LANES), is_odd()) == 1
    strips_at = SUBSTEPS * (chunks + 1) * GROUP
    found = {}
    for g in range(SETS):
        for row in range(height):
            found[row, g] = p_ref[row, g]
        for d in range(depth):
            rows = pl.ds(strips_at + (d * SETS + g) * GROUP, GROUP)
            found[height + d, g], found[-1 - d, g] = pick_rows(odd, a_ref, b_ref, rows)
    return found


def columns_kernel(height, chunks, a_ref, b_ref, p_ref, east_ref, west_ref):
    found = own_strips(height, chunks, a_ref, b_ref, p_ref, SUBSTEPS - 1)
    place = lane_iota() % STRIP
    rows = height + 2 * (SUBSTEPS - 1)
    for block in range(-(-rows // 6)):
        for g in range(SETS):
            east = west = jnp.zeros((GROUP, LANES), F32)
            for i in range(min(6, rows - 6 * block)):
                value = found[6 * block + i - (SUBSTEPS - 1), g]
                here = (place >= 3 * i) & (place < 3 * i + 3)
                east = jnp.where(here, shift(value, 3 * i - 3), east)
                west = jnp.where(here, shift(value, 3 * i - HALF), west)
            at = pl.ds((block * SETS + g) * GROUP, GROUP)
            east_ref[at, :] = east
            west_ref[at, :] = west


def coupling(m, s, m_n, s_n):
    return 0.5 * (s + s_n) * m * m_n


def factors(wet, spread, rows):
    north = {
        row: coupling(wet[row], spread[row], wet[row + 1], spread[row + 1])
        for row in range(rows[0] - 1, rows[-1] + 1)
    }
    found = {}
    for row in rows:
        m, s = wet[row], spread[row]
        east = coupling(m, s, shift(m, -1), shift(s, -1))
        west = shift(east, 1)
        south = north[row - 1]
        found[row] = (1.0 - (north[row] + south + east + west), north[row], south, east, west)
    return found


def substep(value, row, weight):
    centre = value[row]
    return (
        weight[0] * centre
        + (weight[1] * value[row + 1] + weight[2] * value[row - 1])
        + (weight[3] * shift(centre, -1) + weight[4] * shift(centre, 1))
    )


def tile_kernel(height, chunks, x_ref, mask_ref, diff_ref, a_ref, b_ref, out_ref, coef):
    odd = jnp.full((GROUP, LANES), is_odd()) == 1
    stride = (chunks + 1) * GROUP
    low, high = -(SUBSTEPS - 1), height + SUBSTEPS - 1

    def wide(ref, row):
        return jnp.broadcast_to(ref[row : row + 1, :].astype(F32), (GROUP, LANES))

    wet, spread = {}, {}
    for row in range(height):
        wet[row] = wide(mask_ref, row)
        spread[row] = wide(diff_ref, row)
    for d in range(SUBSTEPS):
        at = d * stride + chunks * GROUP
        for held, row in ((wet, at), (spread, at + 1)):
            first, second = wide(a_ref, row), wide(b_ref, row)
            held[height + d] = jnp.where(odd, first, second)
            held[-1 - d] = jnp.where(odd, second, first)
    weights = factors(wet, spread, range(low, high))
    for row in range(low, high):
        for i in range(5):
            coef[row - low, i] = weights[row][i]

    def one(c):
        rows = pl.ds(c * GROUP, GROUP)
        value = {row: x_ref[row, rows, :] for row in range(height)}
        for d in range(SUBSTEPS):
            value[height + d], value[-1 - d] = pick_rows(
                odd, a_ref, b_ref, pl.ds(d * stride + c * GROUP, GROUP)
            )
        for s in range(SUBSTEPS):
            reach = SUBSTEPS - 1 - s
            value = {
                row: substep(value, row, [coef[row - low, i] for i in range(5)])
                for row in range(-reach, height + reach)
            }
        for row in range(height):
            out_ref[row, rows, :] = value[row]

    def pair(i, unused):
        one(2 * i)
        one(2 * i + 1)
        return unused

    lax.fori_loop(0, chunks // 2, pair, 0)


def edge_kernel(
    height, chunks, parts, y_ref, a_ref, b_ref, p_ref, fe_ref, fw_ref, out_ref, final, tile, sems
):
    lane = lane_iota()
    place = lane % STRIP
    strips = own_strips(height, chunks, a_ref, b_ref, p_ref, SUBSTEPS)
    low = -(SUBSTEPS - 1)
    for (row, g), own in strips.items():
        value = jnp.where(place >= 2 * HALF, shift(own, HALF), own)
        at = row - low
        if 0 <= at < height + 2 * (SUBSTEPS - 1):
            block, i = at // 6, at % 6
            rows = pl.ds((block * SETS + g) * GROUP, GROUP)
            east = shift(fe_ref[rows, :], HALF - 3 * i)
            west = shift(fw_ref[rows, :], HALF + 3 - 3 * i)
            value = jnp.where(
                (place >= HALF) & (place < 2 * HALF), jnp.where(place < 9, east, west), value
            )
        strips[row, g] = value
    which, base = base_of(chunks)
    wet, spread = {}, {}
    for row in range(-SUBSTEPS, height + SUBSTEPS):
        value = strips[row, which]
        for held, i in ((wet, 0), (spread, 1)):
            held[row] = take_lanes(
                jnp.broadcast_to(value[i : i + 1, :], (GROUP, LANES)), base + place
            )
    weights = factors(wet, spread, range(low, height - low))
    for g in range(SETS):
        value = {row: strips[row, g] for row in range(-SUBSTEPS, height + SUBSTEPS)}
        for s in range(SUBSTEPS):
            reach = SUBSTEPS - 1 - s
            value = {
                row: substep(value, row, weights[row]) for row in range(-reach, height + reach)
            }
        for row in range(height):
            final[row, g] = jnp.where(
                (place >= HALF) & (place < HALF + 3), shift(value[row], -HALF), value[row]
            )
    at_edge = (lane < 3) | (lane >= LANES - 3)
    each = chunks // parts
    size = each * GROUP * height
    copies = []
    for p in range(parts):
        for c in range(p * each, (p + 1) * each):
            which, base = base_of(c)
            for row in range(height):
                pulled = shift(final[row, which], LANES - 3 - (base + 3))
                tile[pl.ds(c * GROUP * height + row, GROUP, stride=height), :] = jnp.where(
                    at_edge, pulled, y_ref[row, pl.ds(c * GROUP, GROUP), :]
                )
        copy = pltpu.make_async_copy(
            tile.at[pl.ds(p * size, size)], out_ref.at[pl.ds(p * size, size)], sems.at[p]
        )
        copy.start()
        copies.append(copy)
    for copy in copies:
        copy.wait()


def remap_kernel(
    tracers,
    levels,
    height,
    owners,
    owner_ref,
    x_ref,
    cell_ref,
    column_ref,
    weight_ref,
    out_ref,
    even_ref,
    odd_ref,
    total_ref,
    owners_ref,
    sem,
):
    copy = pltpu.make_async_copy(owner_ref, owners_ref, sem)
    copy.start()
    pad = 2 * GROUP
    groups = cell_ref.shape[0] // GROUP
    total_ref[...] = jnp.zeros_like(total_ref)
    column = lax.broadcasted_iota(jnp.int32, (ACOL, LANES), 0)

    def gather(g, picked_ref):
        rows = pl.ds(g * GROUP, GROUP)
        cell = cell_ref[rows, :]
        at_lane = cell % LANES
        at_row = cell // LANES
        found = [jnp.zeros((GROUP, LANES), F32)] * tracers
        for row in range(height):
            here = at_row == row
            for k in range(tracers):
                source = jnp.broadcast_to(x_ref[row, k * levels : k * levels + 1, :], (GROUP, LANES))
                found[k] = jnp.where(here, take_lanes(source, at_lane), found[k])
        weight = weight_ref[rows, :]
        for k in range(tracers):
            picked_ref[pl.ds(k, GROUP, stride=pad), :] = found[k] * weight

    def add(g, picked_ref):
        for j in range(GROUP):
            block = g * GROUP + j
            value = picked_ref[pl.ds(j * pad, pad), :]
            coarse = value.astype(jnp.bfloat16)
            fine = (value - coarse.astype(F32)).astype(jnp.bfloat16)
            chosen = (column == column_ref[pl.ds(block, 1), :]).astype(F32).astype(jnp.bfloat16)
            product = lax.dot_general(
                jnp.concatenate([coarse, fine], axis=0),
                chosen,
                (((1,), (1,)), ((), ())),
                preferred_element_type=F32,
            )
            owner = owners_ref[block]
            total_ref[owner] = total_ref[owner] + (product[:pad] + product[pad:])

    def two(i, unused):
        gather(2 * i + 1, odd_ref)
        add(2 * i, even_ref)
        gather(2 * i + 2, even_ref)
        add(2 * i + 1, odd_ref)
        return unused

    gather(0, even_ref)
    copy.wait()
    lax.fori_loop(0, groups // 2 - 1, two, 0)
    gather(groups - 1, odd_ref)
    add(groups - 2, even_ref)
    add(groups - 1, odd_ref)

    def write(o, unused):
        for half in range(ACOL // LANES):
            out_ref[o, pl.ds(half * tracers, tracers), :] = total_ref[
                o, pl.ds(0, tracers), pl.ds(half * LANES, LANES)
            ]
        return unused

    lax.fori_loop(0, owners, write, 0)


def sum_kernel(tracers, parts_ref, out_ref):
    total = jnp.sum(parts_ref[...], axis=0)
    for half in range(ACOL // LANES):
        out_ref[:, half * LANES : (half + 1) * LANES] = total[half * tracers : (half + 1) * tracers]


def routes(lon, lat):
    def device(i, j):
        return i * lat + j

    def swaps(first, stop):
        found = []
        for i in range(lon):
            for j in range(first, stop, 2):
                found += [(device(i, j), device(i, j + 1)), (device(i, j + 1), device(i, j))]
        return found

    fold = [(device(i, lat - 1), device(lon - 1 - i, lat - 1)) for i in range(lon)]
    east = [(device(i, j), device((i + 1) % lon, j)) for i in range(lon) for j in range(lat)]
    west = [(b, a) for a, b in east]
    return swaps(1, lat - 1) + fold, swaps(0, lat), east, west


def in_vmem(array):
    return pltpu.with_memory_space_constraint(array, pltpu.VMEM)


def in_hbm(array):
    return pltpu.with_memory_space_constraint(array, pltpu.HBM)


def vmem():
    return pl.BlockSpec(memory_space=pltpu.VMEM)


def anywhere():
    return pl.BlockSpec(memory_space=pltpu.HBM)


def settings(microseconds):
    return dict(
        compiler_params=pltpu.CompilerParams(vmem_limit_bytes=16 * 1024 * 1024),
        cost_estimate=pl.CostEstimate(
            flops=0, transcendentals=0, bytes_accessed=int(microseconds * 3.5e6)
        ),
    )


def parts_of(chunks):
    return 5 if chunks % 5 == 0 else 1


def pack(height, layers, flat, ocean_mask, diffusivity):
    chunks = layers // GROUP
    parts = parts_of(chunks)
    with jax.named_scope("pack"):
        return pl.pallas_call(
            functools.partial(pack_kernel, height, chunks, parts),
            **settings(2),
            out_shape=(
                pltpu.VMEM((message_rows(layers)[1], LANES), F32),
                pltpu.VMEM((message_rows(layers)[1], LANES), F32),
                pltpu.VMEM((height, SETS, GROUP, LANES), F32),
                pltpu.VMEM((height, layers, LANES), F32),
            ),
            in_specs=[anywhere()] * 3,
            out_specs=(vmem(),) * 4,
            scratch_shapes=[
                pltpu.VMEM(flat.shape, F32),
                pltpu.VMEM(ocean_mask.shape, ocean_mask.dtype),
                pltpu.VMEM(diffusivity.shape, F32),
                pltpu.SemaphoreType.DMA((parts + 2,)),
            ],
        )(in_hbm(flat), in_hbm(ocean_mask), in_hbm(diffusivity))


def remap(owners, tracers, levels, x, remap_cell, remap_column, remap_weight, remap_owner):
    blocks = remap_cell.shape[0]
    height = x.shape[0]
    with jax.named_scope("remap"):
        return pl.pallas_call(
            functools.partial(remap_kernel, tracers, levels, height, owners),
            **settings(6),
            out_shape=pltpu.VMEM((owners, 3 * GROUP, LANES), F32),
            in_specs=[anywhere()] + [vmem()] * 4,
            out_specs=vmem(),
            scratch_shapes=[
                pltpu.VMEM((2 * GROUP * GROUP, LANES), F32),
                pltpu.VMEM((2 * GROUP * GROUP, LANES), F32),
                pltpu.VMEM((owners, 2 * GROUP, ACOL), F32),
                pltpu.SMEM((blocks,), jnp.int32),
                pltpu.SemaphoreType.DMA,
            ],
        )(
            in_hbm(remap_owner.reshape(-1)),
            in_vmem(x),
            in_vmem(remap_cell),
            in_vmem(remap_column),
            in_vmem(remap_weight),
        )


def columns(height, layers, got_a, got_b, p):
    rows = -(-(height + 2 * (SUBSTEPS - 1)) // 6) * SETS * GROUP
    with jax.named_scope("columns"):
        return pl.pallas_call(
            functools.partial(columns_kernel, height, layers // GROUP),
            **settings(1),
            out_shape=(pltpu.VMEM((rows, LANES), F32), pltpu.VMEM((rows, LANES), F32)),
            in_specs=[vmem()] * 3,
            out_specs=(vmem(), vmem()),
        )(in_vmem(got_a), in_vmem(got_b), in_vmem(p))


def tile_steps(height, layers, x, ocean_mask, diffusivity, got_a, got_b):
    with jax.named_scope("tile"):
        return pl.pallas_call(
            functools.partial(tile_kernel, height, layers // GROUP),
            **settings(4),
            out_shape=pltpu.VMEM(x.shape, F32),
            in_specs=[vmem()] * 5,
            out_specs=vmem(),
            scratch_shapes=[pltpu.VMEM((height + 2 * (SUBSTEPS - 1), 5, GROUP, LANES), F32)],
        )(in_vmem(x), in_vmem(ocean_mask), in_vmem(diffusivity), in_vmem(got_a), in_vmem(got_b))


def edge_steps(height, layers, y, got_a, got_b, p, from_east, from_west):
    chunks = layers // GROUP
    parts = parts_of(chunks)
    with jax.named_scope("edges"):
        return pl.pallas_call(
            functools.partial(edge_kernel, height, chunks, parts),
            **settings(4),
            out_shape=jax.ShapeDtypeStruct((layers * height, LANES), F32),
            in_specs=[vmem()] * 6,
            out_specs=anywhere(),
            scratch_shapes=[
                pltpu.VMEM((height, SETS, GROUP, LANES), F32),
                pltpu.VMEM((layers * height, LANES), F32),
                pltpu.SemaphoreType.DMA((parts,)),
            ],
        )(
            in_vmem(y),
            in_vmem(got_a),
            in_vmem(got_b),
            in_vmem(p),
            in_vmem(from_east),
            in_vmem(from_west),
        )


def on_device(lon, lat, tracer, ocean_mask, diffusivity, remap_cell, remap_column, remap_weight, remap_owner):
    tracers, levels, height, breadth = tracer.shape
    layers = tracers * levels
    both = ("lon", "lat")
    route_a, route_b, route_east, route_west = routes(lon, lat)
    flat = tracer.reshape(layers * height, breadth)

    send_a, send_b, p, x = pack(height, layers, flat, ocean_mask, diffusivity)
    got_a = lax.ppermute(send_a, both, route_a)
    got_b = lax.ppermute(send_b, both, route_b)

    partial = remap(
        lon * lat, tracers, levels, x, remap_cell, remap_column, remap_weight, remap_owner
    )
    parts = lax.all_to_all(partial, both, 0, 0, tiled=True)

    send_east, send_west = columns(height, layers, got_a, got_b, p)
    from_west = lax.ppermute(send_east, both, route_east)
    from_east = lax.ppermute(send_west, both, route_west)

    y = tile_steps(height, layers, x, ocean_mask, diffusivity, got_a, got_b)
    updated = edge_steps(height, layers, y, got_a, got_b, p, from_east, from_west)

    with jax.named_scope("sum"):
        atmosphere = pl.pallas_call(
            functools.partial(sum_kernel, tracers),
            **settings(1),
            out_shape=jax.ShapeDtypeStruct((tracers, ACOL), F32),
            in_specs=[vmem()],
            out_specs=vmem(),
        )(in_vmem(parts))
    return updated.reshape(tracer.shape), atmosphere


def solution(mesh):
    in_specs = (
        P("member", None, "lat", "lon"),
        P("lat", "lon"),
        P("lat", "lon"),
        P(("lon", "lat"), None),
        P(("lon", "lat"), None),
        P(("lon", "lat"), None),
        P(("lon", "lat"), None),
    )
    out_specs = (P("member", None, "lat", "lon"), P("member", ("lon", "lat")))
    return jax.shard_map(
        functools.partial(on_device, mesh.shape["lon"], mesh.shape["lat"]),
        mesh=mesh,
        in_specs=in_specs,
        out_specs=out_specs,
        check_vma=False,
    )
```

time: 265 us -> 39.6 us (0.15)
  the two profiles are of different devices: /device:TPU:0 before, /device:TPU:15 now
where the time goes in v2:
time: 39.6 us; the launch traced here: 39.3 us
  Pallas kernels  16.7 us (42%)
  starting transfers between devices  11.2 us (28%)
  waiting for transfers between devices  10.5 us (27%)
  between operations  0.77 us (2%)
    ppermute x1, waiting for transfers between devices, on_device(): got_a = lax.ppermute(send_a, both, route_a)  10.5 us
    all_to_all x1, starting transfers between devices, on_device(): parts = lax.all_to_all(partial, both, 0, 0, tiled=True)  6.57 us
    pallas_call x1, Pallas kernels, remap(): pl.pallas_call(functools.partial(remap_kernel, tracers, levels, height, o...  5.94 us
    pallas_call x1, Pallas kernels, tile_steps(): pl.pallas_call(functools.partial(tile_kernel, height, layers // GROUP), *...  4.19 us
    pallas_call x1, Pallas kernels, edge_steps(): pl.pallas_call(functools.partial(edge_kernel, height, chunks, parts), **s...  3.78 us
    ppermute x1, starting transfers between devices, on_device(): got_a = lax.ppermute(send_a, both, route_a)  3.08 us
    pallas_call x1, Pallas kernels, pack(): pl.pallas_call(functools.partial(pack_kernel, height, chunks, parts), **s...  2.03 us
    ppermute x1, starting transfers between devices, on_device(): from_west = lax.ppermute(send_east, both, route_east)  1.45 us
  transfers between devices with their start and end apart: 5, of which 1 were waited for; matrix products, arithmetic and copies ran while one was open for 0% of the time, Pallas kernels for 21%

profile of v2, /device:TPU:15, one launch (start us, length us, event | category | flops | bytes accessed | tf_op | source)
XLA Modules:
  0.0 39.3 jit_solution(4357223688587329880)
XLA Ops:
  0.6 0.0 copy-start.2
  0.6 0.0 copy-start.1
  0.7 0.0 copy-start
  0.7 2.0 %pack.1 = (f32[576,128]{1,0:T(8,128)S(1)}, f32[576,128]{1,0:T(8,128)S(1)}, f32[16,3,8,128]{3,2,1,0:T(8,128)S(1)}, f32[16,160,128]{2,1,0:T(8,128)S(1)}) custom-call(f32[2560,128]{1,0:T(8,128)} %bitcast.4, s32[16,128]{1,0:T(8,128)} %mask_ref.3, f32[16,128]{1,0:T(8,128)} %diff_ref.3), custom_call_target="tpu_custom_call" | custom-call | bytes 7000000 | tf_op jit(solution)/shard_map/pack/pallas_call | solution.py:441
  2.7 0.0 copy-done.2
  2.7 0.0 copy-done.1
  2.7 0.0 copy-done
  2.7 0.0 copy-start.3
  2.7 0.0 copy-start.4
  2.8 5.9 %remap.1 = f32[16,24,128]{2,1,0:T(8,128)} custom-call(s32[128]{0:T(128)} %bitcast.5, f32[16,160,128]{2,1,0:T(8,128)S(1)} %get-tuple-element.8.x_ref, s32[128,128]{1,0:T(8,128)S(1)} %copy-done, s32[128,128]{1,0:T(8,128)S(1)} %copy-done.1, f32[128,128]{1,0:T(8,128)S(1)} %copy-done.2), custom_call_target="tpu_custom_call" | custom-call | bytes 21000000 | tf_op jit(solution)/shard_map/remap/pallas_call | solution.py:465
  8.7 6.6 %all-to-all-start = ((f32[16,24,128]{2,1,0:T(8,128)}), f32[16,24,128]{2,1,0:T(8,128)S(1)}, u32[]{:S(2)}, u32[]{:S(2)}) async-start(f32[16,24,128]{2,1,0:T(8,128)} %remap.1), calls=%async_computation | async-start | bytes 393216 | tf_op jit(solution)/shard_map/all_to_all | solution.py:550
  15.3 3.1 %collective-permute-start = (f32[576,128]{1,0:T(8,128)S(1)}, f32[576,128]{1,0:T(8,128)S(1)}, u32[]{:S(2)}, u32[]{:S(2)}) collective-permute-start(f32[576,128]{1,0:T(8,128)S(1)} %get-tuple-element.9), channel_id=1, source_target_pairs={{1,2},{2,1},{5,6},{6,5},{9,10},{10,9},{13,14},{14,13},{3,15},{7,11... | collective-permute-start | bytes 884744 | tf_op jit(solution)/shard_map/ppermute | solution.py:544
  18.4 0.1 collective-permute-start.1
  18.4 10.5 %collective-permute-done.a_ref = f32[576,128]{1,0:T(8,128)S(1)} collective-permute-done((f32[576,128]{1,0:T(8,128)S(1)}, f32[576,128]{1,0:T(8,128)S(1)}, u32[]{:S(2)}, u32[]{:S(2)}) %collective-permute-start) | collective-permute-done | bytes 294944 | tf_op jit(solution)/shard_map/ppermute | solution.py:544
  28.9 0.0 collective-permute-done.1.b_ref
  29.0 0.2 columns.1
  29.1 0.1 collective-permute-start.2
  29.2 1.5 %collective-permute-start.3 = (f32[96,128]{1,0:T(8,128)S(1)}, f32[96,128]{1,0:T(8,128)S(1)}, u32[]{:S(2)}, u32[]{:S(2)}) collective-permute-start(f32[96,128]{1,0:T(8,128)S(1)} %get-tuple-element.13), channel_id=1, source_target_pairs={{0,4},{1,5},{2,6},{3,7},{4,8},{5,9},{6,10},{7,11},{8,12},{9,13},{1... | collective-permute-start | bytes 147464 | tf_op jit(solution)/shard_map/ppermute | solution.py:553
  30.7 0.0 copy-done.3
  30.7 0.0 copy-done.4
  30.7 4.2 %tile.1.y_ref = f32[16,160,128]{2,1,0:T(8,128)S(1)} custom-call(f32[16,160,128]{2,1,0:T(8,128)S(1)} %get-tuple-element.8.x_ref, s32[16,128]{1,0:T(8,128)S(1)} %copy-done.3, f32[16,128]{1,0:T(8,128)S(1)} %copy-done.4, f32[576,128]{1,0:T(8,128)S(1)} %collective-permute-done.a_ref, f32[576,128]{1,0:T(8,128)S(1)} %collective-permute-done.1.b_ref), custom_call_target="tpu_custom_call" | custom-call | bytes 14000000 | tf_op jit(solution)/shard_map/tile/pallas_call | solution.py:501
  34.8 0.0 collective-permute-done.2.fe_ref
  34.8 0.0 collective-permute-done.3.fw_ref
  34.9 3.8 %edges.1 = f32[2560,128]{1,0:T(8,128)} custom-call(f32[16,160,128]{2,1,0:T(8,128)S(1)} %tile.1.y_ref, f32[576,128]{1,0:T(8,128)S(1)} %collective-permute-done.a_ref, f32[576,128]{1,0:T(8,128)S(1)} %collective-permute-done.1.b_ref, f32[16,3,8,128]{3,2,1,0:T(8,128)S(1)} %get-tuple-element.11.p_ref, f32[96,128]{1,0:T(8,128)S(1)} %collective-permute-done.2.fe_ref, ...), custom_call_target="tpu_custom_call" | custom-call | bytes 14000000 | tf_op jit(solution)/shard_map/edges/pallas_call | solution.py:515
  38.6 0.0 all-to-all-done.parts_ref
  38.7 0.6 %sum.1 = f32[10,256]{1,0:T(8,128)} custom-call(f32[16,24,128]{2,1,0:T(8,128)S(1)} %all-to-all-done.parts_ref), custom_call_target="tpu_custom_call" | custom-call | bytes 3500000 | tf_op jit(solution)/shard_map/sum/pallas_call | solution.py:560
Async XLA Ops:
  0.6 2.1 %copy-start.2 = (f32[128,128]{1,0:T(8,128)S(1)}, f32[128,128]{1,0:T(8,128)}, u32[]{:S(2)}) copy-start(f32[128,128]{1,0:T(8,128)} %weight_ref.1) | copy-start | bytes 196612
  0.6 2.1 %copy-start.1 = (s32[128,128]{1,0:T(8,128)S(1)}, s32[128,128]{1,0:T(8,128)}, u32[]{:S(2)}) copy-start(s32[128,128]{1,0:T(8,128)} %column_ref.1) | copy-start | bytes 196612
  0.7 2.1 %copy-start = (s32[128,128]{1,0:T(8,128)S(1)}, s32[128,128]{1,0:T(8,128)}, u32[]{:S(2)}) copy-start(s32[128,128]{1,0:T(8,128)} %cell_ref.1) | copy-start | bytes 196612
  2.7 27.9 %copy-start.3 = (s32[16,128]{1,0:T(8,128)S(1)}, s32[16,128]{1,0:T(8,128)}, u32[]{:S(2)}) copy-start(s32[16,128]{1,0:T(8,128)} %mask_ref.3) | copy-start | bytes 24580
  2.7 27.9 %copy-start.4 = (f32[16,128]{1,0:T(8,128)S(1)}, f32[16,128]{1,0:T(8,128)}, u32[]{:S(2)}) copy-start(f32[16,128]{1,0:T(8,128)} %diff_ref.3) | copy-start | bytes 24580
  8.7 29.9 %all-to-all-start = ((f32[16,24,128]{2,1,0:T(8,128)}), f32[16,24,128]{2,1,0:T(8,128)S(1)}, u32[]{:S(2)}, u32[]{:S(2)}) async-start(f32[16,24,128]{2,1,0:T(8,128)} %remap.1), calls=%async_computation | async-start | bytes 393216 | tf_op jit(solution)/shard_map/all_to_all | solution.py:550
  15.3 13.7 %collective-permute-start = (f32[576,128]{1,0:T(8,128)S(1)}, f32[576,128]{1,0:T(8,128)S(1)}, u32[]{:S(2)}, u32[]{:S(2)}) collective-permute-start(f32[576,128]{1,0:T(8,128)S(1)} %get-tuple-element.9), channel_id=1, source_target_pairs={{1,2},{2,1},{5,6},{6,5},{9,10},{10,9},{13,14},{14,13},{3,15},{7,11... | collective-permute-start | bytes 884744 | tf_op jit(solution)/shard_map/ppermute | solution.py:544
  18.4 10.6 %collective-permute-start.1 = (f32[576,128]{1,0:T(8,128)S(1)}, f32[576,128]{1,0:T(8,128)S(1)}, u32[]{:S(2)}, u32[]{:S(2)}) collective-permute-start(f32[576,128]{1,0:T(8,128)S(1)} %get-tuple-element.10), channel_id=1, source_target_pairs={{0,1},{1,0},{2,3},{3,2},{4,5},{5,4},{6,7},{7,6},{8,9},{9,8},{10,11... | collective-permute-start | bytes 884744 | tf_op jit(solution)/shard_map/ppermute | solution.py:545
  29.1 5.7 %collective-permute-start.2 = (f32[96,128]{1,0:T(8,128)S(1)}, f32[96,128]{1,0:T(8,128)S(1)}, u32[]{:S(2)}, u32[]{:S(2)}) collective-permute-start(f32[96,128]{1,0:T(8,128)S(1)} %get-tuple-element.12), channel_id=1, source_target_pairs={{4,0},{5,1},{6,2},{7,3},{8,4},{9,5},{10,6},{11,7},{12,8},{13,9},{1... | collective-permute-start | bytes 147464 | tf_op jit(solution)/shard_map/ppermute | solution.py:554
  29.2 5.7 %collective-permute-start.3 = (f32[96,128]{1,0:T(8,128)S(1)}, f32[96,128]{1,0:T(8,128)S(1)}, u32[]{:S(2)}, u32[]{:S(2)}) collective-permute-start(f32[96,128]{1,0:T(8,128)S(1)} %get-tuple-element.13), channel_id=1, source_target_pairs={{0,4},{1,5},{2,6},{3,7},{4,8},{5,9},{6,10},{7,11},{8,12},{9,13},{1... | collective-permute-start | bytes 147464 | tf_op jit(solution)/shard_map/ppermute | solution.py:553

commit v3 on v2

--- a/solution.py
+++ b/solution.py
@@ -17,6 +17,7 @@
 PER = 7
 SETS = 3
 HALF = 6
+SLOTS = 5
 
 
 def lane_iota():
@@ -34,6 +35,10 @@
 
 def is_odd():
     return lax.axis_index("lat") % 2
+
+
+def register(row, which):
+    return pl.ds((row * SETS + which) * GROUP, GROUP)
 
 
 def base_of(chunk):
@@ -48,13 +53,14 @@
     height,
     chunks,
     parts,
+    levels,
     tracer_ref,
     mask_ref,
     diff_ref,
     a_ref,
     b_ref,
     p_ref,
-    x_ref,
+    surface_ref,
     tile,
     wet_tile,
     spread_tile,
@@ -105,10 +111,11 @@
             value = {}
             for row in range(height):
                 value[row] = tile[pl.ds(c * GROUP * height + row, GROUP, stride=height), :]
-                x_ref[row, pl.ds(c * GROUP, GROUP), :] = value[row]
             send(c, value)
             edge(c, value)
 
+    for k in range(chunks * GROUP // levels):
+        surface_ref[k] = tile[pl.ds(k * levels * height, height), :]
     copies[parts].wait()
     copies[parts + 1].wait()
     sub = lax.broadcasted_iota(jnp.int32, (GROUP, LANES), 0)
@@ -123,7 +130,7 @@
     zero = jnp.zeros((GROUP, LANES), F32)
     for row in range(height):
         for g in range(SETS):
-            p_ref[row, g] = strips.get((row, g), zero)
+            p_ref[register(row, g), :] = strips.get((row, g), zero)
     for d in range(SUBSTEPS):
         for g in range(SETS):
             near, far = strips.get((d, g), zero), strips.get((height - 1 - d, g), zero)
@@ -144,7 +151,7 @@
     found = {}
     for g in range(SETS):
         for row in range(height):
-            found[row, g] = p_ref[row, g]
+            found[row, g] = p_ref[register(row, g), :]
         for d in range(depth):
             rows = pl.ds(strips_at + (d * SETS + g) * GROUP, GROUP)
             found[height + d, g], found[-1 - d, g] = pick_rows(odd, a_ref, b_ref, rows)
@@ -155,13 +162,14 @@
     found = own_strips(height, chunks, a_ref, b_ref, p_ref, SUBSTEPS - 1)
     place = lane_iota() % STRIP
     rows = height + 2 * (SUBSTEPS - 1)
-    for block in range(-(-rows // 6)):
+    for block in range(-(-rows // SLOTS)):
         for g in range(SETS):
             east = west = jnp.zeros((GROUP, LANES), F32)
-            for i in range(min(6, rows - 6 * block)):
-                value = found[6 * block + i - (SUBSTEPS - 1), g]
+            for i in range(min(SLOTS, rows - SLOTS * block)):
+                value = found[SLOTS * block + i - (SUBSTEPS - 1), g]
                 here = (place >= 3 * i) & (place < 3 * i + 3)
-                east = jnp.where(here, shift(value, 3 * i - 3), east)
+                after = (place >= 3 * i + 3) & (place < 3 * i + 6)
+                east = jnp.where(after, shift(value, 3 * i), east)
                 west = jnp.where(here, shift(value, 3 * i - HALF), west)
             at = pl.ds((block * SETS + g) * GROUP, GROUP)
             east_ref[at, :] = east
@@ -196,7 +204,32 @@
     )
 
 
-def tile_kernel(height, chunks, x_ref, mask_ref, diff_ref, a_ref, b_ref, out_ref, coef):
+def tile_kernel(
+    height,
+    chunks,
+    parts,
+    tracer_ref,
+    mask_ref,
+    diff_ref,
+    a_ref,
+    b_ref,
+    p_ref,
+    out_ref,
+    strips_ref,
+    coef,
+    tile,
+    sems,
+):
+    each = chunks // parts
+    size = each * GROUP * height
+    copies = [
+        pltpu.make_async_copy(
+            tracer_ref.at[pl.ds(p * size, size)], tile.at[pl.ds(p * size, size)], sems.at[p]
+        )
+        for p in range(parts)
+    ]
+    for copy in copies:
+        copy.start()
     odd = jnp.full((GROUP, LANES), is_odd()) == 1
     stride = (chunks + 1) * GROUP
     low, high = -(SUBSTEPS - 1), height + SUBSTEPS - 1
@@ -221,7 +254,10 @@
 
     def one(c):
         rows = pl.ds(c * GROUP, GROUP)
-        value = {row: x_ref[row, rows, :] for row in range(height)}
+        value = {
+            row: tile[pl.ds(c * (GROUP * height) + row, GROUP, stride=height), :]
+            for row in range(height)
+        }
         for d in range(SUBSTEPS):
             value[height + d], value[-1 - d] = pick_rows(
                 odd, a_ref, b_ref, pl.ds(d * stride + c * GROUP, GROUP)
@@ -240,43 +276,70 @@
         one(2 * i + 1)
         return unused
 
-    lax.fori_loop(0, chunks // 2, pair, 0)
+    place = lane_iota() % STRIP
+    for (row, g), own in own_strips(height, chunks, a_ref, b_ref, p_ref, SUBSTEPS).items():
+        strips_ref[register(row + SUBSTEPS, g), :] = jnp.where(
+            place >= 2 * HALF, shift(own, HALF), own
+        )
+    for p in range(parts):
+        copies[p].wait()
+        lax.fori_loop(p * each // 2, (p + 1) * each // 2, pair, 0)
 
 
 def edge_kernel(
-    height, chunks, parts, y_ref, a_ref, b_ref, p_ref, fe_ref, fw_ref, out_ref, final, tile, sems
+    height,
+    chunks,
+    parts,
+    tracers,
+    y_ref,
+    strips_ref,
+    fe_ref,
+    fw_ref,
+    parts_ref,
+    out_ref,
+    atmosphere_ref,
+    strip,
+    coef,
+    final,
+    tile,
+    sums,
+    sems,
 ):
     lane = lane_iota()
     place = lane % STRIP
-    strips = own_strips(height, chunks, a_ref, b_ref, p_ref, SUBSTEPS)
-    low = -(SUBSTEPS - 1)
-    for (row, g), own in strips.items():
-        value = jnp.where(place >= 2 * HALF, shift(own, HALF), own)
-        at = row - low
-        if 0 <= at < height + 2 * (SUBSTEPS - 1):
-            block, i = at // 6, at % 6
-            rows = pl.ds((block * SETS + g) * GROUP, GROUP)
-            east = shift(fe_ref[rows, :], HALF - 3 * i)
-            west = shift(fw_ref[rows, :], HALF + 3 - 3 * i)
-            value = jnp.where(
-                (place >= HALF) & (place < 2 * HALF), jnp.where(place < 9, east, west), value
-            )
-        strips[row, g] = value
+    low, high = -(SUBSTEPS - 1), height + SUBSTEPS - 1
+
+    def with_halo(row, g):
+        own = strips_ref[register(row + SUBSTEPS, g), :]
+        if not low <= row < high:
+            return own
+        block, i = (row - low) // SLOTS, (row - low) % SLOTS
+        rows = pl.ds((block * SETS + g) * GROUP, GROUP)
+        both = shift(jnp.where(place < 3 * i + 3, fe_ref[rows, :], fw_ref[rows, :]), HALF - 3 * i)
+        return jnp.where((place >= HALF) & (place < 2 * HALF), both, own)
+
     which, base = base_of(chunks)
     wet, spread = {}, {}
     for row in range(-SUBSTEPS, height + SUBSTEPS):
-        value = strips[row, which]
+        value = with_halo(row, which)
+        strip[row + SUBSTEPS, which] = value
         for held, i in ((wet, 0), (spread, 1)):
             held[row] = take_lanes(
                 jnp.broadcast_to(value[i : i + 1, :], (GROUP, LANES)), base + place
             )
-    weights = factors(wet, spread, range(low, height - low))
+    weights = factors(wet, spread, range(low, high))
+    for row in range(low, high):
+        for i in range(5):
+            coef[row - low, i] = weights[row][i]
     for g in range(SETS):
-        value = {row: strips[row, g] for row in range(-SUBSTEPS, height + SUBSTEPS)}
+        value = {}
+        for row in range(-SUBSTEPS, height + SUBSTEPS):
+            value[row] = strip[row + SUBSTEPS, g] if g == which else with_halo(row, g)
         for s in range(SUBSTEPS):
             reach = SUBSTEPS - 1 - s
             value = {
-                row: substep(value, row, weights[row]) for row in range(-reach, height + reach)
+                row: substep(value, row, [coef[row - low, i] for i in range(5)])
+                for row in range(-reach, height + reach)
             }
         for row in range(height):
             final[row, g] = jnp.where(
@@ -299,17 +362,22 @@
         )
         copy.start()
         copies.append(copy)
+    total = jnp.sum(parts_ref[...], axis=0)
+    for half in range(ACOL // LANES):
+        sums[:, half * LANES : (half + 1) * LANES] = total[half * tracers : (half + 1) * tracers]
+    copy = pltpu.make_async_copy(sums, atmosphere_ref, sems.at[parts])
+    copy.start()
+    copies.append(copy)
     for copy in copies:
         copy.wait()
 
 
 def remap_kernel(
     tracers,
-    levels,
     height,
     owners,
     owner_ref,
-    x_ref,
+    surface_ref,
     cell_ref,
     column_ref,
     weight_ref,
@@ -336,7 +404,7 @@
         for row in range(height):
             here = at_row == row
             for k in range(tracers):
-                source = jnp.broadcast_to(x_ref[row, k * levels : k * levels + 1, :], (GROUP, LANES))
+                source = jnp.broadcast_to(surface_ref[k, row : row + 1, :], (GROUP, LANES))
                 found[k] = jnp.where(here, take_lanes(source, at_lane), found[k])
         weight = weight_ref[rows, :]
         for k in range(tracers):
@@ -382,12 +450,6 @@
     lax.fori_loop(0, owners, write, 0)
 
 
-def sum_kernel(tracers, parts_ref, out_ref):
-    total = jnp.sum(parts_ref[...], axis=0)
-    for half in range(ACOL // LANES):
-        out_ref[:, half * LANES : (half + 1) * LANES] = total[half * tracers : (half + 1) * tracers]
-
-
 def routes(lon, lat):
     def device(i, j):
         return i * lat + j
@@ -434,18 +496,18 @@
     return 5 if chunks % 5 == 0 else 1
 
 
-def pack(height, layers, flat, ocean_mask, diffusivity):
+def pack(height, layers, levels, flat, ocean_mask, diffusivity):
     chunks = layers // GROUP
     parts = parts_of(chunks)
     with jax.named_scope("pack"):
         return pl.pallas_call(
-            functools.partial(pack_kernel, height, chunks, parts),
+            functools.partial(pack_kernel, height, chunks, parts, levels),
             **settings(2),
             out_shape=(
                 pltpu.VMEM((message_rows(layers)[1], LANES), F32),
                 pltpu.VMEM((message_rows(layers)[1], LANES), F32),
-                pltpu.VMEM((height, SETS, GROUP, LANES), F32),
-                pltpu.VMEM((height, layers, LANES), F32),
+                pltpu.VMEM((height * SETS * GROUP, LANES), F32),
+                pltpu.VMEM((layers // levels, height, LANES), F32),
             ),
             in_specs=[anywhere()] * 3,
             out_specs=(vmem(),) * 4,
@@ -458,12 +520,12 @@
         )(in_hbm(flat), in_hbm(ocean_mask), in_hbm(diffusivity))
 
 
-def remap(owners, tracers, levels, x, remap_cell, remap_column, remap_weight, remap_owner):
+def remap(owners, surface, remap_cell, remap_column, remap_weight, remap_owner):
     blocks = remap_cell.shape[0]
-    height = x.shape[0]
+    tracers, height, unused = surface.shape
     with jax.named_scope("remap"):
         return pl.pallas_call(
-            functools.partial(remap_kernel, tracers, levels, height, owners),
+            functools.partial(remap_kernel, tracers, height, owners),
             **settings(6),
             out_shape=pltpu.VMEM((owners, 3 * GROUP, LANES), F32),
             in_specs=[anywhere()] + [vmem()] * 4,
@@ -477,7 +539,7 @@
             ],
         )(
             in_hbm(remap_owner.reshape(-1)),
-            in_vmem(x),
+            in_vmem(surface),
             in_vmem(remap_cell),
             in_vmem(remap_column),
             in_vmem(remap_weight),
@@ -485,7 +547,7 @@
 
 
 def columns(height, layers, got_a, got_b, p):
-    rows = -(-(height + 2 * (SUBSTEPS - 1)) // 6) * SETS * GROUP
+    rows = -(-(height + 2 * (SUBSTEPS - 1)) // SLOTS) * SETS * GROUP
     with jax.named_scope("columns"):
         return pl.pallas_call(
             functools.partial(columns_kernel, height, layers // GROUP),
@@ -496,41 +558,56 @@
         )(in_vmem(got_a), in_vmem(got_b), in_vmem(p))
 
 
-def tile_steps(height, layers, x, ocean_mask, diffusivity, got_a, got_b):
+def tile_steps(height, layers, flat, ocean_mask, diffusivity, got_a, got_b, p):
+    chunks = layers // GROUP
+    parts = parts_of(chunks)
     with jax.named_scope("tile"):
         return pl.pallas_call(
-            functools.partial(tile_kernel, height, layers // GROUP),
+            functools.partial(tile_kernel, height, chunks, parts),
             **settings(4),
-            out_shape=pltpu.VMEM(x.shape, F32),
-            in_specs=[vmem()] * 5,
-            out_specs=vmem(),
-            scratch_shapes=[pltpu.VMEM((height + 2 * (SUBSTEPS - 1), 5, GROUP, LANES), F32)],
-        )(in_vmem(x), in_vmem(ocean_mask), in_vmem(diffusivity), in_vmem(got_a), in_vmem(got_b))
-
-
-def edge_steps(height, layers, y, got_a, got_b, p, from_east, from_west):
+            out_shape=(
+                pltpu.VMEM((height, layers, LANES), F32),
+                pltpu.VMEM(((height + 2 * SUBSTEPS) * SETS * GROUP, LANES), F32),
+            ),
+            in_specs=[anywhere()] + [vmem()] * 5,
+            out_specs=(vmem(), vmem()),
+            scratch_shapes=[
+                pltpu.VMEM((height + 2 * (SUBSTEPS - 1), 5, GROUP, LANES), F32),
+                pltpu.VMEM(flat.shape, F32),
+                pltpu.SemaphoreType.DMA((parts,)),
+            ],
+        )(
+            in_hbm(flat),
+            in_vmem(ocean_mask),
+            in_vmem(diffusivity),
+            in_vmem(got_a),
+            in_vmem(got_b),
+            in_vmem(p),
+        )
+
+
+def edge_steps(height, layers, tracers, y, strips, from_east, from_west, sums):
     chunks = layers // GROUP
     parts = parts_of(chunks)
     with jax.named_scope("edges"):
         return pl.pallas_call(
-            functools.partial(edge_kernel, height, chunks, parts),
-            **settings(4),
-            out_shape=jax.ShapeDtypeStruct((layers * height, LANES), F32),
-            in_specs=[vmem()] * 6,
-            out_specs=anywhere(),
+            functools.partial(edge_kernel, height, chunks, parts, tracers),
+            **settings(3),
+            out_shape=(
+                jax.ShapeDtypeStruct((layers * height, LANES), F32),
+                jax.ShapeDtypeStruct((tracers, ACOL), F32),
+            ),
+            in_specs=[vmem()] * 5,
+            out_specs=(anywhere(), anywhere()),
             scratch_shapes=[
+                pltpu.VMEM((height + 2 * SUBSTEPS, SETS, GROUP, LANES), F32),
+                pltpu.VMEM((height + 2 * (SUBSTEPS - 1), 5, GROUP, LANES), F32),
                 pltpu.VMEM((height, SETS, GROUP, LANES), F32),
                 pltpu.VMEM((layers * height, LANES), F32),
-                pltpu.SemaphoreType.DMA((parts,)),
+                pltpu.VMEM((tracers, ACOL), F32),
+                pltpu.SemaphoreType.DMA((parts + 1,)),
             ],
-        )(
-            in_vmem(y),
-            in_vmem(got_a),
-            in_vmem(got_b),
-            in_vmem(p),
-            in_vmem(from_east),
-            in_vmem(from_west),
-        )
+        )(in_vmem(y), in_vmem(strips), in_vmem(from_east), in_vmem(from_west), in_vmem(sums))
 
 
 def on_device(lon, lat, tracer, ocean_mask, diffusivity, remap_cell, remap_column, remap_weight, remap_owner):
@@ -540,30 +617,22 @@
     route_a, route_b, route_east, route_west = routes(lon, lat)
     flat = tracer.reshape(layers * height, breadth)
 
-    send_a, send_b, p, x = pack(height, layers, flat, ocean_mask, diffusivity)
+    send_a, send_b, p, surface = pack(height, layers, levels, flat, ocean_mask, diffusivity)
     got_a = lax.ppermute(send_a, both, route_a)
     got_b = lax.ppermute(send_b, both, route_b)
 
-    partial = remap(
-        lon * lat, tracers, levels, x, remap_cell, remap_column, remap_weight, remap_owner
-    )
+    partial = remap(lon * lat, surface, remap_cell, remap_column, remap_weight, remap_owner)
+    partial, got_a, got_b = lax.optimization_barrier((partial, got_a, got_b))
     parts = lax.all_to_all(partial, both, 0, 0, tiled=True)
 
     send_east, send_west = columns(height, layers, got_a, got_b, p)
     from_west = lax.ppermute(send_east, both, route_east)
     from_east = lax.ppermute(send_west, both, route_west)
 
-    y = tile_steps(height, layers, x, ocean_mask, diffusivity, got_a, got_b)
-    updated = edge_steps(height, layers, y, got_a, got_b, p, from_east, from_west)
-
-    with jax.named_scope("sum"):
-        atmosphere = pl.pallas_call(
-            functools.partial(sum_kernel, tracers),
-            **settings(1),
-            out_shape=jax.ShapeDtypeStruct((tracers, ACOL), F32),
-            in_specs=[vmem()],
-            out_specs=vmem(),
-        )(in_vmem(parts))
+    y, strips = tile_steps(height, layers, flat, ocean_mask, diffusivity, got_a, got_b, p)
+    updated, atmosphere = edge_steps(
+        height, layers, tracers, y, strips, from_east, from_west, parts
+    )
     return updated.reshape(tracer.shape), atmosphere
 
 

time: 39.6 us -> 31.8 us (0.80)
  the two profiles are of different devices: /device:TPU:15 before, /device:TPU:0 now
where the time goes in v3:
time: 31.8 us; the launch traced here: 31.6 us
  Pallas kernels  15.4 us (48%)
  starting transfers between devices  14.2 us (45%)
  waiting for transfers between devices  1.2 us (4%)
  between operations  0.75 us (2%)
    pallas_call x1, Pallas kernels, remap(): pl.pallas_call(functools.partial(remap_kernel, tracers, height, owners),...  5.95 us
    all_to_all x1, starting transfers between devices, on_device(): parts = lax.all_to_all(partial, both, 0, 0, tiled=True)  5.39 us
    pallas_call x1, Pallas kernels, tile_steps(): pl.pallas_call(functools.partial(tile_kernel, height, chunks, parts), **s...  5.13 us
    ppermute x1, starting transfers between devices, on_device(): got_b = lax.ppermute(send_b, both, route_b)  4.35 us
    ppermute x1, starting transfers between devices, on_device(): from_east = lax.ppermute(send_west, both, route_west)  3.78 us
    pallas_call x1, Pallas kernels, edge_steps(): pl.pallas_call(functools.partial(edge_kernel, height, chunks, parts, trac...  2.12 us
    pallas_call x1, Pallas kernels, pack(): pl.pallas_call(functools.partial(pack_kernel, height, chunks, parts, leve...  2.02 us
    ppermute x1, waiting for transfers between devices, on_device(): from_west = lax.ppermute(send_east, both, route_east)  1.19 us
  transfers between devices with their start and end apart: 5, of which 1 were waited for; matrix products, arithmetic and copies ran while one was open for 0% of the time, Pallas kernels for 36%

profile of v3, /device:TPU:0, one launch (start us, length us, event | category | flops | bytes accessed | tf_op | source)
XLA Modules:
  0.0 31.6 jit_solution(11124611902326921502)
XLA Ops:
  0.6 0.0 copy-start.2
  0.6 0.0 copy-start.1
  0.7 0.0 copy-start
  0.7 0.0 copy-start.3
  0.7 0.0 copy-start.4
  0.7 2.0 %pack.1 = (f32[576,128]{1,0:T(8,128)S(1)}, f32[576,128]{1,0:T(8,128)S(1)}, f32[384,128]{1,0:T(8,128)S(1)}, f32[10,16,128]{2,1,0:T(8,128)S(1)}) custom-call(f32[2560,128]{1,0:T(8,128)} %bitcast.3, s32[16,128]{1,0:T(8,128)} %mask_ref.3, f32[16,128]{1,0:T(8,128)} %diff_ref.3), custom_call_target="tpu_custom_call" | custom-call | bytes 7000000 | tf_op jit(solution)/shard_map/pack/pallas_call | solution.py:503
  2.7 0.7 %collective-permute-start = (f32[576,128]{1,0:T(8,128)S(1)}, f32[576,128]{1,0:T(8,128)S(1)}, u32[]{:S(2)}, u32[]{:S(2)}) collective-permute-start(f32[576,128]{1,0:T(8,128)S(1)} %get-tuple-element.16), channel_id=1, source_target_pairs={{1,2},{2,1},{5,6},{6,5},{9,10},{10,9},{13,14},{14,13},{3,15},{7,11... | collective-permute-start | bytes 884744 | tf_op jit(solution)/shard_map/ppermute | solution.py:621
  3.4 4.3 %collective-permute-start.1 = (f32[576,128]{1,0:T(8,128)S(1)}, f32[576,128]{1,0:T(8,128)S(1)}, u32[]{:S(2)}, u32[]{:S(2)}) collective-permute-start(f32[576,128]{1,0:T(8,128)S(1)} %get-tuple-element.17), channel_id=1, source_target_pairs={{0,1},{1,0},{2,3},{3,2},{4,5},{5,4},{6,7},{7,6},{8,9},{9,8},{10,11... | collective-permute-start | bytes 884744 | tf_op jit(solution)/shard_map/ppermute | solution.py:622
  7.7 0.0 copy-done.2
  7.7 0.0 copy-done.1
  7.7 0.0 copy-done
  7.7 6.0 %remap.1 = f32[16,24,128]{2,1,0:T(8,128)} custom-call(s32[128]{0:T(128)} %bitcast.5, f32[10,16,128]{2,1,0:T(8,128)S(1)} %get-tuple-element.15.surface_ref, s32[128,128]{1,0:T(8,128)S(1)} %copy-done, s32[128,128]{1,0:T(8,128)S(1)} %copy-done.1, f32[128,128]{1,0:T(8,128)S(1)} %copy-done.2), custom_call_target="tpu_custom_call" | custom-call | bytes 21000000 | tf_op jit(solution)/shard_map/remap/pallas_call | solution.py:527
  13.7 0.0 collective-permute-done.a_ref
  13.7 0.0 collective-permute-done.1.b_ref
  13.7 5.4 %all-to-all-start = ((f32[16,24,128]{2,1,0:T(8,128)}), f32[16,24,128]{2,1,0:T(8,128)S(1)}, u32[]{:S(2)}, u32[]{:S(2)}) async-start(f32[16,24,128]{2,1,0:T(8,128)} %remap.1), calls=%async_computation | async-start | bytes 393216 | tf_op jit(solution)/shard_map/all_to_all | solution.py:626
  19.1 0.2 columns.1
  19.3 3.8 %collective-permute-start.2 = (f32[96,128]{1,0:T(8,128)S(1)}, f32[96,128]{1,0:T(8,128)S(1)}, u32[]{:S(2)}, u32[]{:S(2)}) collective-permute-start(f32[96,128]{1,0:T(8,128)S(1)} %get-tuple-element.23), channel_id=1, source_target_pairs={{4,0},{5,1},{6,2},{7,3},{8,4},{9,5},{10,6},{11,7},{12,8},{13,9},{1... | collective-permute-start | bytes 147464 | tf_op jit(solution)/shard_map/ppermute | solution.py:630
  23.1 0.0 collective-permute-start.3
  23.1 0.0 copy-done.3
  23.1 0.0 copy-done.4
  23.1 5.1 %tile.1 = (f32[16,160,128]{2,1,0:T(8,128)S(1)}, f32[528,128]{1,0:T(8,128)S(1)}) custom-call(f32[2560,128]{1,0:T(8,128)} %bitcast.4, s32[16,128]{1,0:T(8,128)S(1)} %copy-done.3, f32[16,128]{1,0:T(8,128)S(1)} %copy-done.4, f32[576,128]{1,0:T(8,128)S(1)} %collective-permute-done.a_ref, f32[576,128]{1,0:T(8,128)S(1)} %collective-permute-done.1.b_ref, ...), custom_call_target="tpu_custom_call" | custom-call | bytes 14000000 | tf_op jit(solution)/shard_map/tile/pallas_call | solution.py:565
  28.2 0.0 collective-permute-done.2.fe_ref
  28.2 1.2 %collective-permute-done.3.fw_ref = f32[96,128]{1,0:T(8,128)S(1)} collective-permute-done((f32[96,128]{1,0:T(8,128)S(1)}, f32[96,128]{1,0:T(8,128)S(1)}, u32[]{:S(2)}, u32[]{:S(2)}) %collective-permute-start.3) | collective-permute-done | bytes 49184 | tf_op jit(solution)/shard_map/ppermute | solution.py:629
  29.4 0.0 all-to-all-done.parts_ref
  29.4 2.1 %edges.1 = (f32[2560,128]{1,0:T(8,128)}, f32[10,256]{1,0:T(8,128)}) custom-call(f32[16,160,128]{2,1,0:T(8,128)S(1)} %get-tuple-element.21.y_ref, f32[528,128]{1,0:T(8,128)S(1)} %get-tuple-element.22.strips_ref, f32[96,128]{1,0:T(8,128)S(1)} %collective-permute-done.2.fe_ref, f32[96,128]{1,0:T(8,128)S(1)} %collective-permute-done.3.fw_ref, ...), custom_call_target="tpu_custom_call" | custom-call | bytes 10500000 | tf_op jit(solution)/shard_map/edges/pallas_call | solution.py:593
Async XLA Ops:
  0.6 7.1 %copy-start.2 = (f32[128,128]{1,0:T(8,128)S(1)}, f32[128,128]{1,0:T(8,128)}, u32[]{:S(2)}) copy-start(f32[128,128]{1,0:T(8,128)} %weight_ref.1) | copy-start | bytes 196612
  0.6 7.1 %copy-start.1 = (s32[128,128]{1,0:T(8,128)S(1)}, s32[128,128]{1,0:T(8,128)}, u32[]{:S(2)}) copy-start(s32[128,128]{1,0:T(8,128)} %column_ref.1) | copy-start | bytes 196612
  0.7 7.1 %copy-start = (s32[128,128]{1,0:T(8,128)S(1)}, s32[128,128]{1,0:T(8,128)}, u32[]{:S(2)}) copy-start(s32[128,128]{1,0:T(8,128)} %cell_ref.1) | copy-start | bytes 196612
  0.7 22.4 %copy-start.3 = (s32[16,128]{1,0:T(8,128)S(1)}, s32[16,128]{1,0:T(8,128)}, u32[]{:S(2)}) copy-start(s32[16,128]{1,0:T(8,128)} %mask_ref.3) | copy-start | bytes 24580
  0.7 22.4 %copy-start.4 = (f32[16,128]{1,0:T(8,128)S(1)}, f32[16,128]{1,0:T(8,128)}, u32[]{:S(2)}) copy-start(f32[16,128]{1,0:T(8,128)} %diff_ref.3) | copy-start | bytes 24580
  2.7 11.0 %collective-permute-start = (f32[576,128]{1,0:T(8,128)S(1)}, f32[576,128]{1,0:T(8,128)S(1)}, u32[]{:S(2)}, u32[]{:S(2)}) collective-permute-start(f32[576,128]{1,0:T(8,128)S(1)} %get-tuple-element.16), channel_id=1, source_target_pairs={{1,2},{2,1},{5,6},{6,5},{9,10},{10,9},{13,14},{14,13},{3,15},{7,11... | collective-permute-start | bytes 884744 | tf_op jit(solution)/shard_map/ppermute | solution.py:621
  3.4 10.3 %collective-permute-start.1 = (f32[576,128]{1,0:T(8,128)S(1)}, f32[576,128]{1,0:T(8,128)S(1)}, u32[]{:S(2)}, u32[]{:S(2)}) collective-permute-start(f32[576,128]{1,0:T(8,128)S(1)} %get-tuple-element.17), channel_id=1, source_target_pairs={{0,1},{1,0},{2,3},{3,2},{4,5},{5,4},{6,7},{7,6},{8,9},{9,8},{10,11... | collective-permute-start | bytes 884744 | tf_op jit(solution)/shard_map/ppermute | solution.py:622
  13.7 15.7 %all-to-all-start = ((f32[16,24,128]{2,1,0:T(8,128)}), f32[16,24,128]{2,1,0:T(8,128)S(1)}, u32[]{:S(2)}, u32[]{:S(2)}) async-start(f32[16,24,128]{2,1,0:T(8,128)} %remap.1), calls=%async_computation | async-start | bytes 393216 | tf_op jit(solution)/shard_map/all_to_all | solution.py:626
  19.3 8.9 %collective-permute-start.2 = (f32[96,128]{1,0:T(8,128)S(1)}, f32[96,128]{1,0:T(8,128)S(1)}, u32[]{:S(2)}, u32[]{:S(2)}) collective-permute-start(f32[96,128]{1,0:T(8,128)S(1)} %get-tuple-element.23), channel_id=1, source_target_pairs={{4,0},{5,1},{6,2},{7,3},{8,4},{9,5},{10,6},{11,7},{12,8},{13,9},{1... | collective-permute-start | bytes 147464 | tf_op jit(solution)/shard_map/ppermute | solution.py:630
  23.1 6.3 %collective-permute-start.3 = (f32[96,128]{1,0:T(8,128)S(1)}, f32[96,128]{1,0:T(8,128)S(1)}, u32[]{:S(2)}, u32[]{:S(2)}) collective-permute-start(f32[96,128]{1,0:T(8,128)S(1)} %get-tuple-element.24), channel_id=1, source_target_pairs={{0,4},{1,5},{2,6},{3,7},{4,8},{5,9},{6,10},{7,11},{8,12},{9,13},{1... | collective-permute-start | bytes 147464 | tf_op jit(solution)/shard_map/ppermute | solution.py:629

commit v4 on v3

--- a/solution.py
+++ b/solution.py
@@ -57,10 +57,12 @@
     tracer_ref,
     mask_ref,
     diff_ref,
+    owner_ref,
     a_ref,
     b_ref,
     p_ref,
     surface_ref,
+    owners_ref,
     tile,
     wet_tile,
     spread_tile,
@@ -78,6 +80,7 @@
     ]
     copies.append(pltpu.make_async_copy(mask_ref, wet_tile, sems.at[parts]))
     copies.append(pltpu.make_async_copy(diff_ref, spread_tile, sems.at[parts + 1]))
+    copies.append(pltpu.make_async_copy(owner_ref, owners_ref, sems.at[parts + 2]))
     for copy in copies:
         copy.start()
 
@@ -118,6 +121,7 @@
         surface_ref[k] = tile[pl.ds(k * levels * height, height), :]
     copies[parts].wait()
     copies[parts + 1].wait()
+    copies[parts + 2].wait()
     sub = lax.broadcasted_iota(jnp.int32, (GROUP, LANES), 0)
     value = {}
     for row in range(height):
@@ -137,6 +141,10 @@
             rows = pl.ds(strips_at + (d * SETS + g) * GROUP, GROUP)
             a_ref[rows, :] = take_lanes(jnp.where(odd, far, near), flip_strip)
             b_ref[rows, :] = jnp.where(odd, near, far)
+
+
+def beyond_south():
+    return jnp.full((GROUP, LANES), lax.axis_index("lat")) == 0
 
 
 def pick_rows(odd, a_ref, b_ref, rows):
@@ -238,6 +246,7 @@
         return jnp.broadcast_to(ref[row : row + 1, :].astype(F32), (GROUP, LANES))
 
     wet, spread = {}, {}
+    south = beyond_south()
     for row in range(height):
         wet[row] = wide(mask_ref, row)
         spread[row] = wide(diff_ref, row)
@@ -247,6 +256,7 @@
             first, second = wide(a_ref, row), wide(b_ref, row)
             held[height + d] = jnp.where(odd, first, second)
             held[-1 - d] = jnp.where(odd, second, first)
+        wet[-1 - d] = jnp.where(south, 0.0, wet[-1 - d])
     weights = factors(wet, spread, range(low, high))
     for row in range(low, high):
         for i in range(5):
@@ -327,6 +337,8 @@
             held[row] = take_lanes(
                 jnp.broadcast_to(value[i : i + 1, :], (GROUP, LANES)), base + place
             )
+        if row < 0:
+            wet[row] = jnp.where(beyond_south(), 0.0, wet[row])
     weights = factors(wet, spread, range(low, high))
     for row in range(low, high):
         for i in range(5):
@@ -385,11 +397,7 @@
     even_ref,
     odd_ref,
     total_ref,
-    owners_ref,
-    sem,
 ):
-    copy = pltpu.make_async_copy(owner_ref, owners_ref, sem)
-    copy.start()
     pad = 2 * GROUP
     groups = cell_ref.shape[0] // GROUP
     total_ref[...] = jnp.zeros_like(total_ref)
@@ -423,7 +431,7 @@
                 (((1,), (1,)), ((), ())),
                 preferred_element_type=F32,
             )
-            owner = owners_ref[block]
+            owner = owner_ref[block]
             total_ref[owner] = total_ref[owner] + (product[:pad] + product[pad:])
 
     def two(i, unused):
@@ -434,7 +442,6 @@
         return unused
 
     gather(0, even_ref)
-    copy.wait()
     lax.fori_loop(0, groups // 2 - 1, two, 0)
     gather(groups - 1, odd_ref)
     add(groups - 2, even_ref)
@@ -462,6 +469,8 @@
         return found
 
     fold = [(device(i, lat - 1), device(lon - 1 - i, lat - 1)) for i in range(lon)]
+    for i in range(0, lon - 1, 2):
+        fold += [(device(i, 0), device(i + 1, 0)), (device(i + 1, 0), device(i, 0))]
     east = [(device(i, j), device((i + 1) % lon, j)) for i in range(lon) for j in range(lat)]
     west = [(b, a) for a, b in east]
     return swaps(1, lat - 1) + fold, swaps(0, lat), east, west
@@ -477,6 +486,10 @@
 
 def vmem():
     return pl.BlockSpec(memory_space=pltpu.VMEM)
+
+
+def smem():
+    return pl.BlockSpec(memory_space=pltpu.SMEM)
 
 
 def anywhere():
@@ -496,7 +509,7 @@
     return 5 if chunks % 5 == 0 else 1
 
 
-def pack(height, layers, levels, flat, ocean_mask, diffusivity):
+def pack(height, layers, levels, flat, ocean_mask, diffusivity, remap_owner):
     chunks = layers // GROUP
     parts = parts_of(chunks)
     with jax.named_scope("pack"):
@@ -508,37 +521,40 @@
                 pltpu.VMEM((message_rows(layers)[1], LANES), F32),
                 pltpu.VMEM((height * SETS * GROUP, LANES), F32),
                 pltpu.VMEM((layers // levels, height, LANES), F32),
+                pltpu.SMEM((remap_owner.shape[0],), jnp.int32),
             ),
-            in_specs=[anywhere()] * 3,
-            out_specs=(vmem(),) * 4,
+            in_specs=[anywhere()] * 4,
+            out_specs=(vmem(),) * 4 + (smem(),),
             scratch_shapes=[
                 pltpu.VMEM(flat.shape, F32),
                 pltpu.VMEM(ocean_mask.shape, ocean_mask.dtype),
                 pltpu.VMEM(diffusivity.shape, F32),
-                pltpu.SemaphoreType.DMA((parts + 2,)),
+                pltpu.SemaphoreType.DMA((parts + 3,)),
             ],
-        )(in_hbm(flat), in_hbm(ocean_mask), in_hbm(diffusivity))
-
-
-def remap(owners, surface, remap_cell, remap_column, remap_weight, remap_owner):
-    blocks = remap_cell.shape[0]
+        )(
+            in_hbm(flat),
+            in_hbm(ocean_mask),
+            in_hbm(diffusivity),
+            in_hbm(remap_owner.reshape(-1)),
+        )
+
+
+def remap(owners, surface, remap_cell, remap_column, remap_weight, owner):
     tracers, height, unused = surface.shape
     with jax.named_scope("remap"):
         return pl.pallas_call(
             functools.partial(remap_kernel, tracers, height, owners),
             **settings(6),
             out_shape=pltpu.VMEM((owners, 3 * GROUP, LANES), F32),
-            in_specs=[anywhere()] + [vmem()] * 4,
+            in_specs=[smem()] + [vmem()] * 4,
             out_specs=vmem(),
             scratch_shapes=[
                 pltpu.VMEM((2 * GROUP * GROUP, LANES), F32),
                 pltpu.VMEM((2 * GROUP * GROUP, LANES), F32),
                 pltpu.VMEM((owners, 2 * GROUP, ACOL), F32),
-                pltpu.SMEM((blocks,), jnp.int32),
-                pltpu.SemaphoreType.DMA,
             ],
         )(
-            in_hbm(remap_owner.reshape(-1)),
+            pltpu.with_memory_space_constraint(owner, pltpu.SMEM),
             in_vmem(surface),
             in_vmem(remap_cell),
             in_vmem(remap_column),
@@ -617,11 +633,13 @@
     route_a, route_b, route_east, route_west = routes(lon, lat)
     flat = tracer.reshape(layers * height, breadth)
 
-    send_a, send_b, p, surface = pack(height, layers, levels, flat, ocean_mask, diffusivity)
+    send_a, send_b, p, surface, owner = pack(
+        height, layers, levels, flat, ocean_mask, diffusivity, remap_owner
+    )
     got_a = lax.ppermute(send_a, both, route_a)
     got_b = lax.ppermute(send_b, both, route_b)
 
-    partial = remap(lon * lat, surface, remap_cell, remap_column, remap_weight, remap_owner)
+    partial = remap(lon * lat, surface, remap_cell, remap_column, remap_weight, owner)
     partial, got_a, got_b = lax.optimization_barrier((partial, got_a, got_b))
     parts = lax.all_to_all(partial, both, 0, 0, tiled=True)
 

time: 31.8 us -> 30 us (0.943)
  starting transfers between devices: 14.2 us -> 12.9 us
  Pallas kernels: 15.4 us -> 14.9 us
    ppermute x1, starting transfers between devices: 4.35 us -> 0.03 us  [on_device(): got_b = lax.ppermute(send_b, both, route_b)]
    ppermute x1, starting transfers between devices: 0.68 us -> 3.09 us  [on_device(): got_a = lax.ppermute(send_a, both, route_a)]
    all_to_all x1, starting transfers between devices: 5.39 us -> 5.97 us  [on_device(): parts = lax.all_to_all(partial, both, 0, 0, tiled=True)]
    pallas_call x1, Pallas kernels: 5.95 us -> 5.48 us  [remap(): pl.pallas_call(functools.partial(remap_kernel, tracers, height, owners),...]
where the time goes in v4:
time: 30 us; the launch traced here: 29.7 us
  Pallas kernels  14.9 us (50%)
  starting transfers between devices  12.9 us (43%)
  waiting for transfers between devices  1.2 us (4%)
  between operations  0.72 us (2%)
    all_to_all x1, starting transfers between devices, on_device(): parts = lax.all_to_all(partial, both, 0, 0, tiled=True)  5.97 us
    pallas_call x1, Pallas kernels, remap(): pl.pallas_call(functools.partial(remap_kernel, tracers, height, owners),...  5.48 us
    pallas_call x1, Pallas kernels, tile_steps(): pl.pallas_call(functools.partial(tile_kernel, height, chunks, parts), **s...  5.13 us
    ppermute x1, starting transfers between devices, on_device(): from_east = lax.ppermute(send_west, both, route_west)  3.78 us
    ppermute x1, starting transfers between devices, on_device(): got_a = lax.ppermute(send_a, both, route_a)  3.09 us
    pallas_call x1, Pallas kernels, edge_steps(): pl.pallas_call(functools.partial(edge_kernel, height, chunks, parts, trac...  2.12 us
    pallas_call x1, Pallas kernels, pack(): pl.pallas_call(functools.partial(pack_kernel, height, chunks, parts, leve...  2.03 us
    ppermute x1, waiting for transfers between devices, on_device(): from_west = lax.ppermute(send_east, both, route_east)  1.19 us
  transfers between devices with their start and end apart: 5, of which 1 were waited for; matrix products, arithmetic and copies ran while one was open for 0% of the time, Pallas kernels for 36%

profile of v4, /device:TPU:0, one launch (start us, length us, event | category | flops | bytes accessed | tf_op | source)
XLA Modules:
  0.0 29.7 jit_solution(1102863852972072289)
XLA Ops:
  0.6 0.0 copy-start.2
  0.6 0.0 copy-start.1
  0.7 0.0 copy-start
  0.7 0.0 copy-start.3
  0.7 0.0 copy-start.4
  0.7 2.0 %pack.1 = (f32[576,128]{1,0:T(8,128)S(1)}, f32[576,128]{1,0:T(8,128)S(1)}, f32[384,128]{1,0:T(8,128)S(1)}, f32[10,16,128]{2,1,0:T(8,128)S(1)}, s32[128]{0:T(128)S(4)}) custom-call(f32[2560,128]{1,0:T(8,128)} %bitcast.3, s32[16,128]{1,0:T(8,128)} %mask_ref.3, f32[16,128]{1,0:T(8,128)} %diff_ref.3, s32[128]{0:T(128)} %bitcast.5), custom_call_target="tpu_custom_call" | custom-call | bytes 7000000 | tf_op jit(solution)/shard_map/pack/pallas_call | solution.py:516
  2.7 3.1 %collective-permute-start = (f32[576,128]{1,0:T(8,128)S(1)}, f32[576,128]{1,0:T(8,128)S(1)}, u32[]{:S(2)}, u32[]{:S(2)}) collective-permute-start(f32[576,128]{1,0:T(8,128)S(1)} %get-tuple-element.18), channel_id=1, source_target_pairs={{1,2},{2,1},{5,6},{6,5},{9,10},{10,9},{13,14},{14,13},{3,15},{7,11... | collective-permute-start | bytes 884744 | tf_op jit(solution)/shard_map/ppermute | solution.py:639
  5.8 0.0 collective-permute-start.1
  5.8 0.0 copy-done.2
  5.8 0.0 copy-done.1
  5.8 0.0 copy-done
  5.9 5.5 %remap.1 = f32[16,24,128]{2,1,0:T(8,128)} custom-call(s32[128]{0:T(128)S(4)} %get-tuple-element.16.owner_ref, f32[10,16,128]{2,1,0:T(8,128)S(1)} %get-tuple-element.17.surface_ref, s32[128,128]{1,0:T(8,128)S(1)} %copy-done, s32[128,128]{1,0:T(8,128)S(1)} %copy-done.1, f32[128,128]{1,0:T(8,128)S(1)} %copy-done.2), custom_call_target="tpu_custom_call" | custom-call | bytes 21000000 | tf_op jit(solution)/shard_map/remap/pallas_call | solution.py:545
  11.3 0.0 collective-permute-done.a_ref
  11.3 0.0 collective-permute-done.1.b_ref
  11.3 6.0 %all-to-all-start = ((f32[16,24,128]{2,1,0:T(8,128)}), f32[16,24,128]{2,1,0:T(8,128)S(1)}, u32[]{:S(2)}, u32[]{:S(2)}) async-start(f32[16,24,128]{2,1,0:T(8,128)} %remap.1), calls=%async_computation | async-start | bytes 393216 | tf_op jit(solution)/shard_map/all_to_all | solution.py:644
  17.3 0.2 columns.1
  17.5 3.8 %collective-permute-start.2 = (f32[96,128]{1,0:T(8,128)S(1)}, f32[96,128]{1,0:T(8,128)S(1)}, u32[]{:S(2)}, u32[]{:S(2)}) collective-permute-start(f32[96,128]{1,0:T(8,128)S(1)} %get-tuple-element.25), channel_id=1, source_target_pairs={{4,0},{5,1},{6,2},{7,3},{8,4},{9,5},{10,6},{11,7},{12,8},{13,9},{1... | collective-permute-start | bytes 147464 | tf_op jit(solution)/shard_map/ppermute | solution.py:648
  21.3 0.0 collective-permute-start.3
  21.3 0.0 copy-done.3
  21.3 0.0 copy-done.4
  21.3 5.1 %tile.1 = (f32[16,160,128]{2,1,0:T(8,128)S(1)}, f32[528,128]{1,0:T(8,128)S(1)}) custom-call(f32[2560,128]{1,0:T(8,128)} %bitcast.4, s32[16,128]{1,0:T(8,128)S(1)} %copy-done.3, f32[16,128]{1,0:T(8,128)S(1)} %copy-done.4, f32[576,128]{1,0:T(8,128)S(1)} %collective-permute-done.a_ref, f32[576,128]{1,0:T(8,128)S(1)} %collective-permute-done.1.b_ref, ...), custom_call_target="tpu_custom_call" | custom-call | bytes 14000000 | tf_op jit(solution)/shard_map/tile/pallas_call | solution.py:581
  26.4 0.0 collective-permute-done.2.fe_ref
  26.4 1.2 %collective-permute-done.3.fw_ref = f32[96,128]{1,0:T(8,128)S(1)} collective-permute-done((f32[96,128]{1,0:T(8,128)S(1)}, f32[96,128]{1,0:T(8,128)S(1)}, u32[]{:S(2)}, u32[]{:S(2)}) %collective-permute-start.3) | collective-permute-done | bytes 49184 | tf_op jit(solution)/shard_map/ppermute | solution.py:647
  27.6 0.0 all-to-all-done.parts_ref
  27.6 2.1 %edges.1 = (f32[2560,128]{1,0:T(8,128)}, f32[10,256]{1,0:T(8,128)}) custom-call(f32[16,160,128]{2,1,0:T(8,128)S(1)} %get-tuple-element.23.y_ref, f32[528,128]{1,0:T(8,128)S(1)} %get-tuple-element.24.strips_ref, f32[96,128]{1,0:T(8,128)S(1)} %collective-permute-done.2.fe_ref, f32[96,128]{1,0:T(8,128)S(1)} %collective-permute-done.3.fw_ref, ...), custom_call_target="tpu_custom_call" | custom-call | bytes 10500000 | tf_op jit(solution)/shard_map/edges/pallas_call | solution.py:609
Async XLA Ops:
  0.6 5.2 %copy-start.2 = (f32[128,128]{1,0:T(8,128)S(1)}, f32[128,128]{1,0:T(8,128)}, u32[]{:S(2)}) copy-start(f32[128,128]{1,0:T(8,128)} %weight_ref.1) | copy-start | bytes 196612
  0.6 5.2 %copy-start.1 = (s32[128,128]{1,0:T(8,128)S(1)}, s32[128,128]{1,0:T(8,128)}, u32[]{:S(2)}) copy-start(s32[128,128]{1,0:T(8,128)} %column_ref.1) | copy-start | bytes 196612
  0.7 5.2 %copy-start = (s32[128,128]{1,0:T(8,128)S(1)}, s32[128,128]{1,0:T(8,128)}, u32[]{:S(2)}) copy-start(s32[128,128]{1,0:T(8,128)} %cell_ref.1) | copy-start | bytes 196612
  0.7 20.6 %copy-start.3 = (s32[16,128]{1,0:T(8,128)S(1)}, s32[16,128]{1,0:T(8,128)}, u32[]{:S(2)}) copy-start(s32[16,128]{1,0:T(8,128)} %mask_ref.3) | copy-start | bytes 24580
  0.7 20.6 %copy-start.4 = (f32[16,128]{1,0:T(8,128)S(1)}, f32[16,128]{1,0:T(8,128)}, u32[]{:S(2)}) copy-start(f32[16,128]{1,0:T(8,128)} %diff_ref.3) | copy-start | bytes 24580
  2.7 8.6 %collective-permute-start = (f32[576,128]{1,0:T(8,128)S(1)}, f32[576,128]{1,0:T(8,128)S(1)}, u32[]{:S(2)}, u32[]{:S(2)}) collective-permute-start(f32[576,128]{1,0:T(8,128)S(1)} %get-tuple-element.18), channel_id=1, source_target_pairs={{1,2},{2,1},{5,6},{6,5},{9,10},{10,9},{13,14},{14,13},{3,15},{7,11... | collective-permute-start | bytes 884744 | tf_op jit(solution)/shard_map/ppermute | solution.py:639
  5.8 5.5 %collective-permute-start.1 = (f32[576,128]{1,0:T(8,128)S(1)}, f32[576,128]{1,0:T(8,128)S(1)}, u32[]{:S(2)}, u32[]{:S(2)}) collective-permute-start(f32[576,128]{1,0:T(8,128)S(1)} %get-tuple-element.19), channel_id=1, source_target_pairs={{0,1},{1,0},{2,3},{3,2},{4,5},{5,4},{6,7},{7,6},{8,9},{9,8},{10,11... | collective-permute-start | bytes 884744 | tf_op jit(solution)/shard_map/ppermute | solution.py:640
  11.3 16.3 %all-to-all-start = ((f32[16,24,128]{2,1,0:T(8,128)}), f32[16,24,128]{2,1,0:T(8,128)S(1)}, u32[]{:S(2)}, u32[]{:S(2)}) async-start(f32[16,24,128]{2,1,0:T(8,128)} %remap.1), calls=%async_computation | async-start | bytes 393216 | tf_op jit(solution)/shard_map/all_to_all | solution.py:644
  17.5 8.9 %collective-permute-start.2 = (f32[96,128]{1,0:T(8,128)S(1)}, f32[96,128]{1,0:T(8,128)S(1)}, u32[]{:S(2)}, u32[]{:S(2)}) collective-permute-start(f32[96,128]{1,0:T(8,128)S(1)} %get-tuple-element.25), channel_id=1, source_target_pairs={{4,0},{5,1},{6,2},{7,3},{8,4},{9,5},{10,6},{11,7},{12,8},{13,9},{1... | collective-permute-start | bytes 147464 | tf_op jit(solution)/shard_map/ppermute | solution.py:648
  21.3 6.3 %collective-permute-start.3 = (f32[96,128]{1,0:T(8,128)S(1)}, f32[96,128]{1,0:T(8,128)S(1)}, u32[]{:S(2)}, u32[]{:S(2)}) collective-permute-start(f32[96,128]{1,0:T(8,128)S(1)} %get-tuple-element.26), channel_id=1, source_target_pairs={{0,4},{1,5},{2,6},{3,7},{4,8},{5,9},{6,10},{7,11},{8,12},{9,13},{1... | collective-permute-start | bytes 147464 | tf_op jit(solution)/shard_map/ppermute | solution.py:647

commit v5 on v4

--- a/solution.py
+++ b/solution.py
@@ -13,6 +13,7 @@
 GROUP = 8
 F32 = jnp.float32
 
+CORNER = GROUP // 2
 STRIP = 18
 PER = 7
 SETS = 3
@@ -63,6 +64,8 @@
     p_ref,
     surface_ref,
     owners_ref,
+    c_ref,
+    d_ref,
     tile,
     wet_tile,
     spread_tile,
@@ -85,10 +88,8 @@
         copy.start()
 
     lane = lane_iota()
-    place = lane % STRIP
     is_top = jnp.full((GROUP, LANES), top) == 1
     flip = jnp.where(is_top, LANES - 1 - lane, lane)
-    flip_strip = jnp.where(is_top & (place < 2 * HALF), lane - place + 2 * HALF - 1 - place, lane)
     stride = (chunks + 1) * GROUP
     strips_at = SUBSTEPS * stride
 
@@ -102,11 +103,8 @@
     strips = {}
 
     def edge(c, value):
-        which, base = base_of(c)
-        here = (lane >= base) & (lane < base + 2 * HALF)
         for row in range(height):
-            before = strips.get((row, which), jnp.zeros((GROUP, LANES), F32))
-            strips[row, which] = jnp.where(here, shift(value[row], base + HALF), before)
+            add_strip(strips, row, c, value[row])
 
     for p in range(parts):
         copies[p].wait()
@@ -139,8 +137,53 @@
         for g in range(SETS):
             near, far = strips.get((d, g), zero), strips.get((height - 1 - d, g), zero)
             rows = pl.ds(strips_at + (d * SETS + g) * GROUP, GROUP)
-            a_ref[rows, :] = take_lanes(jnp.where(odd, far, near), flip_strip)
             b_ref[rows, :] = jnp.where(odd, near, far)
+    pack_columns(height, strips, c_ref, d_ref)
+
+
+def add_strip(strips, row, chunk, value):
+    which, base = base_of(chunk)
+    lane = lane_iota()
+    here = (lane >= base) & (lane < base + 2 * HALF)
+    before = strips.get((row, which), jnp.zeros((GROUP, LANES), F32))
+    strips[row, which] = jnp.where(here, shift(value, base + HALF), before)
+
+
+def pack_columns(height, strips, c_ref, d_ref):
+    place = lane_iota() % STRIP
+    for block in range(-(-height // SLOTS)):
+        for g in range(SETS):
+            east = west = jnp.zeros((GROUP, LANES), F32)
+            for i in range(min(SLOTS, height - SLOTS * block)):
+                value = strips[SLOTS * block + i, g]
+                here = (place >= 3 * i) & (place < 3 * i + 3)
+                after = (place >= 3 * i + 3) & (place < 3 * i + 6)
+                east = jnp.where(after, shift(value, 3 * i), east)
+                west = jnp.where(here, shift(value, 3 * i - HALF), west)
+            at = register(block, g)
+            swap = jnp.full((GROUP, LANES), lax.axis_index("lon") % 2) == 1
+            c_ref[at, :] = jnp.where(swap, west, east)
+            d_ref[at, :] = jnp.where(swap, east, west)
+
+
+def corner_register(p_ref, rows, first):
+    lane = lane_iota()
+    place = lane % STRIP
+    slot = place % HALF
+    column = jnp.where(slot == 1, 1, 0)
+    index = lane - place + (HALF + column if first else HALF - 1 - column)
+    index = jnp.where(slot < 3, index, lane)
+    found = jnp.zeros((GROUP, LANES), F32)
+    for g in range(SETS):
+        outer = take_lanes(p_ref[register(rows[0], g), :], index)
+        inner = take_lanes(p_ref[register(rows[1], g), :], index)
+        found = jnp.where(place // HALF == g, jnp.where(slot == 2, inner, outer), found)
+    return found
+
+
+def position():
+    lon, lat = lax.axis_size("lon"), lax.axis_size("lat")
+    return lon, lat, lax.axis_index("lon"), lax.axis_index("lat")
 
 
 def beyond_south():
@@ -153,35 +196,24 @@
     return jnp.where(odd, first, second), jnp.where(odd, second, first)
 
 
-def own_strips(height, chunks, a_ref, b_ref, p_ref, depth):
+def own_strips(height, chunks, a_ref, b_ref, p_ref):
     odd = jnp.full((GROUP, LANES), is_odd()) == 1
-    strips_at = SUBSTEPS * (chunks + 1) * GROUP
-    found = {}
+    stride = (chunks + 1) * GROUP
+    strips_at = SUBSTEPS * stride
+    first, found = {}, {}
+    for d in range(SUBSTEPS):
+        for c in range(chunks + 1):
+            add_strip(first, d, c, a_ref[pl.ds(d * stride + c * GROUP, GROUP), :])
+    zero = jnp.zeros((GROUP, LANES), F32)
     for g in range(SETS):
         for row in range(height):
             found[row, g] = p_ref[register(row, g), :]
-        for d in range(depth):
-            rows = pl.ds(strips_at + (d * SETS + g) * GROUP, GROUP)
-            found[height + d, g], found[-1 - d, g] = pick_rows(odd, a_ref, b_ref, rows)
+        for d in range(SUBSTEPS):
+            one = first.get((d, g), zero)
+            two = b_ref[pl.ds(strips_at + (d * SETS + g) * GROUP, GROUP), :]
+            found[height + d, g] = jnp.where(odd, one, two)
+            found[-1 - d, g] = jnp.where(odd, two, one)
     return found
-
-
-def columns_kernel(height, chunks, a_ref, b_ref, p_ref, east_ref, west_ref):
-    found = own_strips(height, chunks, a_ref, b_ref, p_ref, SUBSTEPS - 1)
-    place = lane_iota() % STRIP
-    rows = height + 2 * (SUBSTEPS - 1)
-    for block in range(-(-rows // SLOTS)):
-        for g in range(SETS):
-            east = west = jnp.zeros((GROUP, LANES), F32)
-            for i in range(min(SLOTS, rows - SLOTS * block)):
-                value = found[SLOTS * block + i - (SUBSTEPS - 1), g]
-                here = (place >= 3 * i) & (place < 3 * i + 3)
-                after = (place >= 3 * i + 3) & (place < 3 * i + 6)
-                east = jnp.where(after, shift(value, 3 * i), east)
-                west = jnp.where(here, shift(value, 3 * i - HALF), west)
-            at = pl.ds((block * SETS + g) * GROUP, GROUP)
-            east_ref[at, :] = east
-            west_ref[at, :] = west
 
 
 def coupling(m, s, m_n, s_n):
@@ -287,7 +319,7 @@
         return unused
 
     place = lane_iota() % STRIP
-    for (row, g), own in own_strips(height, chunks, a_ref, b_ref, p_ref, SUBSTEPS).items():
+    for (row, g), own in own_strips(height, chunks, a_ref, b_ref, p_ref).items():
         strips_ref[register(row + SUBSTEPS, g), :] = jnp.where(
             place >= 2 * HALF, shift(own, HALF), own
         )
@@ -303,8 +335,8 @@
     tracers,
     y_ref,
     strips_ref,
-    fe_ref,
-    fw_ref,
+    got_c_ref,
+    got_d_ref,
     parts_ref,
     out_ref,
     atmosphere_ref,
@@ -313,20 +345,62 @@
     final,
     tile,
     sums,
+    unfold,
     sems,
 ):
     lane = lane_iota()
     place = lane % STRIP
     low, high = -(SUBSTEPS - 1), height + SUBSTEPS - 1
+    lon, lat, i_lon, i_lat = position()
+    at_top = i_lat == lat - 1
+    upper, lower = jnp.minimum(i_lat + 1, lat - 1), jnp.maximum(i_lat - 1, 0)
+    north_east = jnp.where(at_top, (2 * lon - 2 - i_lon) % lon, (i_lon + 1) % lon) * lat + upper
+    north_west = jnp.where(at_top, (lon - i_lon) % lon, (i_lon + lon - 1) % lon) * lat + upper
+    south_east = (i_lon + 1) % lon * lat + lower
+    south_west = (i_lon + lon - 1) % lon * lat + lower
+    sub = lax.broadcasted_iota(jnp.int32, (GROUP, LANES), 0)
+    carried = tracers * ACOL // LANES
+
+    def corner(source, slot):
+        folded = parts_ref[source, pl.ds(carried, CORNER), :]
+        unfold[slot, 0:CORNER, :] = folded
+        unfold[slot, CORNER:GROUP, :] = folded
+        both = unfold[slot]
+        return jnp.where(sub < CORNER, both, shift(both, -3))
+
+    def corners(east, west, slot):
+        one, two = corner(east, slot), corner(west, slot + 1)
+        return jnp.where(place % HALF < 3, one, shift(two, 3))
+
+    beyond = {
+        "north": corners(north_east, north_west, 0),
+        "south": corners(south_east, south_west, 2),
+    }
+
+    def at_corner(side, d, g):
+        index = lane - place + HALF * g
+        if d == 0:
+            index = index + jnp.where(place < 9, place - HALF, 3 + 2 * HALF - 1 - place)
+        else:
+            index = index + jnp.where(place < 9, 2, 5)
+        return take_lanes(beyond[side], jnp.clip(index, 0, LANES - 1))
 
     def with_halo(row, g):
         own = strips_ref[register(row + SUBSTEPS, g), :]
         if not low <= row < high:
             return own
-        block, i = (row - low) // SLOTS, (row - low) % SLOTS
-        rows = pl.ds((block * SETS + g) * GROUP, GROUP)
-        both = shift(jnp.where(place < 3 * i + 3, fe_ref[rows, :], fw_ref[rows, :]), HALF - 3 * i)
-        return jnp.where((place >= HALF) & (place < 2 * HALF), both, own)
+        if row < 0:
+            halo = at_corner("south", -1 - row, g)
+        elif row >= height:
+            halo = at_corner("north", row - height, g)
+        else:
+            i, rows = row % SLOTS, register(row // SLOTS, g)
+            swap = jnp.full((GROUP, LANES), i_lon % 2) == 1
+            from_east = jnp.where(swap, got_d_ref[rows, :], got_c_ref[rows, :])
+            from_west = jnp.where(swap, got_c_ref[rows, :], got_d_ref[rows, :])
+            halo = jnp.where(place < 3 * i + 3, from_east, from_west)
+            halo = shift(halo, HALF - 3 * i)
+        return jnp.where((place >= HALF) & (place < 2 * HALF), halo, own)
 
     which, base = base_of(chunks)
     wet, spread = {}, {}
@@ -393,10 +467,13 @@
     cell_ref,
     column_ref,
     weight_ref,
+    p_ref,
     out_ref,
     even_ref,
     odd_ref,
     total_ref,
+    corner_ref,
+    fold,
 ):
     pad = 2 * GROUP
     groups = cell_ref.shape[0] // GROUP
@@ -447,7 +524,30 @@
     add(groups - 2, even_ref)
     add(groups - 1, odd_ref)
 
+    slot = lane_iota() % HALF
+    for which in range(4):
+        rows = (height - 1, height - 2) if which >= 2 else (0, 1)
+        found = corner_register(p_ref, rows, which % 2 == 0)
+        fold[which, 0:GROUP, :] = found
+        fold[which, GROUP : 2 * GROUP, :] = shift(found, 3)
+        corner_ref[which] = jnp.where(
+            slot[:CORNER] < 3, fold[which, 0:CORNER, :], fold[which, GROUP + CORNER : 2 * GROUP, :]
+        )
+    lon, lat, i_lon, i_lat = position()
+
+    def corner_for(o):
+        to_lon, to_lat = lax.div(o, lat), lax.rem(o, lat)
+        after = (i_lon + 1) % lon
+        row = jnp.where(to_lat == i_lat + 1, 2, 0)
+        which = row + jnp.where(to_lon == after, 1, 0)
+        fold_which = jnp.where(to_lon == (2 * lon - 2 - i_lon) % lon, 3, 2)
+        across = (i_lat == lat - 1) & (to_lat == lat - 1)
+        return jnp.where(across, fold_which, which)
+
+    carried = tracers * ACOL // LANES
+
     def write(o, unused):
+        out_ref[o, pl.ds(carried, CORNER), :] = corner_ref[corner_for(o)]
         for half in range(ACOL // LANES):
             out_ref[o, pl.ds(half * tracers, tracers), :] = total_ref[
                 o, pl.ds(0, tracers), pl.ds(half * LANES, LANES)
@@ -471,8 +571,12 @@
     fold = [(device(i, lat - 1), device(lon - 1 - i, lat - 1)) for i in range(lon)]
     for i in range(0, lon - 1, 2):
         fold += [(device(i, 0), device(i + 1, 0)), (device(i + 1, 0), device(i, 0))]
-    east = [(device(i, j), device((i + 1) % lon, j)) for i in range(lon) for j in range(lat)]
-    west = [(b, a) for a, b in east]
+    east, west = [], []
+    for i in range(0, lon, 2):
+        for j in range(lat):
+            one, two, three = device(i, j), device(i + 1, j), device((i + 2) % lon, j)
+            east += [(one, two), (two, one)]
+            west += [(two, three), (three, two)]
     return swaps(1, lat - 1) + fold, swaps(0, lat), east, west
 
 
@@ -512,19 +616,22 @@
 def pack(height, layers, levels, flat, ocean_mask, diffusivity, remap_owner):
     chunks = layers // GROUP
     parts = parts_of(chunks)
+    columns = -(-height // SLOTS) * SETS * GROUP
     with jax.named_scope("pack"):
         return pl.pallas_call(
             functools.partial(pack_kernel, height, chunks, parts, levels),
             **settings(2),
             out_shape=(
-                pltpu.VMEM((message_rows(layers)[1], LANES), F32),
+                pltpu.VMEM((message_rows(layers)[0], LANES), F32),
                 pltpu.VMEM((message_rows(layers)[1], LANES), F32),
                 pltpu.VMEM((height * SETS * GROUP, LANES), F32),
                 pltpu.VMEM((layers // levels, height, LANES), F32),
                 pltpu.SMEM((remap_owner.shape[0],), jnp.int32),
+                pltpu.VMEM((columns, LANES), F32),
+                pltpu.VMEM((columns, LANES), F32),
             ),
             in_specs=[anywhere()] * 4,
-            out_specs=(vmem(),) * 4 + (smem(),),
+            out_specs=(vmem(),) * 4 + (smem(), vmem(), vmem()),
             scratch_shapes=[
                 pltpu.VMEM(flat.shape, F32),
                 pltpu.VMEM(ocean_mask.shape, ocean_mask.dtype),
@@ -539,19 +646,21 @@
         )
 
 
-def remap(owners, surface, remap_cell, remap_column, remap_weight, owner):
+def remap(owners, surface, remap_cell, remap_column, remap_weight, owner, p):
     tracers, height, unused = surface.shape
     with jax.named_scope("remap"):
         return pl.pallas_call(
             functools.partial(remap_kernel, tracers, height, owners),
             **settings(6),
             out_shape=pltpu.VMEM((owners, 3 * GROUP, LANES), F32),
-            in_specs=[smem()] + [vmem()] * 4,
+            in_specs=[smem()] + [vmem()] * 5,
             out_specs=vmem(),
             scratch_shapes=[
                 pltpu.VMEM((2 * GROUP * GROUP, LANES), F32),
                 pltpu.VMEM((2 * GROUP * GROUP, LANES), F32),
                 pltpu.VMEM((owners, 2 * GROUP, ACOL), F32),
+                pltpu.VMEM((4, CORNER, LANES), F32),
+                pltpu.VMEM((4, 2 * GROUP, LANES), F32),
             ],
         )(
             pltpu.with_memory_space_constraint(owner, pltpu.SMEM),
@@ -559,19 +668,8 @@
             in_vmem(remap_cell),
             in_vmem(remap_column),
             in_vmem(remap_weight),
+            in_vmem(p),
         )
-
-
-def columns(height, layers, got_a, got_b, p):
-    rows = -(-(height + 2 * (SUBSTEPS - 1)) // SLOTS) * SETS * GROUP
-    with jax.named_scope("columns"):
-        return pl.pallas_call(
-            functools.partial(columns_kernel, height, layers // GROUP),
-            **settings(1),
-            out_shape=(pltpu.VMEM((rows, LANES), F32), pltpu.VMEM((rows, LANES), F32)),
-            in_specs=[vmem()] * 3,
-            out_specs=(vmem(), vmem()),
-        )(in_vmem(got_a), in_vmem(got_b), in_vmem(p))
 
 
 def tile_steps(height, layers, flat, ocean_mask, diffusivity, got_a, got_b, p):
@@ -602,7 +700,7 @@
         )
 
 
-def edge_steps(height, layers, tracers, y, strips, from_east, from_west, sums):
+def edge_steps(height, layers, tracers, y, strips, got_c, got_d, sums):
     chunks = layers // GROUP
     parts = parts_of(chunks)
     with jax.named_scope("edges"):
@@ -621,35 +719,34 @@
                 pltpu.VMEM((height, SETS, GROUP, LANES), F32),
                 pltpu.VMEM((layers * height, LANES), F32),
                 pltpu.VMEM((tracers, ACOL), F32),
+                pltpu.VMEM((4, GROUP, LANES), F32),
                 pltpu.SemaphoreType.DMA((parts + 1,)),
             ],
-        )(in_vmem(y), in_vmem(strips), in_vmem(from_east), in_vmem(from_west), in_vmem(sums))
+        )(in_vmem(y), in_vmem(strips), in_vmem(got_c), in_vmem(got_d), in_vmem(sums))
 
 
 def on_device(lon, lat, tracer, ocean_mask, diffusivity, remap_cell, remap_column, remap_weight, remap_owner):
     tracers, levels, height, breadth = tracer.shape
     layers = tracers * levels
     both = ("lon", "lat")
-    route_a, route_b, route_east, route_west = routes(lon, lat)
+    route_a, route_b, route_c, route_d = routes(lon, lat)
     flat = tracer.reshape(layers * height, breadth)
 
-    send_a, send_b, p, surface, owner = pack(
+    send_a, send_b, p, surface, owner, send_c, send_d = pack(
         height, layers, levels, flat, ocean_mask, diffusivity, remap_owner
     )
     got_a = lax.ppermute(send_a, both, route_a)
     got_b = lax.ppermute(send_b, both, route_b)
-
-    partial = remap(lon * lat, surface, remap_cell, remap_column, remap_weight, owner)
-    partial, got_a, got_b = lax.optimization_barrier((partial, got_a, got_b))
+    got_c = lax.ppermute(send_c, both, route_c)
+    got_d = lax.ppermute(send_d, both, route_d)
+
+    partial = remap(lon * lat, surface, remap_cell, remap_column, remap_weight, owner, p)
+    partial, got_a, got_b, got_c = lax.optimization_barrier((partial, got_a, got_b, got_c))
     parts = lax.all_to_all(partial, both, 0, 0, tiled=True)
-
-    send_east, send_west = columns(height, layers, got_a, got_b, p)
-    from_west = lax.ppermute(send_east, both, route_east)
-    from_east = lax.ppermute(send_west, both, route_west)
 
     y, strips = tile_steps(height, layers, flat, ocean_mask, diffusivity, got_a, got_b, p)
     updated, atmosphere = edge_steps(
-        height, layers, tracers, y, strips, from_east, from_west, parts
+        height, layers, tracers, y, strips, got_c, got_d, parts
     )
     return updated.reshape(tracer.shape), atmosphere
 

time: 30 us -> 29.3 us (0.977)
  waiting for transfers between devices: 1.2 us -> 0.74 us
    ppermute x2, waiting for transfers between devices: 1.19 us -> 0.42 us  [the longest x1 0.42 us: on_device(): got_d = lax.ppermute(send_d, both, route_d)]
    ppermute x1, starting transfers between devices: 0.03 us -> 0.52 us  [on_device(): got_b = lax.ppermute(send_b, both, route_b)]
    ppermute x1, starting transfers between devices: 3.09 us -> 2.65 us  [on_device(): got_a = lax.ppermute(send_a, both, route_a)]
    all_to_all x1, waiting for transfers between devices: 0.01 us -> 0.32 us  [on_device(): parts = lax.all_to_all(partial, both, 0, 0, tiled=True)]
  transfers between devices with their start and end apart: 5 -> 5, of which waited for: 1 -> 2; matrix products, arithmetic and copies ran while one was open for 0% -> 0% of each run, Pallas kernels for 36% -> 37%
where the time goes in v5:
time: 29.3 us; the launch traced here: 29.1 us
  Pallas kernels  14.9 us (51%)
  starting transfers between devices  12.7 us (43%)
  waiting for transfers between devices  0.74 us (3%)
  between operations  0.71 us (2%)
    all_to_all x1, starting transfers between devices, on_device(): parts = lax.all_to_all(partial, both, 0, 0, tiled=True)  5.77 us
    pallas_call x1, Pallas kernels, remap(): pl.pallas_call(functools.partial(remap_kernel, tracers, height, owners),...  5.64 us
    pallas_call x1, Pallas kernels, tile_steps(): pl.pallas_call(functools.partial(tile_kernel, height, chunks, parts), **s...  4.99 us
    ppermute x1, starting transfers between devices, on_device(): got_d = lax.ppermute(send_d, both, route_d)  3.73 us
    ppermute x1, starting transfers between devices, on_device(): got_a = lax.ppermute(send_a, both, route_a)  2.65 us
    pallas_call x1, Pallas kernels, edge_steps(): pl.pallas_call(functools.partial(edge_kernel, height, chunks, parts, trac...  2.19 us
    pallas_call x1, Pallas kernels, pack(): pl.pallas_call(functools.partial(pack_kernel, height, chunks, parts, leve...  2.06 us
  transfers between devices with their start and end apart: 5, of which 2 were waited for; matrix products, arithmetic and copies ran while one was open for 0% of the time, Pallas kernels for 37%

profile of v5, /device:TPU:0, one launch (start us, length us, event | category | flops | bytes accessed | tf_op | source)
XLA Modules:
  0.0 29.1 jit_solution(11288901672032384917)
XLA Ops:
  0.6 0.0 copy-start.4
  0.6 0.0 copy-start.3
  0.7 0.0 copy-start.2
  0.7 0.0 copy-start.1
  0.7 0.0 copy-start
  0.7 2.1 %pack.1 = (f32[504,128]{1,0:T(8,128)S(1)}, f32[576,128]{1,0:T(8,128)S(1)}, f32[384,128]{1,0:T(8,128)S(1)}, f32[10,16,128]{2,1,0:T(8,128)S(1)}, s32[128]{0:T(128)...) custom-call(f32[2560,128]{1,0:T(8,128)} %bitcast.3, s32[16,128]{1,0:T(8,128)} %mask_ref.3, f32[16,128]{1,0:T(8,128)} %diff_ref.3, ...), custom_call_target="tpu_custom_call" | custom-call | bytes 7000000 | tf_op jit(solution)/shard_map/pack/pallas_call | solution.py:621
  2.8 0.5 %collective-permute-start.1 = (f32[576,128]{1,0:T(8,128)S(1)}, f32[576,128]{1,0:T(8,128)S(1)}, u32[]{:S(2)}, u32[]{:S(2)}) collective-permute-start(f32[576,128]{1,0:T(8,128)S(1)} %get-tuple-element.21), channel_id=1, source_target_pairs={{0,1},{1,0},{2,3},{3,2},{4,5},{5,4},{6,7},{7,6},{8,9},{9,8},{10,11... | collective-permute-start | bytes 884744 | tf_op jit(solution)/shard_map/ppermute | solution.py:739
  3.3 2.6 %collective-permute-start = (f32[504,128]{1,0:T(8,128)S(1)}, f32[504,128]{1,0:T(8,128)S(1)}, u32[]{:S(2)}, u32[]{:S(2)}) collective-permute-start(f32[504,128]{1,0:T(8,128)S(1)} %get-tuple-element.20), channel_id=1, source_target_pairs={{1,2},{2,1},{5,6},{6,5},{9,10},{10,9},{13,14},{14,13},{3,15},{7,11... | collective-permute-start | bytes 774152 | tf_op jit(solution)/shard_map/ppermute | solution.py:738
  5.9 0.1 collective-permute-start.2
  6.0 0.0 copy-done.2
  6.0 0.0 copy-done.1
  6.0 0.0 copy-done
  6.0 5.6 %remap.1 = f32[16,24,128]{2,1,0:T(8,128)} custom-call(s32[128]{0:T(128)S(4)} %get-tuple-element.17.owner_ref, f32[10,16,128]{2,1,0:T(8,128)S(1)} %get-tuple-element.18.surface_ref, s32[128,128]{1,0:T(8,128)S(1)} %copy-done, s32[128,128]{1,0:T(8,128)S(1)} %copy-done.1, f32[128,128]{1,0:T(8,128)S(1)} %copy-done.2, f32[384,128]{1,0:T(8,128)S(1)} %get-tuple-element.19.p_ref), custom_call_target="tpu_custom_call" | custom-call | bytes 21000000 | tf_op jit(solution)/shard_map/remap/pallas_call | solution.py:652
  11.7 0.0 collective-permute-done.2.got_c_ref
  11.7 0.0 collective-permute-done.a_ref
  11.7 0.0 collective-permute-done.1.b_ref
  11.7 5.8 %all-to-all-start = ((f32[16,24,128]{2,1,0:T(8,128)}), f32[16,24,128]{2,1,0:T(8,128)S(1)}, u32[]{:S(2)}, u32[]{:S(2)}) async-start(f32[16,24,128]{2,1,0:T(8,128)} %remap.1), calls=%async_computation | async-start | bytes 393216 | tf_op jit(solution)/shard_map/all_to_all | solution.py:745
  17.4 3.7 %collective-permute-start.3 = (f32[96,128]{1,0:T(8,128)S(1)}, f32[96,128]{1,0:T(8,128)S(1)}, u32[]{:S(2)}, u32[]{:S(2)}) collective-permute-start(f32[96,128]{1,0:T(8,128)S(1)} %get-tuple-element.28), channel_id=1, source_target_pairs={{4,8},{8,4},{5,9},{9,5},{6,10},{10,6},{7,11},{11,7},{12,0},{0,12},... | collective-permute-start | bytes 147464 | tf_op jit(solution)/shard_map/ppermute | solution.py:741
  21.2 0.0 copy-done.4
  21.2 0.0 copy-done.3
  21.2 5.0 %tile.1 = (f32[16,160,128]{2,1,0:T(8,128)S(1)}, f32[528,128]{1,0:T(8,128)S(1)}) custom-call(f32[2560,128]{1,0:T(8,128)} %bitcast.4, s32[16,128]{1,0:T(8,128)S(1)} %copy-done.3, f32[16,128]{1,0:T(8,128)S(1)} %copy-done.4, f32[504,128]{1,0:T(8,128)S(1)} %collective-permute-done.a_ref, f32[576,128]{1,0:T(8,128)S(1)} %collective-permute-done.1.b_ref, ...), custom_call_target="tpu_custom_call" | custom-call | bytes 14000000 | tf_op jit(solution)/shard_map/tile/pallas_call | solution.py:679
  26.2 0.4 %collective-permute-done.3.got_d_ref = f32[96,128]{1,0:T(8,128)S(1)} collective-permute-done((f32[96,128]{1,0:T(8,128)S(1)}, f32[96,128]{1,0:T(8,128)S(1)}, u32[]{:S(2)}, u32[]{:S(2)}) %collective-permute-start.3) | collective-permute-done | bytes 49184 | tf_op jit(solution)/shard_map/ppermute | solution.py:741
  26.6 0.3 %all-to-all-done.parts_ref = f32[16,24,128]{2,1,0:T(8,128)S(1)} async-done(((f32[16,24,128]{2,1,0:T(8,128)}), f32[16,24,128]{2,1,0:T(8,128)S(1)}, u32[]{:S(2)}, u32[]{:S(2)}) %all-to-all-start) | async-done | bytes 196640 | tf_op jit(solution)/shard_map/all_to_all | solution.py:745
  26.9 2.2 %edges.1 = (f32[2560,128]{1,0:T(8,128)}, f32[10,256]{1,0:T(8,128)}) custom-call(f32[16,160,128]{2,1,0:T(8,128)S(1)} %get-tuple-element.25.y_ref, f32[528,128]{1,0:T(8,128)S(1)} %get-tuple-element.26.strips_ref, f32[96,128]{1,0:T(8,128)S(1)} %collective-permute-done.2.got_c_ref, f32[96,128]{1,0:T(8,128)S(1)} %collective-permute-done.3.got_d_ref, ...), custom_call_target="tpu_custom_call" | custom-call | bytes 10500000 | tf_op jit(solution)/shard_map/edges/pallas_call | solution.py:707
Async XLA Ops:
  0.6 20.5 %copy-start.4 = (f32[16,128]{1,0:T(8,128)S(1)}, f32[16,128]{1,0:T(8,128)}, u32[]{:S(2)}) copy-start(f32[16,128]{1,0:T(8,128)} %diff_ref.3) | copy-start | bytes 24580
  0.6 20.5 %copy-start.3 = (s32[16,128]{1,0:T(8,128)S(1)}, s32[16,128]{1,0:T(8,128)}, u32[]{:S(2)}) copy-start(s32[16,128]{1,0:T(8,128)} %mask_ref.3) | copy-start | bytes 24580
  0.7 5.3 %copy-start.2 = (f32[128,128]{1,0:T(8,128)S(1)}, f32[128,128]{1,0:T(8,128)}, u32[]{:S(2)}) copy-start(f32[128,128]{1,0:T(8,128)} %weight_ref.1) | copy-start | bytes 196612
  0.7 5.3 %copy-start.1 = (s32[128,128]{1,0:T(8,128)S(1)}, s32[128,128]{1,0:T(8,128)}, u32[]{:S(2)}) copy-start(s32[128,128]{1,0:T(8,128)} %column_ref.1) | copy-start | bytes 196612
  0.7 5.3 %copy-start = (s32[128,128]{1,0:T(8,128)S(1)}, s32[128,128]{1,0:T(8,128)}, u32[]{:S(2)}) copy-start(s32[128,128]{1,0:T(8,128)} %cell_ref.1) | copy-start | bytes 196612
  2.8 8.9 %collective-permute-start.1 = (f32[576,128]{1,0:T(8,128)S(1)}, f32[576,128]{1,0:T(8,128)S(1)}, u32[]{:S(2)}, u32[]{:S(2)}) collective-permute-start(f32[576,128]{1,0:T(8,128)S(1)} %get-tuple-element.21), channel_id=1, source_target_pairs={{0,1},{1,0},{2,3},{3,2},{4,5},{5,4},{6,7},{7,6},{8,9},{9,8},{10,11... | collective-permute-start | bytes 884744 | tf_op jit(solution)/shard_map/ppermute | solution.py:739
  3.3 8.4 %collective-permute-start = (f32[504,128]{1,0:T(8,128)S(1)}, f32[504,128]{1,0:T(8,128)S(1)}, u32[]{:S(2)}, u32[]{:S(2)}) collective-permute-start(f32[504,128]{1,0:T(8,128)S(1)} %get-tuple-element.20), channel_id=1, source_target_pairs={{1,2},{2,1},{5,6},{6,5},{9,10},{10,9},{13,14},{14,13},{3,15},{7,11... | collective-permute-start | bytes 774152 | tf_op jit(solution)/shard_map/ppermute | solution.py:738
  5.9 5.7 %collective-permute-start.2 = (f32[96,128]{1,0:T(8,128)S(1)}, f32[96,128]{1,0:T(8,128)S(1)}, u32[]{:S(2)}, u32[]{:S(2)}) collective-permute-start(f32[96,128]{1,0:T(8,128)S(1)} %get-tuple-element.22), channel_id=1, source_target_pairs={{0,4},{4,0},{1,5},{5,1},{2,6},{6,2},{3,7},{7,3},{8,12},{12,8},{9,1... | collective-permute-start | bytes 147464 | tf_op jit(solution)/shard_map/ppermute | solution.py:740
  11.7 15.2 %all-to-all-start = ((f32[16,24,128]{2,1,0:T(8,128)}), f32[16,24,128]{2,1,0:T(8,128)S(1)}, u32[]{:S(2)}, u32[]{:S(2)}) async-start(f32[16,24,128]{2,1,0:T(8,128)} %remap.1), calls=%async_computation | async-start | bytes 393216 | tf_op jit(solution)/shard_map/all_to_all | solution.py:745
  17.4 9.1 %collective-permute-start.3 = (f32[96,128]{1,0:T(8,128)S(1)}, f32[96,128]{1,0:T(8,128)S(1)}, u32[]{:S(2)}, u32[]{:S(2)}) collective-permute-start(f32[96,128]{1,0:T(8,128)S(1)} %get-tuple-element.28), channel_id=1, source_target_pairs={{4,8},{8,4},{5,9},{9,5},{6,10},{10,6},{7,11},{11,7},{12,0},{0,12},... | collective-permute-start | bytes 147464 | tf_op jit(solution)/shard_map/ppermute | solution.py:741

commit v6 on v5

--- a/solution.py
+++ b/solution.py
@@ -53,7 +53,7 @@
 def pack_kernel(
     height,
     chunks,
-    parts,
+    cuts,
     levels,
     tracer_ref,
     mask_ref,
@@ -73,14 +73,11 @@
 ):
     odd = jnp.full((GROUP, LANES), is_odd()) == 1
     top = (lax.axis_index("lat") == lax.axis_size("lat") - 1).astype(jnp.int32)
-    each = chunks // parts
-    size = each * GROUP * height
-    copies = [
-        pltpu.make_async_copy(
-            tracer_ref.at[pl.ds(p * size, size)], tile.at[pl.ds(p * size, size)], sems.at[p]
-        )
-        for p in range(parts)
-    ]
+    parts = len(cuts) - 1
+    copies = []
+    for p in range(parts):
+        rows = pl.ds(cuts[p] * GROUP * height, (cuts[p + 1] - cuts[p]) * GROUP * height)
+        copies.append(pltpu.make_async_copy(tracer_ref.at[rows], tile.at[rows], sems.at[p]))
     copies.append(pltpu.make_async_copy(mask_ref, wet_tile, sems.at[parts]))
     copies.append(pltpu.make_async_copy(diff_ref, spread_tile, sems.at[parts + 1]))
     copies.append(pltpu.make_async_copy(owner_ref, owners_ref, sems.at[parts + 2]))
@@ -108,7 +105,7 @@
 
     for p in range(parts):
         copies[p].wait()
-        for c in range(p * each, (p + 1) * each):
+        for c in range(cuts[p], cuts[p + 1]):
             value = {}
             for row in range(height):
                 value[row] = tile[pl.ds(c * GROUP * height + row, GROUP, stride=height), :]
@@ -133,11 +130,6 @@
     for row in range(height):
         for g in range(SETS):
             p_ref[register(row, g), :] = strips.get((row, g), zero)
-    for d in range(SUBSTEPS):
-        for g in range(SETS):
-            near, far = strips.get((d, g), zero), strips.get((height - 1 - d, g), zero)
-            rows = pl.ds(strips_at + (d * SETS + g) * GROUP, GROUP)
-            b_ref[rows, :] = jnp.where(odd, near, far)
     pack_columns(height, strips, c_ref, d_ref)
 
 
@@ -172,7 +164,7 @@
     slot = place % HALF
     column = jnp.where(slot == 1, 1, 0)
     index = lane - place + (HALF + column if first else HALF - 1 - column)
-    index = jnp.where(slot < 3, index, lane)
+    index = jnp.clip(jnp.where(slot < 3, index, lane), 0, LANES - 1)
     found = jnp.zeros((GROUP, LANES), F32)
     for g in range(SETS):
         outer = take_lanes(p_ref[register(rows[0], g), :], index)
@@ -200,17 +192,17 @@
     odd = jnp.full((GROUP, LANES), is_odd()) == 1
     stride = (chunks + 1) * GROUP
     strips_at = SUBSTEPS * stride
-    first, found = {}, {}
+    first, second, found = {}, {}, {}
     for d in range(SUBSTEPS):
         for c in range(chunks + 1):
             add_strip(first, d, c, a_ref[pl.ds(d * stride + c * GROUP, GROUP), :])
+            add_strip(second, d, c, b_ref[pl.ds(d * stride + c * GROUP, GROUP), :])
     zero = jnp.zeros((GROUP, LANES), F32)
     for g in range(SETS):
         for row in range(height):
             found[row, g] = p_ref[register(row, g), :]
         for d in range(SUBSTEPS):
-            one = first.get((d, g), zero)
-            two = b_ref[pl.ds(strips_at + (d * SETS + g) * GROUP, GROUP), :]
+            one, two = first.get((d, g), zero), second.get((d, g), zero)
             found[height + d, g] = jnp.where(odd, one, two)
             found[-1 - d, g] = jnp.where(odd, two, one)
     return found
@@ -359,7 +351,7 @@
     south_east = (i_lon + 1) % lon * lat + lower
     south_west = (i_lon + lon - 1) % lon * lat + lower
     sub = lax.broadcasted_iota(jnp.int32, (GROUP, LANES), 0)
-    carried = tracers * ACOL // LANES
+    carried = 2 * GROUP + CORNER
 
     def corner(source, slot):
         folded = parts_ref[source, pl.ds(carried, CORNER), :]
@@ -449,8 +441,12 @@
         copy.start()
         copies.append(copy)
     total = jnp.sum(parts_ref[...], axis=0)
+    rest = tracers - GROUP
     for half in range(ACOL // LANES):
-        sums[:, half * LANES : (half + 1) * LANES] = total[half * tracers : (half + 1) * tracers]
+        lanes = slice(half * LANES, (half + 1) * LANES)
+        sums[0:GROUP, lanes] = total[half * GROUP : (half + 1) * GROUP]
+        at = 2 * GROUP + half * rest
+        sums[GROUP:tracers, lanes] = total[at : at + rest]
     copy = pltpu.make_async_copy(sums, atmosphere_ref, sems.at[parts])
     copy.start()
     copies.append(copy)
@@ -473,12 +469,12 @@
     odd_ref,
     total_ref,
     corner_ref,
-    fold,
 ):
     pad = 2 * GROUP
     groups = cell_ref.shape[0] // GROUP
     total_ref[...] = jnp.zeros_like(total_ref)
-    column = lax.broadcasted_iota(jnp.int32, (ACOL, LANES), 0)
+    column = lax.broadcasted_iota(jnp.int32, (ACOL, LANES), 0).astype(jnp.bfloat16)
+    one, none = jnp.ones((), jnp.bfloat16), jnp.zeros((), jnp.bfloat16)
 
     def gather(g, picked_ref):
         rows = pl.ds(g * GROUP, GROUP)
@@ -501,7 +497,8 @@
             value = picked_ref[pl.ds(j * pad, pad), :]
             coarse = value.astype(jnp.bfloat16)
             fine = (value - coarse.astype(F32)).astype(jnp.bfloat16)
-            chosen = (column == column_ref[pl.ds(block, 1), :]).astype(F32).astype(jnp.bfloat16)
+            named = column_ref[pl.ds(block, 1), :].astype(F32).astype(jnp.bfloat16)
+            chosen = jnp.where(column == named, one, none)
             product = lax.dot_general(
                 jnp.concatenate([coarse, fine], axis=0),
                 chosen,
@@ -528,11 +525,7 @@
     for which in range(4):
         rows = (height - 1, height - 2) if which >= 2 else (0, 1)
         found = corner_register(p_ref, rows, which % 2 == 0)
-        fold[which, 0:GROUP, :] = found
-        fold[which, GROUP : 2 * GROUP, :] = shift(found, 3)
-        corner_ref[which] = jnp.where(
-            slot[:CORNER] < 3, fold[which, 0:CORNER, :], fold[which, GROUP + CORNER : 2 * GROUP, :]
-        )
+        corner_ref[which] = jnp.where(slot < 3, pltpu.roll(found, CORNER, 0), shift(found, 3))
     lon, lat, i_lon, i_lat = position()
 
     def corner_for(o):
@@ -544,14 +537,16 @@
         across = (i_lat == lat - 1) & (to_lat == lat - 1)
         return jnp.where(across, fold_which, which)
 
-    carried = tracers * ACOL // LANES
+    rest = tracers - GROUP
+    sub = lax.broadcasted_iota(jnp.int32, (GROUP, LANES), 0)
 
     def write(o, unused):
-        out_ref[o, pl.ds(carried, CORNER), :] = corner_ref[corner_for(o)]
-        for half in range(ACOL // LANES):
-            out_ref[o, pl.ds(half * tracers, tracers), :] = total_ref[
-                o, pl.ds(0, tracers), pl.ds(half * LANES, LANES)
-            ]
+        out_ref[o, 0:GROUP, :] = total_ref[o, 0:GROUP, 0:LANES]
+        out_ref[o, GROUP : 2 * GROUP, :] = total_ref[o, 0:GROUP, LANES:ACOL]
+        left = total_ref[o, GROUP : 2 * GROUP, 0:LANES]
+        right = pltpu.roll(total_ref[o, GROUP : 2 * GROUP, LANES:ACOL], rest, 0)
+        last = jnp.where(sub < rest, left, jnp.where(sub < CORNER, right, corner_ref[corner_for(o)]))
+        out_ref[o, 2 * GROUP : 3 * GROUP, :] = last
         return unused
 
     lax.fori_loop(0, owners, write, 0)
@@ -609,21 +604,21 @@
     )
 
 
-def parts_of(chunks):
-    return 5 if chunks % 5 == 0 else 1
+def parts_of(chunks, wanted):
+    return wanted if chunks % wanted == 0 else 1
 
 
 def pack(height, layers, levels, flat, ocean_mask, diffusivity, remap_owner):
     chunks = layers // GROUP
-    parts = parts_of(chunks)
+    cuts = (0, chunks // 2, chunks)
     columns = -(-height // SLOTS) * SETS * GROUP
     with jax.named_scope("pack"):
         return pl.pallas_call(
-            functools.partial(pack_kernel, height, chunks, parts, levels),
+            functools.partial(pack_kernel, height, chunks, cuts, levels),
             **settings(2),
             out_shape=(
                 pltpu.VMEM((message_rows(layers)[0], LANES), F32),
-                pltpu.VMEM((message_rows(layers)[1], LANES), F32),
+                pltpu.VMEM((message_rows(layers)[0], LANES), F32),
                 pltpu.VMEM((height * SETS * GROUP, LANES), F32),
                 pltpu.VMEM((layers // levels, height, LANES), F32),
                 pltpu.SMEM((remap_owner.shape[0],), jnp.int32),
@@ -636,7 +631,7 @@
                 pltpu.VMEM(flat.shape, F32),
                 pltpu.VMEM(ocean_mask.shape, ocean_mask.dtype),
                 pltpu.VMEM(diffusivity.shape, F32),
-                pltpu.SemaphoreType.DMA((parts + 3,)),
+                pltpu.SemaphoreType.DMA((len(cuts) + 2,)),
             ],
         )(
             in_hbm(flat),
@@ -659,8 +654,7 @@
                 pltpu.VMEM((2 * GROUP * GROUP, LANES), F32),
                 pltpu.VMEM((2 * GROUP * GROUP, LANES), F32),
                 pltpu.VMEM((owners, 2 * GROUP, ACOL), F32),
-                pltpu.VMEM((4, CORNER, LANES), F32),
-                pltpu.VMEM((4, 2 * GROUP, LANES), F32),
+                pltpu.VMEM((4, GROUP, LANES), F32),
             ],
         )(
             pltpu.with_memory_space_constraint(owner, pltpu.SMEM),
@@ -674,7 +668,7 @@
 
 def tile_steps(height, layers, flat, ocean_mask, diffusivity, got_a, got_b, p):
     chunks = layers // GROUP
-    parts = parts_of(chunks)
+    parts = parts_of(chunks, 10)
     with jax.named_scope("tile"):
         return pl.pallas_call(
             functools.partial(tile_kernel, height, chunks, parts),
@@ -702,7 +696,7 @@
 
 def edge_steps(height, layers, tracers, y, strips, got_c, got_d, sums):
     chunks = layers // GROUP
-    parts = parts_of(chunks)
+    parts = parts_of(chunks, 5)
     with jax.named_scope("edges"):
         return pl.pallas_call(
             functools.partial(edge_kernel, height, chunks, parts, tracers),

time: 29.3 us -> 29.1 us (level)
  Pallas kernels: 14.9 us -> 14.6 us
    ppermute x1, starting transfers between devices: 0.08 us -> 1.58 us  [on_device(): got_c = lax.ppermute(send_c, both, route_c)]
    all_to_all x1, starting transfers between devices: 5.77 us -> 4.3 us  [on_device(): parts = lax.all_to_all(partial, both, 0, 0, tiled=True)]
    ppermute x1, starting transfers between devices: 0.52 us -> 0.03 us  [on_device(): got_b = lax.ppermute(send_b, both, route_b)]
    ppermute x1, starting transfers between devices: 2.65 us -> 3.09 us  [on_device(): got_a = lax.ppermute(send_a, both, route_a)]
  transfers between devices with their start and end apart: 5 -> 5, of which waited for: 2 -> 2; matrix products, arithmetic and copies ran while one was open for 0% -> 0% of each run, Pallas kernels for 37% -> 36%
where the time goes in v6:
time: 29.1 us; the launch traced here: 28.8 us
  Pallas kernels  14.6 us (50%)
  starting transfers between devices  12.7 us (44%)
  waiting for transfers between devices  0.73 us (3%)
  between operations  0.71 us (2%)
    pallas_call x1, Pallas kernels, remap(): pl.pallas_call(functools.partial(remap_kernel, tracers, height, owners),...  5.49 us
    pallas_call x1, Pallas kernels, tile_steps(): pl.pallas_call(functools.partial(tile_kernel, height, chunks, parts), **s...  5 us
    all_to_all x1, starting transfers between devices, on_device(): parts = lax.all_to_all(partial, both, 0, 0, tiled=True)  4.3 us
    ppermute x1, starting transfers between devices, on_device(): got_d = lax.ppermute(send_d, both, route_d)  3.73 us
    ppermute x1, starting transfers between devices, on_device(): got_a = lax.ppermute(send_a, both, route_a)  3.09 us
    pallas_call x1, Pallas kernels, edge_steps(): pl.pallas_call(functools.partial(edge_kernel, height, chunks, parts, trac...  2.19 us
    pallas_call x1, Pallas kernels, pack(): pl.pallas_call(functools.partial(pack_kernel, height, chunks, cuts, level...  1.95 us
    ppermute x1, starting transfers between devices, on_device(): got_c = lax.ppermute(send_c, both, route_c)  1.58 us
  transfers between devices with their start and end apart: 5, of which 2 were waited for; matrix products, arithmetic and copies ran while one was open for 0% of the time, Pallas kernels for 36%

profile of v6, /device:TPU:0, one launch (start us, length us, event | category | flops | bytes accessed | tf_op | source)
XLA Modules:
  0.0 28.8 jit_solution(4075839833532981493)
XLA Ops:
  0.6 0.0 copy-start.4
  0.6 0.0 copy-start.3
  0.7 0.0 copy-start.2
  0.7 0.0 copy-start.1
  0.7 0.0 copy-start
  0.7 2.0 %pack.1 = (f32[504,128]{1,0:T(8,128)S(1)}, f32[504,128]{1,0:T(8,128)S(1)}, f32[384,128]{1,0:T(8,128)S(1)}, f32[10,16,128]{2,1,0:T(8,128)S(1)}, s32[128]{0:T(128)...) custom-call(f32[2560,128]{1,0:T(8,128)} %bitcast.3, s32[16,128]{1,0:T(8,128)} %mask_ref.3, f32[16,128]{1,0:T(8,128)} %diff_ref.3, ...), custom_call_target="tpu_custom_call" | custom-call | bytes 7000000 | tf_op jit(solution)/shard_map/pack/pallas_call | solution.py:616
  2.6 3.1 %collective-permute-start = (f32[504,128]{1,0:T(8,128)S(1)}, f32[504,128]{1,0:T(8,128)S(1)}, u32[]{:S(2)}, u32[]{:S(2)}) collective-permute-start(f32[504,128]{1,0:T(8,128)S(1)} %get-tuple-element.20), channel_id=1, source_target_pairs={{1,2},{2,1},{5,6},{6,5},{9,10},{10,9},{13,14},{14,13},{3,15},{7,11... | collective-permute-start | bytes 774152 | tf_op jit(solution)/shard_map/ppermute | solution.py:732
  5.7 0.0 collective-permute-start.1
  5.8 1.6 %collective-permute-start.2 = (f32[96,128]{1,0:T(8,128)S(1)}, f32[96,128]{1,0:T(8,128)S(1)}, u32[]{:S(2)}, u32[]{:S(2)}) collective-permute-start(f32[96,128]{1,0:T(8,128)S(1)} %get-tuple-element.22), channel_id=1, source_target_pairs={{0,4},{4,0},{1,5},{5,1},{2,6},{6,2},{3,7},{7,3},{8,12},{12,8},{9,1... | collective-permute-start | bytes 147464 | tf_op jit(solution)/shard_map/ppermute | solution.py:734
  7.3 0.0 copy-done.2
  7.3 0.0 copy-done.1
  7.3 0.0 copy-done
  7.3 5.5 %remap.1 = f32[16,24,128]{2,1,0:T(8,128)} custom-call(s32[128]{0:T(128)S(4)} %get-tuple-element.17.owner_ref, f32[10,16,128]{2,1,0:T(8,128)S(1)} %get-tuple-element.18.surface_ref, s32[128,128]{1,0:T(8,128)S(1)} %copy-done, s32[128,128]{1,0:T(8,128)S(1)} %copy-done.1, f32[128,128]{1,0:T(8,128)S(1)} %copy-done.2, f32[384,128]{1,0:T(8,128)S(1)} %get-tuple-element.19.p_ref), custom_call_target="tpu_custom_call" | custom-call | bytes 21000000 | tf_op jit(solution)/shard_map/remap/pallas_call | solution.py:647
  12.8 0.0 collective-permute-done.2.got_c_ref
  12.8 0.0 collective-permute-done.a_ref
  12.8 0.0 collective-permute-done.1.b_ref
  12.9 4.3 %all-to-all-start = ((f32[16,24,128]{2,1,0:T(8,128)}), f32[16,24,128]{2,1,0:T(8,128)S(1)}, u32[]{:S(2)}, u32[]{:S(2)}) async-start(f32[16,24,128]{2,1,0:T(8,128)} %remap.1), calls=%async_computation | async-start | bytes 393216 | tf_op jit(solution)/shard_map/all_to_all | solution.py:739
  17.2 3.7 %collective-permute-start.3 = (f32[96,128]{1,0:T(8,128)S(1)}, f32[96,128]{1,0:T(8,128)S(1)}, u32[]{:S(2)}, u32[]{:S(2)}) collective-permute-start(f32[96,128]{1,0:T(8,128)S(1)} %get-tuple-element.28), channel_id=1, source_target_pairs={{4,8},{8,4},{5,9},{9,5},{6,10},{10,6},{7,11},{11,7},{12,0},{0,12},... | collective-permute-start | bytes 147464 | tf_op jit(solution)/shard_map/ppermute | solution.py:735
  20.9 0.0 copy-done.4
  20.9 0.0 copy-done.3
  20.9 5.0 %tile.1 = (f32[16,160,128]{2,1,0:T(8,128)S(1)}, f32[528,128]{1,0:T(8,128)S(1)}) custom-call(f32[2560,128]{1,0:T(8,128)} %bitcast.4, s32[16,128]{1,0:T(8,128)S(1)} %copy-done.3, f32[16,128]{1,0:T(8,128)S(1)} %copy-done.4, f32[504,128]{1,0:T(8,128)S(1)} %collective-permute-done.a_ref, f32[504,128]{1,0:T(8,128)S(1)} %collective-permute-done.1.b_ref, ...), custom_call_target="tpu_custom_call" | custom-call | bytes 14000000 | tf_op jit(solution)/shard_map/tile/pallas_call | solution.py:673
  25.9 0.4 %collective-permute-done.3.got_d_ref = f32[96,128]{1,0:T(8,128)S(1)} collective-permute-done((f32[96,128]{1,0:T(8,128)S(1)}, f32[96,128]{1,0:T(8,128)S(1)}, u32[]{:S(2)}, u32[]{:S(2)}) %collective-permute-start.3) | collective-permute-done | bytes 49184 | tf_op jit(solution)/shard_map/ppermute | solution.py:735
  26.3 0.3 %all-to-all-done.parts_ref = f32[16,24,128]{2,1,0:T(8,128)S(1)} async-done(((f32[16,24,128]{2,1,0:T(8,128)}), f32[16,24,128]{2,1,0:T(8,128)S(1)}, u32[]{:S(2)}, u32[]{:S(2)}) %all-to-all-start) | async-done | bytes 196640 | tf_op jit(solution)/shard_map/all_to_all | solution.py:739
  26.6 2.2 %edges.1 = (f32[2560,128]{1,0:T(8,128)}, f32[10,256]{1,0:T(8,128)}) custom-call(f32[16,160,128]{2,1,0:T(8,128)S(1)} %get-tuple-element.25.y_ref, f32[528,128]{1,0:T(8,128)S(1)} %get-tuple-element.26.strips_ref, f32[96,128]{1,0:T(8,128)S(1)} %collective-permute-done.2.got_c_ref, f32[96,128]{1,0:T(8,128)S(1)} %collective-permute-done.3.got_d_ref, ...), custom_call_target="tpu_custom_call" | custom-call | bytes 10500000 | tf_op jit(solution)/shard_map/edges/pallas_call | solution.py:701
Async XLA Ops:
  0.6 20.3 %copy-start.4 = (f32[16,128]{1,0:T(8,128)S(1)}, f32[16,128]{1,0:T(8,128)}, u32[]{:S(2)}) copy-start(f32[16,128]{1,0:T(8,128)} %diff_ref.3) | copy-start | bytes 24580
  0.6 20.3 %copy-start.3 = (s32[16,128]{1,0:T(8,128)S(1)}, s32[16,128]{1,0:T(8,128)}, u32[]{:S(2)}) copy-start(s32[16,128]{1,0:T(8,128)} %mask_ref.3) | copy-start | bytes 24580
  0.7 6.7 %copy-start.2 = (f32[128,128]{1,0:T(8,128)S(1)}, f32[128,128]{1,0:T(8,128)}, u32[]{:S(2)}) copy-start(f32[128,128]{1,0:T(8,128)} %weight_ref.1) | copy-start | bytes 196612
  0.7 6.7 %copy-start.1 = (s32[128,128]{1,0:T(8,128)S(1)}, s32[128,128]{1,0:T(8,128)}, u32[]{:S(2)}) copy-start(s32[128,128]{1,0:T(8,128)} %column_ref.1) | copy-start | bytes 196612
  0.7 6.7 %copy-start = (s32[128,128]{1,0:T(8,128)S(1)}, s32[128,128]{1,0:T(8,128)}, u32[]{:S(2)}) copy-start(s32[128,128]{1,0:T(8,128)} %cell_ref.1) | copy-start | bytes 196612
  2.6 10.2 %collective-permute-start = (f32[504,128]{1,0:T(8,128)S(1)}, f32[504,128]{1,0:T(8,128)S(1)}, u32[]{:S(2)}, u32[]{:S(2)}) collective-permute-start(f32[504,128]{1,0:T(8,128)S(1)} %get-tuple-element.20), channel_id=1, source_target_pairs={{1,2},{2,1},{5,6},{6,5},{9,10},{10,9},{13,14},{14,13},{3,15},{7,11... | collective-permute-start | bytes 774152 | tf_op jit(solution)/shard_map/ppermute | solution.py:732
  5.7 7.1 %collective-permute-start.1 = (f32[504,128]{1,0:T(8,128)S(1)}, f32[504,128]{1,0:T(8,128)S(1)}, u32[]{:S(2)}, u32[]{:S(2)}) collective-permute-start(f32[504,128]{1,0:T(8,128)S(1)} %get-tuple-element.21), channel_id=1, source_target_pairs={{0,1},{1,0},{2,3},{3,2},{4,5},{5,4},{6,7},{7,6},{8,9},{9,8},{10,11... | collective-permute-start | bytes 774152 | tf_op jit(solution)/shard_map/ppermute | solution.py:733
  5.8 7.1 %collective-permute-start.2 = (f32[96,128]{1,0:T(8,128)S(1)}, f32[96,128]{1,0:T(8,128)S(1)}, u32[]{:S(2)}, u32[]{:S(2)}) collective-permute-start(f32[96,128]{1,0:T(8,128)S(1)} %get-tuple-element.22), channel_id=1, source_target_pairs={{0,4},{4,0},{1,5},{5,1},{2,6},{6,2},{3,7},{7,3},{8,12},{12,8},{9,1... | collective-permute-start | bytes 147464 | tf_op jit(solution)/shard_map/ppermute | solution.py:734
  12.9 13.8 %all-to-all-start = ((f32[16,24,128]{2,1,0:T(8,128)}), f32[16,24,128]{2,1,0:T(8,128)S(1)}, u32[]{:S(2)}, u32[]{:S(2)}) async-start(f32[16,24,128]{2,1,0:T(8,128)} %remap.1), calls=%async_computation | async-start | bytes 393216 | tf_op jit(solution)/shard_map/all_to_all | solution.py:739
  17.2 9.1 %collective-permute-start.3 = (f32[96,128]{1,0:T(8,128)S(1)}, f32[96,128]{1,0:T(8,128)S(1)}, u32[]{:S(2)}, u32[]{:S(2)}) collective-permute-start(f32[96,128]{1,0:T(8,128)S(1)} %get-tuple-element.28), channel_id=1, source_target_pairs={{4,8},{8,4},{5,9},{9,5},{6,10},{10,6},{7,11},{11,7},{12,0},{0,12},... | collective-permute-start | bytes 147464 | tf_op jit(solution)/shard_map/ppermute | solution.py:735
